TPU v7x, 32 devices: a whole 2x2x4 slice. The times are simulated.
32 devices in a mesh: dp: 8 (over z, y), fsdp: 4 (over x, core).
Axes of the slice: x: 2, y: 2, z: 4, core: 2. Of those that a mesh axis runs over, the one named last changes fastest.
Arguments:
- patches: bfloat16 [8, 832, 768], P('dp', 'fsdp'), may hold values from -6 to 6
- segment_ids: int32 [8, 832], P('dp', 'fsdp'), may hold values from 0 to 9, as said below
- live: int32 [8, 832], P('dp', 'fsdp'), may hold values from 0 to 1, as said below
- expert_ids: int32 [8, 832, 2], P('dp', 'fsdp'), may hold values from 0 to 7, as said below
- ranks: int32 [8, 832, 2], P('dp', 'fsdp'), may hold values from 0 to 55, as said below
- norm_gains: bfloat16 [4, 768], P(None, ('dp', 'fsdp')), may hold values from 0.099609375 to 1.8984375
- norm_biases: bfloat16 [4, 768], P(None, ('dp', 'fsdp')), may hold values from -1.75 to 1.75
- attn_qkv: bfloat16 [2, 768, 2304], P(None, ('dp', 'fsdp')), may hold values from -0.21875 to 0.21875
- attn_out: bfloat16 [2, 768, 768], P(None, ('dp', 'fsdp')), may hold values from -1.75 to 1.75
- mlp_in: bfloat16 [768, 3072], P(('dp', 'fsdp')), may hold values from -0.21875 to 0.21875
- mlp_out: bfloat16 [3072, 768], P(('dp', 'fsdp')), may hold values from -0.21875 to 0.21875
- router: bfloat16 [768, 8], P(('dp', 'fsdp')), may hold values from -0.109375 to 0.109375
- exp_in: bfloat16 [8, 768, 3072], P(None, ('dp', 'fsdp')), may hold values from -0.21875 to 0.21875
- exp_out: bfloat16 [8, 3072, 768], P(None, ('dp', 'fsdp')), may hold values from -0.4375 to 0.4375
- cotangent: bfloat16 [8, 832, 768], P('dp', 'fsdp'), may hold values from -6 to 6
Outputs:
- activations: bfloat16 [8, 832, 768], P('dp', 'fsdp')
- patch_grads: float32 [8, 832, 768], P('dp', 'fsdp')
- gain_grads: float32 [4, 768], P(None, ('dp', 'fsdp'))
- bias_grads: float32 [3, 768], P(None, ('dp', 'fsdp'))
- moe_bias_grad: float32 [768], P(('dp', 'fsdp'))
- qkv_grads: float32 [2, 768, 2304], P(None, ('dp', 'fsdp'))
- proj_grads: float32 [2, 768, 768], P(None, ('dp', 'fsdp'))
- mlp_in_grads: float32 [768, 3072], P(('dp', 'fsdp'))
- mlp_out_grads: float32 [3072, 768], P(('dp', 'fsdp'))
- router_grads: float32 [768, 8], P(('dp', 'fsdp'))
- exp_in_grads: float32 [8, 768, 3072], P(None, ('dp', 'fsdp'))
- exp_out_grads: float32 [8, 3072, 768], P(None, ('dp', 'fsdp'))
Inputs may be any that keep to these rules, and one draw needn't show every extreme that they name: `segment_ids`: within a row segment numbers never fall and each image is contiguous, numbered from 0; every row ends with padding, at least its last patch, and every padded patch carries segment number 9, which no live patch shares. In each group of 1 row of one dp index one row, drawn from the seed, begins with an image from patch 0 past patch 3 * 208. `live`: padding only at the end of a row. `expert_ids`: A patch's two experts differ; every expert is named. For the patches of one device and each expert, the live choices naming that expert, all first choices before all second ones and earlier patches first, hold ranks 0, 1, 2, ... in order; 55 marks a choice dropped by capacity and every choice of a padded patch.
All inputs are finite; a program needn't handle non-finite values.
Results may differ from a plain program's by a relative error of at most 0.028.
Values may be sent and summed in bfloat16 or wider, within the bound.
No kernel may reach another device: no remote copies, remote signals or barrier semaphores. Data moves between devices by JAX's collectives and lax.ppermute only.
A program may use at most 512 MiB of HBM per device.

v0:
```python
import jax
import jax.numpy as jnp
from jax import lax
from jax.sharding import PartitionSpec as P

HEADS = 12
HD = 64


EPSILON = 1e-06


def contract_rows(left, right):
    return lax.dot_general(
        left, right, (((0,), (0,)), ((), ())), preferred_element_type=jnp.float32
    )


def times_transpose(left, right):
    return lax.dot_general(
        left, right, (((1,), (1,)), ((), ())), preferred_element_type=jnp.float32
    )


def gelu_exact(values):
    return jax.nn.gelu(values, approximate=False)


def normalize(flat_rows, norm_gain, norm_bias):
    centre = jnp.mean(flat_rows, axis=-1, keepdims=True)
    centred = flat_rows - centre
    inv_scale = lax.rsqrt(jnp.mean(centred * centred, axis=-1, keepdims=True) + EPSILON)
    scaled = centred * inv_scale
    return (scaled * norm_gain + norm_bias, scaled, inv_scale)


def norm_back(out_grad, scaled, inv_scale, norm_gain):
    weighted = out_grad * norm_gain
    input_grad = inv_scale * (
        weighted
        - jnp.mean(weighted, axis=-1, keepdims=True)
        - scaled * jnp.mean(weighted * scaled, axis=-1, keepdims=True)
    )
    return (input_grad, jnp.sum(out_grad * scaled, axis=0), jnp.sum(out_grad, axis=0))


def scaled_scores(queries, keys_all, allowed):
    scores = jnp.einsum(
        "sqhd,skhd->shqk", queries, keys_all, preferred_element_type=jnp.float32
    ) * HD ** (-0.5)
    return jnp.where(allowed, scores, -1e30)


def attention_forward(state, seg_here, live_here, weights):
    w_qkv, w_out, gains, biases = weights
    rows_here, patch_here, width = state.shape
    normed, scaled, inv_scale = normalize(
        state.reshape(-1, width), gains[0].astype(jnp.float32), biases[0].astype(jnp.float32)
    )
    normed_low = normed.astype(jnp.bfloat16)
    mixed_all = jnp.dot(normed_low, w_qkv, preferred_element_type=jnp.float32).astype(jnp.bfloat16)
    mixed_all = mixed_all.reshape(rows_here, patch_here, 3 * width)
    queries = mixed_all[..., :width]
    keys_here = mixed_all[..., width : 2 * width]
    values_here = mixed_all[..., 2 * width :]
    keys_all, values_all, seg_all = (
        lax.all_gather(keys_here, "fsdp", axis=1, tiled=True),
        lax.all_gather(values_here, "fsdp", axis=1, tiled=True),
        lax.all_gather(seg_here, "fsdp", axis=1, tiled=True),
    )
    query_heads = queries.reshape(rows_here, patch_here, HEADS, HD)
    key_heads = keys_all.reshape(rows_here, -1, HEADS, HD)
    value_heads = values_all.reshape(rows_here, -1, HEADS, HD)
    allowed = (seg_here[:, :, None] == seg_all[:, None, :])[:, None]
    scores = scaled_scores(query_heads, key_heads, allowed)
    row_max = jnp.max(scores, axis=-1, keepdims=True)
    shifted = jnp.exp(scores - row_max)
    row_sum = jnp.sum(shifted, axis=-1, keepdims=True)
    weights_low = (shifted / row_sum).astype(jnp.bfloat16)
    log_total = row_max + jnp.log(row_sum)
    heads_out = jnp.einsum(
        "shqk,skhd->sqhd", weights_low, value_heads, preferred_element_type=jnp.float32
    )
    heads_out = heads_out * live_here[:, :, None, None]
    heads_low = heads_out.astype(jnp.bfloat16).reshape(-1, width)
    branch = jnp.dot(heads_low, w_out, preferred_element_type=jnp.float32)
    saved = (
        scaled,
        inv_scale,
        normed_low,
        query_heads,
        key_heads,
        value_heads,
        allowed,
        log_total,
        heads_low,
    )
    return (state + branch.reshape(state.shape), saved)


def attention_backward(residual_grad, live_here, weights, saved):
    w_qkv, w_out, gains, biases = weights
    (
        scaled,
        inv_scale,
        normed_low,
        query_heads,
        key_heads,
        value_heads,
        allowed,
        log_total,
        heads_low,
    ) = saved
    rows_here, patch_here, width = residual_grad.shape
    branch_grad = residual_grad.astype(jnp.bfloat16).reshape(-1, width)
    out_grad = contract_rows(heads_low, branch_grad)
    live_low = live_here.astype(jnp.bfloat16).reshape(-1, 1)
    heads_grad = times_transpose(branch_grad, w_out).astype(jnp.bfloat16) * live_low
    heads_grad = heads_grad.reshape(rows_here, patch_here, HEADS, HD)
    scores = scaled_scores(query_heads, key_heads, allowed)
    soft_rows = jnp.exp(scores - log_total)
    soft_low = soft_rows.astype(jnp.bfloat16)
    values_grad = jnp.einsum(
        "shqk,sqhd->skhd", soft_low, heads_grad, preferred_element_type=jnp.float32
    )
    soft_grad = jnp.einsum(
        "sqhd,skhd->shqk", heads_grad, value_heads, preferred_element_type=jnp.float32
    )
    row_dot = jnp.sum(soft_rows * soft_grad, axis=-1, keepdims=True)
    score_grad = (soft_rows * (soft_grad - row_dot)).astype(jnp.bfloat16)
    query_grad = jnp.einsum(
        "shqk,skhd->sqhd", score_grad, key_heads, preferred_element_type=jnp.float32
    ) * HD ** (-0.5)
    keys_grad = jnp.einsum(
        "shqk,sqhd->skhd", score_grad, query_heads, preferred_element_type=jnp.float32
    ) * HD ** (-0.5)
    keys_mine, values_mine = (
        lax.psum_scatter(
            keys_grad.reshape(rows_here, -1, width).astype(jnp.bfloat16),
            "fsdp",
            scatter_dimension=1,
            tiled=True,
        ).astype(jnp.float32),
        lax.psum_scatter(
            values_grad.reshape(rows_here, -1, width).astype(jnp.bfloat16),
            "fsdp",
            scatter_dimension=1,
            tiled=True,
        ).astype(jnp.float32),
    )
    mixed_grad = jnp.concatenate(
        [query_grad.reshape(rows_here, patch_here, width), keys_mine, values_mine], axis=-1
    )
    mixed_grad = mixed_grad.astype(jnp.bfloat16).reshape(-1, 3 * width)
    qkv_grad = contract_rows(normed_low, mixed_grad)
    normed_grad = times_transpose(mixed_grad, w_qkv)
    input_grad, gain_grad, bias_grad = norm_back(
        normed_grad, scaled, inv_scale, gains[0].astype(jnp.float32)
    )
    return (
        residual_grad + input_grad.reshape(residual_grad.shape),
        qkv_grad,
        out_grad,
        gain_grad,
        bias_grad,
    )


def ffn_forward(state, weights, norm_gain, norm_bias):
    w_in, w_back = weights
    width = state.shape[-1]
    normed, scaled, inv_scale = normalize(state.reshape(-1, width), norm_gain, norm_bias)
    normed_low = normed.astype(jnp.bfloat16)
    inner_pre = jnp.dot(normed_low, w_in, preferred_element_type=jnp.float32)
    hidden = gelu_exact(inner_pre).astype(jnp.bfloat16)
    branch = jnp.dot(hidden, w_back, preferred_element_type=jnp.float32)
    return (state + branch.reshape(state.shape), (scaled, inv_scale, normed_low, inner_pre, hidden))


def ffn_backward(residual_grad, weights, norm_gain, saved):
    w_in, w_back = weights
    scaled, inv_scale, normed_low, inner_pre, hidden = saved
    width = residual_grad.shape[-1]
    branch_grad = residual_grad.astype(jnp.bfloat16).reshape(-1, width)
    back_grad = contract_rows(hidden, branch_grad)
    hidden_grad = times_transpose(branch_grad, w_back)
    unused, gelu_back = jax.vjp(gelu_exact, inner_pre)
    inner_grad = gelu_back(hidden_grad)[0].astype(jnp.bfloat16)
    in_grad = contract_rows(normed_low, inner_grad)
    normed_grad = times_transpose(inner_grad, w_in)
    input_grad, gain_grad, bias_grad = norm_back(normed_grad, scaled, inv_scale, norm_gain)
    return (
        residual_grad + input_grad.reshape(residual_grad.shape),
        in_grad,
        back_grad,
        gain_grad,
        bias_grad,
    )


def route_tables(normed_low, w_router, expert_ids, ranks, capacity, slots):
    tokens = normed_low.shape[0]
    experts = w_router.shape[1]
    logits = jnp.dot(normed_low, w_router, preferred_element_type=jnp.float32)
    soft_rows = jax.nn.softmax(logits, axis=-1)
    choice_ids = expert_ids.reshape(tokens, 2)
    rank_ids = ranks.reshape(tokens, 2)
    choose = (choice_ids[:, :, None] == jnp.arange(experts)[None, None, :]).astype(jnp.float32)
    slot_hot = (rank_ids[:, :, None] == jnp.arange(slots)[None, None, :]).astype(jnp.bfloat16)
    kept_mask = (rank_ids < capacity).astype(jnp.float32)
    gate_low = (jnp.sum(soft_rows[:, None, :] * choose, axis=-1) * kept_mask).astype(jnp.bfloat16)
    dispatch = jnp.einsum(
        "tke,tkc->tec", choose.astype(jnp.bfloat16), slot_hot, preferred_element_type=jnp.float32
    ).astype(jnp.bfloat16)
    gated_choose = (choose * gate_low.astype(jnp.float32)[:, :, None]).astype(jnp.bfloat16)
    combine = jnp.einsum(
        "tke,tkc->tec", gated_choose, slot_hot, preferred_element_type=jnp.float32
    ).astype(jnp.bfloat16)
    return (soft_rows, choose, slot_hot, kept_mask, dispatch, combine)


def gate_back(branch_grad, result, tables, normed_low, w_router):
    soft_rows, choose, slot_hot, kept_mask, dispatch, combine = tables
    result_grad = jnp.einsum(
        "tec,td->ecd", combine, branch_grad, preferred_element_type=jnp.float32
    ).astype(jnp.bfloat16)
    combine_grad = jnp.einsum(
        "td,ecd->tec", branch_grad, result, preferred_element_type=jnp.float32
    )
    gate_grad = (
        jnp.einsum("tec,tke,tkc->tk", combine_grad, choose, slot_hot.astype(jnp.float32))
        * kept_mask
    )
    soft_grad = jnp.sum(gate_grad[:, :, None] * choose, axis=1)
    logit_grad = soft_rows * (soft_grad - jnp.sum(soft_rows * soft_grad, axis=-1, keepdims=True))
    logit_grad = logit_grad.astype(jnp.bfloat16)
    router_grad = contract_rows(normed_low, logit_grad)
    normed_grad = times_transpose(logit_grad, w_router)
    return (result_grad, router_grad, normed_grad)


def moe_forward(state, weights, norm_gain, norm_bias, expert_ids, ranks):
    w_router, w_in, w_back = weights
    width = state.shape[-1]
    experts = w_in.shape[0]
    normed, scaled, inv_scale = normalize(state.reshape(-1, width), norm_gain, norm_bias)
    tokens = normed.shape[0]
    capacity = (210 * tokens + 100 * experts - 1) // (100 * experts)
    normed_low = normed.astype(jnp.bfloat16)
    tables = route_tables(normed_low, w_router, expert_ids, ranks, capacity, capacity)
    dispatch, combine = (tables[4], tables[5])
    slot_rows = jnp.einsum(
        "tec,td->ecd", dispatch, normed_low, preferred_element_type=jnp.float32
    ).astype(jnp.bfloat16)
    inner_pre = jnp.einsum("ecd,edf->ecf", slot_rows, w_in, preferred_element_type=jnp.float32)
    hidden = gelu_exact(inner_pre).astype(jnp.bfloat16)
    result = jnp.einsum("ecf,efd->ecd", hidden, w_back, preferred_element_type=jnp.float32).astype(
        jnp.bfloat16
    )
    branch = jnp.einsum("tec,ecd->td", combine, result, preferred_element_type=jnp.float32)
    saved = (scaled, inv_scale, normed_low, tables, slot_rows, inner_pre, hidden, result)
    return (state + branch.reshape(state.shape), saved)


def moe_backward(residual_grad, weights, norm_gain, saved):
    w_router, w_in, w_back = weights
    scaled, inv_scale, normed_low, tables, slot_rows, inner_pre, hidden, result = saved
    width = residual_grad.shape[-1]
    branch_grad = residual_grad.astype(jnp.bfloat16).reshape(-1, width)
    result_grad, router_grad, normed_grad = gate_back(
        branch_grad, result, tables, normed_low, w_router
    )
    back_grad = jnp.einsum("ecf,ecd->efd", hidden, result_grad, preferred_element_type=jnp.float32)
    hidden_grad = jnp.einsum(
        "ecd,efd->ecf", result_grad, w_back, preferred_element_type=jnp.float32
    )
    unused, gelu_back = jax.vjp(gelu_exact, inner_pre)
    inner_grad = gelu_back(hidden_grad)[0].astype(jnp.bfloat16)
    in_grad = jnp.einsum("ecd,ecf->edf", slot_rows, inner_grad, preferred_element_type=jnp.float32)
    slot_grad = jnp.einsum(
        "ecf,edf->ecd", inner_grad, w_in, preferred_element_type=jnp.float32
    ).astype(jnp.bfloat16)
    normed_grad = normed_grad + jnp.einsum(
        "tec,ecd->td", tables[4], slot_grad, preferred_element_type=jnp.float32
    )
    input_grad, gain_grad, bias_grad = norm_back(normed_grad, scaled, inv_scale, norm_gain)
    return (
        residual_grad + input_grad.reshape(residual_grad.shape),
        router_grad,
        in_grad,
        back_grad,
        gain_grad,
        bias_grad,
    )


def shards(
    patches,
    segment_ids,
    live,
    expert_ids,
    ranks,
    norm_gains,
    norm_biases,
    attn_qkv,
    attn_out,
    mlp_in,
    mlp_out,
    router,
    exp_in,
    exp_out,
    cotangent,
):
    seg_here = segment_ids.astype(jnp.bfloat16)
    live_here = live.astype(jnp.float32)

    def attn_weights(layer_index):
        rows_pick = slice(2 * layer_index, 2 * layer_index + 2)
        return (
            lax.all_gather(attn_qkv[layer_index], ("dp", "fsdp"), axis=0, tiled=True),
            lax.all_gather(attn_out[layer_index], ("dp", "fsdp"), axis=0, tiled=True),
            lax.all_gather(norm_gains[rows_pick], ("dp", "fsdp"), axis=1, tiled=True),
            lax.all_gather(norm_biases[rows_pick], ("dp", "fsdp"), axis=1, tiled=True),
        )

    def ffn_weights():
        return (
            lax.all_gather(mlp_in, ("dp", "fsdp"), axis=0, tiled=True),
            lax.all_gather(mlp_out, ("dp", "fsdp"), axis=0, tiled=True),
        )

    def expert_weights():
        return (
            lax.all_gather(router, ("dp", "fsdp"), axis=0, tiled=True),
            lax.all_gather(exp_in, ("dp", "fsdp"), axis=1, tiled=True),
            lax.all_gather(exp_out, ("dp", "fsdp"), axis=1, tiled=True),
        )

    def send_attn(qkv_grad, out_grad, gain_pair, bias_pair):
        return (
            lax.psum_scatter(qkv_grad, ("dp", "fsdp"), scatter_dimension=0, tiled=True),
            lax.psum_scatter(out_grad, ("dp", "fsdp"), scatter_dimension=0, tiled=True),
            lax.psum_scatter(gain_pair, ("dp", "fsdp"), scatter_dimension=1, tiled=True),
            lax.psum_scatter(bias_pair, ("dp", "fsdp"), scatter_dimension=1, tiled=True),
        )

    start = patches.astype(jnp.float32)
    first_weights = attn_weights(0)
    state_one, saved_first = attention_forward(start, seg_here, live_here, first_weights)
    first_gains = first_weights[2].astype(jnp.float32)
    first_biases = first_weights[3].astype(jnp.float32)
    dense_weights = ffn_weights()
    state_two, saved_dense = ffn_forward(state_one, dense_weights, first_gains[1], first_biases[1])
    second_weights = attn_weights(1)
    state_three, saved_second = attention_forward(state_two, seg_here, live_here, second_weights)
    second_gains = second_weights[2].astype(jnp.float32)
    second_biases = second_weights[3].astype(jnp.float32)
    moe_weights = expert_weights()
    state_four, saved_moe = moe_forward(
        state_three, moe_weights, second_gains[1], second_biases[1], expert_ids, ranks
    )
    activations = state_four.astype(jnp.bfloat16)
    residual_grad = cotangent.astype(jnp.float32)
    back_second = attn_weights(1)
    back_gains_two = back_second[2].astype(jnp.float32)
    back_moe = expert_weights()
    residual_grad, router_grad, in_grad, back_grad, gain_moe, bias_moe = moe_backward(
        residual_grad, back_moe, back_gains_two[1], saved_moe
    )
    router_grads, exp_in_grads, exp_out_grads = (
        lax.psum_scatter(router_grad, ("dp", "fsdp"), scatter_dimension=0, tiled=True),
        lax.psum_scatter(in_grad, ("dp", "fsdp"), scatter_dimension=1, tiled=True),
        lax.psum_scatter(back_grad, ("dp", "fsdp"), scatter_dimension=1, tiled=True),
    )
    residual_grad, qkv_two, out_two, gain_att_two, bias_att_two = attention_backward(
        residual_grad, live_here, back_second, saved_second
    )
    second_sent = send_attn(
        qkv_two, out_two, jnp.stack([gain_att_two, gain_moe]), jnp.stack([bias_att_two, bias_moe])
    )
    back_dense = ffn_weights()
    back_first = attn_weights(0)
    back_gains_one = back_first[2].astype(jnp.float32)
    residual_grad, dense_in, dense_back, gain_dense, bias_dense = ffn_backward(
        residual_grad, back_dense, back_gains_one[1], saved_dense
    )
    mlp_in_grads, mlp_out_grads = (
        lax.psum_scatter(dense_in, ("dp", "fsdp"), scatter_dimension=0, tiled=True),
        lax.psum_scatter(dense_back, ("dp", "fsdp"), scatter_dimension=0, tiled=True),
    )
    residual_grad, qkv_one, out_one, gain_att_one, bias_att_one = attention_backward(
        residual_grad, live_here, back_first, saved_first
    )
    first_sent = send_attn(
        qkv_one,
        out_one,
        jnp.stack([gain_att_one, gain_dense]),
        jnp.stack([bias_att_one, bias_dense]),
    )
    gain_grads = jnp.concatenate([first_sent[2], second_sent[2]], axis=0)
    bias_grads = jnp.concatenate([first_sent[3], second_sent[3][:1]], axis=0)
    moe_bias_grad = second_sent[3][1]
    qkv_grads = jnp.stack([first_sent[0], second_sent[0]])
    proj_grads = jnp.stack([first_sent[1], second_sent[1]])
    return (
        activations,
        residual_grad,
        gain_grads,
        bias_grads,
        moe_bias_grad,
        qkv_grads,
        proj_grads,
        mlp_in_grads,
        mlp_out_grads,
        router_grads,
        exp_in_grads,
        exp_out_grads,
    )


def solution(mesh):
    return jax.shard_map(
        shards,
        mesh=mesh,
        in_specs=(
            P("dp", "fsdp", None),
            P("dp", "fsdp"),
            P("dp", "fsdp"),
            P("dp", "fsdp", None),
            P("dp", "fsdp", None),
            P(None, ("dp", "fsdp")),
            P(None, ("dp", "fsdp")),
            P(None, ("dp", "fsdp"), None),
            P(None, ("dp", "fsdp"), None),
            P(("dp", "fsdp"), None),
            P(("dp", "fsdp"), None),
            P(("dp", "fsdp"), None),
            P(None, ("dp", "fsdp"), None),
            P(None, ("dp", "fsdp"), None),
            P("dp", "fsdp", None),
        ),
        out_specs=(
            P("dp", "fsdp", None),
            P("dp", "fsdp", None),
            P(None, ("dp", "fsdp")),
            P(None, ("dp", "fsdp")),
            P(("dp", "fsdp")),
            P(None, ("dp", "fsdp"), None),
            P(None, ("dp", "fsdp"), None),
            P(("dp", "fsdp"), None),
            P(("dp", "fsdp"), None),
            P(("dp", "fsdp"), None),
            P(None, ("dp", "fsdp"), None),
            P(None, ("dp", "fsdp"), None),
        ),
        check_vma=False,
    )
```

profile of v0, /device:TPU:5, one launch (start us, length us, event | category | flops | bytes accessed | tf_op | source)
XLA Modules:
  0.0 3230.1 jit_solution(4268615832609576475)
XLA Ops:
  9.7 38.4 %all-gather.5 = bf16[32,24,2]{1,2,0:T(2,128)(2,1)S(1)} all-gather(bf16[1,24,2]{1,2,0:T(2,128)(2,1)S(1)} %get-tuple-element.66), channel_id=1, replica_groups=mesh['dp'=8,'fsdp'=4] {'dp','fsdp'}, dimensions={0}, use_global_device_ids=true | all-gather | bytes 3168 | tf_op jit(solution)/shard_map/all_gather | solution.py:323
  49.0 36.5 %all-gather.4 = bf16[32,24,2]{1,2,0:T(2,128)(2,1)S(1)} all-gather(bf16[1,24,2]{1,2,0:T(2,128)(2,1)S(1)} %get-tuple-element.64), channel_id=1, replica_groups=mesh['dp'=8,'fsdp'=4] {'dp','fsdp'}, dimensions={0}, use_global_device_ids=true | all-gather | bytes 3168 | tf_op jit(solution)/shard_map/all_gather | solution.py:322
  95.6 37.8 %all-gather.7 = bf16[32,24,2]{1,2,0:T(2,128)(2,1)S(1)} all-gather(bf16[1,24,2]{1,2,0:T(2,128)(2,1)S(1)} %get-tuple-element.65), channel_id=1, replica_groups=mesh['dp'=8,'fsdp'=4] {'dp','fsdp'}, dimensions={0}, use_global_device_ids=true | all-gather | bytes 3168 | tf_op jit(solution)/shard_map/all_gather | solution.py:323
  133.5 36.5 %all-gather.6 = bf16[32,24,2]{1,2,0:T(2,128)(2,1)S(1)} all-gather(bf16[1,24,2]{1,2,0:T(2,128)(2,1)S(1)} %get-tuple-element.63), channel_id=1, replica_groups=mesh['dp'=8,'fsdp'=4] {'dp','fsdp'}, dimensions={0}, use_global_device_ids=true | all-gather | bytes 3168 | tf_op jit(solution)/shard_map/all_gather | solution.py:322
  192.1 62.2 %all-gather.26.cloned.1.call-done = bf16[768,3072]{1,0:T(8,128)(2,1)} async-done(((bf16[24,3072]{1,0:T(8,128)(2,1)}), bf16[768,3072]{1,0:T(8,128)(2,1)}) %all-gather.26.cloned.1.call-update) | async-done | bytes 4718608 | tf_op jit(solution)/shard_map/all_gather | solution.py:328
  263.8 55.8 %all-gather.28.cloned.1.call-done = bf16[3072,768]{1,0:T(8,128)(2,1)} async-done(((bf16[96,768]{1,0:T(8,128)(2,1)}), bf16[3072,768]{1,0:T(8,128)(2,1)}) %all-gather.28.cloned.1.call-update) | async-done | bytes 4718608 | tf_op jit(solution)/shard_map/all_gather | solution.py:329
  323.4 58.5 %all-gather.42.cloned.1.call-done = bf16[1,768,2304]{2,1,0:T(8,128)(2,1)} async-done(((bf16[1,24,2304]{2,1,0:T(8,128)(2,1)}), bf16[1,768,2304]{2,1,0:T(8,128)(2,1)}) %all-gather.42.cloned.1.call-update) | async-done | bytes 3538960 | tf_op jit(solution)/shard_map/all_gather | solution.py:320
  388.6 36.5 %all-gather.8 = bf16[32,24,8]{1,2,0:T(8,128)(2,1)S(1)} all-gather(bf16[1,24,8]{1,2,0:T(8,128)(2,1)S(1)} %bitcast.424), channel_id=1, replica_groups=mesh['dp'=8,'fsdp'=4] {'dp','fsdp'}, dimensions={0}, use_global_device_ids=true | all-gather | bytes 12672 | tf_op jit(solution)/shard_map/all_gather | solution.py:334
  444.0 36.7 %all-gather.44.cloned.1.call-done = bf16[1,768,768]{2,1,0:T(8,128)(2,1)} async-done(((bf16[1,24,768]{2,1,0:T(8,128)(2,1)}), bf16[1,768,768]{2,1,0:T(8,128)(2,1)}) %all-gather.44.cloned.1.call-update) | async-done | bytes 1179664 | tf_op jit(solution)/shard_map/all_gather | solution.py:321
  485.5 212.0 %all-gather.34.cloned.1.call-done = bf16[8,768,3072]{2,1,0:T(8,128)(2,1)} async-done(((bf16[8,24,3072]{2,1,0:T(8,128)(2,1)}), bf16[8,768,3072]{2,1,0:T(8,128)(2,1)}) %all-gather.34.cloned.1.call-update) | async-done | bytes 37748752 | tf_op jit(solution)/shard_map/all_gather | solution.py:335
  697.6 19.1 fusion.39
  731.1 182.5 %all-gather.36.cloned.1.call-done = bf16[8,3072,768]{2,1,0:T(8,128)(2,1)} async-done(((bf16[8,96,768]{2,1,0:T(8,128)(2,1)}), bf16[8,3072,768]{2,1,0:T(8,128)(2,1)}) %all-gather.36.cloned.1.call-update) | async-done | bytes 37748752 | tf_op jit(solution)/shard_map/all_gather | solution.py:336
  940.5 19.5 add_convert_fusion
  960.1 18.5 fusion.46
  1176.9 27.6 fusion.150
  1206.8 27.5 fusion.151
  1240.7 40.1 %all-reduce.6 = (f32[2,768]{1,0:T(2,128)S(1)}, f32[2,768]{1,0:T(2,128)S(1)}, f32[2,768]{1,0:T(2,128)S(1)}, f32[2,768]{1,0:T(2,128)S(1)}, f32[768,8]{0,1:T(8,128)S(1)}) all-reduce(f32[2,768]{1,0:T(2,128)S(1)} %pad_maximum_fusion.9, f32[2,768]{1,0:T(2,128)S(1)} %pad_maximum_fusion.8, ...), channel_id=11, replica_groups=mesh['dp'=8,'fsdp'=4] {'dp','fsdp'}, use_global_device_ids=true, to_apply=%region_36.37.clone | all-reduce | flops 12288 | bytes 98304
  1284.6 73.4 %reduce-scatter.30.cloned.1.call-done = f32[24,768]{1,0:T(8,128)} async-done(((f32[768,768]{1,0:T(8,128)}), f32[24,768]{1,0:T(8,128)}) %reduce-scatter.30.cloned.1.call-update) | async-done | bytes 73744 | tf_op jit(solution)/shard_map/reduce_scatter | solution.py:342
  1359.6 122.2 %reduce-scatter.28.cloned.1.call-done = f32[24,2304]{1,0:T(8,128)} async-done(((f32[768,2304]{1,0:T(8,128)}), f32[24,2304]{1,0:T(8,128)}) %reduce-scatter.28.cloned.1.call-update) | async-done | bytes 221200 | tf_op jit(solution)/shard_map/reduce_scatter | solution.py:341
  1481.8 124.9 %reduce-scatter.26.cloned.1.call-done = f32[24,2304]{1,0:T(8,128)} async-done(((f32[768,2304]{1,0:T(8,128)}), f32[24,2304]{1,0:T(8,128)}) %reduce-scatter.26.cloned.1.call-update) | async-done | bytes 221200 | tf_op jit(solution)/shard_map/reduce_scatter | solution.py:341
  1608.5 139.2 %reduce-scatter.34.cloned.1.call-done = f32[24,3072]{1,0:T(8,128)} async-done(((f32[768,3072]{1,0:T(8,128)}), f32[24,3072]{1,0:T(8,128)}) %reduce-scatter.34.cloned.1.call-update) | async-done | bytes 294928 | tf_op jit(solution)/shard_map/reduce_scatter | solution.py:388
  1747.7 142.1 %reduce-scatter.36.cloned.1.call-done = f32[96,768]{1,0:T(8,128)} async-done(((f32[3072,768]{1,0:T(8,128)}), f32[96,768]{1,0:T(8,128)}) %reduce-scatter.36.cloned.1.call-update) | async-done | bytes 294928 | tf_op jit(solution)/shard_map/reduce_scatter | solution.py:389
  1889.8 667.0 %reduce-scatter.38.cloned.1.call-done = f32[8,24,3072]{2,1,0:T(8,128)} async-done(((f32[8,768,3072]{2,1,0:T(8,128)}), f32[8,24,3072]{2,1,0:T(8,128)}) %reduce-scatter.38.cloned.1.call-update) | async-done | bytes 2359312 | tf_op jit(solution)/shard_map/reduce_scatter | solution.py:372
  2556.8 666.4 %reduce-scatter.40.cloned.1.call-done = f32[8,96,768]{2,1,0:T(8,128)} async-done(((f32[8,3072,768]{2,1,0:T(8,128)}), f32[8,96,768]{2,1,0:T(8,128)}) %reduce-scatter.40.cloned.1.call-update) | async-done | bytes 2359312 | tf_op jit(solution)/shard_map/reduce_scatter | solution.py:373
  (423 shorter events, 332.4 us)
Async XLA Ops:
  7.2 80.8 %all-gather.38.cloned.1.call-start = ((), (), s32[]{:S(2)}) async-start(), calls=%async_computation.28 | async-start | bytes 3649536 | tf_op jit(solution)/shard_map/all_gather | solution.py:320
  8.9 168.6 %all-gather.22.cloned.1.call-start = ((), (), s32[]{:S(2)}) async-start(), calls=%async_computation.12 | async-start | bytes 1597440 | tf_op jit(solution)/shard_map/all_gather | solution.py:68
  92.1 87.3 %all-gather.24.cloned.1.call-start = ((), (), s32[]{:S(2)}) async-start(), calls=%async_computation.13 | async-start | bytes 1597440 | tf_op jit(solution)/shard_map/all_gather | solution.py:67
  92.9 97.0 %all-gather.40.cloned.1.call-start = ((), (), s32[]{:S(2)}) async-start(), calls=%async_computation.29 | async-start | bytes 1216512 | tf_op jit(solution)/shard_map/all_gather | solution.py:321
  93.6 160.7 %all-gather.26.cloned.1.call-start = ((), (), s32[]{:S(2)}) async-start(), calls=%async_computation.14 | async-start | bytes 4866048 | tf_op jit(solution)/shard_map/all_gather | solution.py:328
  94.2 225.4 %all-gather.28.cloned.1.call-start = ((), (), s32[]{:S(2)}) async-start(), calls=%async_computation.15 | async-start | bytes 4866048 | tf_op jit(solution)/shard_map/all_gather | solution.py:329
  94.8 287.2 %all-gather.42.cloned.1.call-start = ((), (), s32[]{:S(2)}) async-start(), calls=%async_computation.30 | async-start | bytes 3649536 | tf_op jit(solution)/shard_map/all_gather | solution.py:320
  95.5 334.7 %all-gather.30.cloned.1.call-start = ((), (), s32[]{:S(2)}) async-start(), calls=%async_computation.16 | async-start | bytes 1597440 | tf_op jit(solution)/shard_map/all_gather | solution.py:68
  385.9 46.2 %all-gather.32.cloned.1.call-start = ((), (), s32[]{:S(2)}) async-start(), calls=%async_computation.17 | async-start | bytes 1597440 | tf_op jit(solution)/shard_map/all_gather | solution.py:67
  386.6 94.1 %all-gather.44.cloned.1.call-start = ((), (), s32[]{:S(2)}) async-start(), calls=%async_computation.31 | async-start | bytes 1216512 | tf_op jit(solution)/shard_map/all_gather | solution.py:321
  387.2 310.4 %all-gather.34.cloned.1.call-start = ((), (), s32[]{:S(2)}) async-start(), calls=%async_computation.18 | async-start | bytes 38928384 | tf_op jit(solution)/shard_map/all_gather | solution.py:335
  387.9 525.6 %all-gather.36.cloned.1.call-start = ((), (), s32[]{:S(2)}) async-start(), calls=%async_computation.19 | async-start | bytes 38928384 | tf_op jit(solution)/shard_map/all_gather | solution.py:336
  388.5 648.5 %reduce-scatter.44.cloned.1.call-start = ((), (), s32[]{:S(2)}) async-start(), calls=%async_computation.33 | async-start | bytes 1597440
  1004.3 53.8 %reduce-scatter.42.cloned.1.call-start = ((), (), s32[]{:S(2)}) async-start(), calls=%async_computation.32 | async-start | bytes 1597440
  1031.8 107.7 %reduce-scatter.48.cloned.1.call-start = ((), (), s32[]{:S(2)}) async-start(), calls=%async_computation.35 | async-start | bytes 1597440
  1095.2 56.1 %reduce-scatter.46.cloned.1.call-start = ((), (), s32[]{:S(2)}) async-start(), calls=%async_computation.34 | async-start | bytes 1597440
  1122.8 161.7 %reduce-scatter.32.cloned.1.call-start = ((), (), s32[]{:S(2)}) async-start(), calls=%async_computation.23 | async-start | bytes 2433024 | tf_op jit(solution)/shard_map/reduce_scatter | solution.py:342
  1126.4 231.6 %reduce-scatter.30.cloned.1.call-start = ((), (), s32[]{:S(2)}) async-start(), calls=%async_computation.22 | async-start | bytes 2433024 | tf_op jit(solution)/shard_map/reduce_scatter | solution.py:342
  1129.5 352.2 %reduce-scatter.28.cloned.1.call-start = ((), (), s32[]{:S(2)}) async-start(), calls=%async_computation.21 | async-start | bytes 7299072 | tf_op jit(solution)/shard_map/reduce_scatter | solution.py:341
  1135.0 471.7 %reduce-scatter.26.cloned.1.call-start = ((), (), s32[]{:S(2)}) async-start(), calls=%async_computation.20 | async-start | bytes 7299072 | tf_op jit(solution)/shard_map/reduce_scatter | solution.py:341
  1160.8 586.9 %reduce-scatter.34.cloned.1.call-start = ((), (), s32[]{:S(2)}) async-start(), calls=%async_computation.24 | async-start | bytes 9732096 | tf_op jit(solution)/shard_map/reduce_scatter | solution.py:388
  1168.4 721.4 %reduce-scatter.36.cloned.1.call-start = ((), (), s32[]{:S(2)}) async-start(), calls=%async_computation.25 | async-start | bytes 9732096 | tf_op jit(solution)/shard_map/reduce_scatter | solution.py:389
  1175.9 1380.9 %reduce-scatter.38.cloned.1.call-start = ((), (), s32[]{:S(2)}) async-start(), calls=%async_computation.26 | async-start | bytes 77856768 | tf_op jit(solution)/shard_map/reduce_scatter | solution.py:372
  1204.6 2018.5 %reduce-scatter.40.cloned.1.call-start = ((), (), s32[]{:S(2)}) async-start(), calls=%async_computation.27 | async-start | bytes 77856768 | tf_op jit(solution)/shard_map/reduce_scatter | solution.py:373
  (101 other events, 2354.3 us)
Sparse Core Ops, SparseCore 0:
  11.5 61.7 all-gather.37
  92.2 19.0 all-gather.21
  113.5 18.0 all-gather.23
  134.9 54.0 all-gather.39
  191.7 62.5 all-gather.25
  257.1 62.4 all-gather.27
  323.0 58.8 all-gather.41
  386.0 16.9 all-gather.29
  405.1 18.0 all-gather.31
  426.5 54.1 all-gather.43
  483.6 213.8 all-gather.33
  700.4 213.1 all-gather.35
  1004.4 24.0 reduce-scatter.43
  1031.9 26.1 reduce-scatter.41
  1095.4 26.3 reduce-scatter.47
  1125.0 26.3 reduce-scatter.45
  1156.4 97.4 reduce-scatter.31
  1259.9 98.0 reduce-scatter.29
  1363.6 118.0 reduce-scatter.27
  1488.2 118.3 reduce-scatter.25
  1613.1 134.4 reduce-scatter.33
  1755.2 134.5 reduce-scatter.35
  1896.8 659.9 reduce-scatter.37
  2564.8 658.3 reduce-scatter.39
where the time goes:
time: 3240 us; the launch traced here: 3230 us
  waiting for transfers between devices  2570 us (79%)
  matrix products  261 us (8%)
  blocking collectives  231 us (7%)
  local copies, waits for them, and re-layouts  105 us (3%)
  other arithmetic  42.6 us (1%)
    reduce_scatter x1, waiting for transfers between devices, shards(): lax.psum_scatter(in_grad, ('dp', 'fsdp'), scatter_dimension=1, tiled=True)  667 us
    reduce_scatter x1, waiting for transfers between devices, shards(): lax.psum_scatter(back_grad, ('dp', 'fsdp'), scatter_dimension=1, tiled=True)  666 us
    reduce_scatter x2, waiting for transfers between devices, send_attn(): lax.psum_scatter(qkv_grad, ('dp', 'fsdp'), scatter_dimension=0, tiled=True)  247 us
    all_gather x1, waiting for transfers between devices, expert_weights(): lax.all_gather(exp_in, ('dp', 'fsdp'), axis=1, tiled=True)  212 us
    all_gather x1, waiting for transfers between devices, expert_weights(): lax.all_gather(exp_out, ('dp', 'fsdp'), axis=1, tiled=True)  182 us
    reduce_scatter x1, waiting for transfers between devices, shards(): lax.psum_scatter(dense_back, ('dp', 'fsdp'), scatter_dimension=0, tiled=T...  142 us
    reduce_scatter x1, waiting for transfers between devices, shards(): lax.psum_scatter(dense_in, ('dp', 'fsdp'), scatter_dimension=0, tiled=True)  139 us
    unnamed x234, local copies, waits for them, and re-layouts  83.3 us
  transfers between devices with their start and end apart: 24, of which 15 were waited for; matrix products, arithmetic and copies ran while one was open for 8% of the time, Pallas kernels for 0%

commit v1 on v0

v1 whole, which is shorter than its diff:
```python
import jax
import jax.numpy as jnp
from jax import lax
from jax.sharding import PartitionSpec as P

HEADS = 12
HD = 64
EPSILON = 1e-06
NF = 4
ALL = ("dp", "fsdp")
BF = jnp.bfloat16
F32 = jnp.float32


def mm(left, right):
    return jnp.dot(left, right, preferred_element_type=F32)


def mm_tn(left, right):
    return lax.dot_general(left, right, (((0,), (0,)), ((), ())), preferred_element_type=F32)


def mm_nt(left, right):
    return lax.dot_general(left, right, (((1,), (1,)), ((), ())), preferred_element_type=F32)


def gelu(values):
    return 0.5 * values * (1.0 + lax.erf(values * (0.5**0.5)))


def gelu_slope(values):
    cdf = 0.5 * (1.0 + lax.erf(values * (0.5**0.5)))
    return cdf + values * jnp.exp(-0.5 * values * values) * 0.3989422804014327


def scale_rows(rows):
    centre = jnp.mean(rows, axis=-1, keepdims=True)
    centred = rows - centre
    inv_scale = lax.rsqrt(jnp.mean(centred * centred, axis=-1, keepdims=True) + EPSILON)
    return centred * inv_scale, inv_scale


def norm_back(out_grad, scaled, inv_scale, gain):
    weighted = out_grad * gain
    return inv_scale * (
        weighted
        - jnp.mean(weighted, axis=-1, keepdims=True)
        - scaled * jnp.mean(weighted * scaled, axis=-1, keepdims=True)
    )


def swap(value, bits):
    return lax.ppermute(value, "fsdp", [(i, i ^ bits) for i in range(NF)])


def gather_row(block):
    across = swap(block, 2)
    beside = swap(block, 1)
    corner = swap(across, 1)
    return jnp.concatenate([block, beside, across, corner], axis=0)


def scatter_row(partial):
    blocks = partial.reshape((NF, -1) + partial.shape[1:])
    send = jnp.stack([blocks[1], blocks[3]]).astype(BF)
    got = swap(send, 1).astype(F32)
    far = swap((blocks[2] + got[1]).astype(BF), 2).astype(F32)
    return blocks[0] + got[0] + far


def exchange(value, axes, groups=None):
    return lax.all_to_all(value, axes, 0, 0, axis_index_groups=groups, tiled=True)


def attend(qkv, code_row, live_all):
    tokens = qkv.shape[0]
    heads = HEADS // NF
    parts = qkv.reshape(tokens, 3, heads, HD)
    allowed = (code_row[:, None] == code_row[None, :])[None]
    scores = jnp.einsum("qhd,khd->hqk", parts[:, 0], parts[:, 1], preferred_element_type=F32)
    scores = jnp.where(allowed, scores * HD**-0.5, -1e30)
    top = jnp.max(scores, axis=-1, keepdims=True)
    shifted = jnp.exp(scores - top)
    total = jnp.sum(shifted, axis=-1, keepdims=True)
    low = (shifted / total).astype(BF)
    out = jnp.einsum("hqk,khd->qhd", low, parts[:, 2], preferred_element_type=F32)
    out = (out.reshape(tokens, heads * HD) * live_all[:, None]).astype(BF)
    return out, top + jnp.log(total)


def attend_back(qkv, out_grad, lse, code_row):
    tokens = qkv.shape[0]
    heads = HEADS // NF
    parts = qkv.reshape(tokens, 3, heads, HD)
    out_grad = out_grad.reshape(tokens, heads, HD)
    allowed = (code_row[:, None] == code_row[None, :])[None]
    scores = jnp.einsum("qhd,khd->hqk", parts[:, 0], parts[:, 1], preferred_element_type=F32)
    soft = jnp.exp(jnp.where(allowed, scores * HD**-0.5, -1e30) - lse)
    values_grad = jnp.einsum("hqk,qhd->khd", soft.astype(BF), out_grad, preferred_element_type=F32)
    soft_grad = jnp.einsum("qhd,khd->hqk", out_grad, parts[:, 2], preferred_element_type=F32)
    row_dot = jnp.sum(soft * soft_grad, axis=-1, keepdims=True)
    score_grad = (soft * (soft_grad - row_dot)).astype(BF)
    query_grad = jnp.einsum("hqk,khd->qhd", score_grad, parts[:, 1], preferred_element_type=F32)
    keys_grad = jnp.einsum("hqk,qhd->khd", score_grad, parts[:, 0], preferred_element_type=F32)
    scale = HD**-0.5
    grads = jnp.stack([query_grad * scale, keys_grad * scale, values_grad], axis=1)
    return grads.astype(BF).reshape(tokens, 3 * heads * HD)


def make_shards(n_dp):
    n_all = n_dp * NF

    def shards(
        patches, segment_ids, live, expert_ids, ranks, norm_gains, norm_biases, attn_qkv, attn_out,
        mlp_in, mlp_out, router, exp_in, exp_out, cotangent,
    ):
        width = patches.shape[-1]
        tokens = patches.shape[0] * patches.shape[1]
        experts = exp_in.shape[0]
        clones = n_dp // experts
        part = width // NF
        rows = attn_qkv.shape[1]
        hid = mlp_out.shape[0]
        own_f = lax.axis_index("fsdp")
        own_dp = lax.axis_index("dp")
        groups = ring = None
        if clones > 1:
            groups = [[g * experts + e for e in range(experts)] for g in range(clones)]
            ring = [[g * experts + e for g in range(clones)] for e in range(experts)]
        capacity = (210 * tokens + 100 * experts - 1) // (100 * experts)
        slots = (capacity + 7) // 8 * 8

        code = (segment_ids * 2 + live).reshape(tokens)
        code_all = gather_row(code)
        live_all = (code_all % 2).astype(F32)
        rows_all = gather_row(patches.reshape(tokens, width))

        def qkv_block(layer):
            weight = attn_qkv[layer].reshape(rows, 3, NF, part)
            return jnp.transpose(weight, (2, 0, 1, 3)).reshape(NF, rows, 3 * part)

        def to_everyone(blocks):
            full = jnp.broadcast_to(blocks[None], (n_dp,) + blocks.shape)
            full = full.reshape((n_all,) + blocks.shape[1:])
            return exchange(full, ALL).reshape((n_all * blocks.shape[1],) + blocks.shape[2:])

        small = jnp.concatenate(
            [norm_gains.T, norm_biases.T, router, jnp.zeros((rows, 128 - 8 - experts), BF)], axis=1
        )
        first = to_everyone(
            jnp.concatenate([jnp.broadcast_to(small[None], (NF, rows, 128)), qkv_block(0)], axis=2)
        )
        small_all, w_qkv0 = first[:, :128], first[:, 128:]
        norms = small_all[:, :8].T.astype(F32)
        gains, biases = norms[:4], norms[4:]
        w_router = small_all[:, 8 : 8 + experts]
        w_out0 = lax.all_gather(attn_out[0], ALL, axis=0, tiled=True)
        w_out1 = lax.all_gather(attn_out[1], ALL, axis=0, tiled=True)

        mlp_block = jnp.transpose(mlp_in.reshape(rows, n_dp, NF, hid), (2, 0, 1, 3))
        w_mlp_in = to_everyone(mlp_block.reshape(NF, rows, n_dp * hid))
        w_mlp_out = lax.all_gather(mlp_out, "dp", axis=0, tiled=True)
        w_qkv1 = to_everyone(qkv_block(1))

        in_block = jnp.transpose(exp_in.reshape(experts, rows, n_dp, NF, hid), (0, 3, 1, 2, 4))
        in_block = in_block.reshape(experts * NF, rows, n_dp * hid)
        if clones == 1:
            w_exp_in = exchange(in_block, ALL).reshape(width, n_dp * hid)
        else:
            held = in_block.reshape(experts, NF, rows, n_dp * hid)
            held = exchange(jnp.swapaxes(held, 0, 1), "fsdp")
            held = exchange(jnp.swapaxes(held, 0, 1), "dp", groups)
            w_exp_in = lax.all_gather(held, "dp", axis_index_groups=ring).reshape(width, n_dp * hid)
        w_exp_out = exchange(exp_out, "dp", groups)
        if clones > 1:
            w_exp_out = lax.all_gather(w_exp_out, "dp", axis_index_groups=ring)
        w_exp_out = w_exp_out.reshape(n_dp * hid, width)

        choice = expert_ids.reshape(tokens, 2)
        rank = ranks.reshape(tokens, 2)
        place = jnp.where(rank < capacity, choice * slots + rank, -1)
        slot_index = jnp.arange(experts * slots, dtype=jnp.int32)[:, None]
        pick = (place[:, 0][None] == slot_index) | (place[:, 1][None] == slot_index)
        pick = pick.astype(BF)

        def to_experts(block):
            held = mm(pick, block).astype(BF).reshape(experts, slots, width)
            return gather_row(exchange(held, "dp", groups).reshape(experts * slots, width))

        def from_experts(partial):
            held = scatter_row(partial).astype(BF).reshape(experts, slots, width)
            held = exchange(held, "dp", groups).reshape(experts * slots, width)
            return mm_tn(pick, held)

        top_grad = cotangent.reshape(tokens, width)
        dz = to_experts(top_grad)

        def out_project(out, weight):
            blocks = out.reshape(NF, tokens, part)
            total = None
            for k in range(NF):
                got = blocks[0] if k == 0 else swap(blocks[k], k)
                piece = lax.dynamic_slice_in_dim(weight, (own_f ^ k) * part, part, 0)
                term = mm(got, piece)
                total = term if total is None else total + term
            return total

        h0 = patches.reshape(tokens, width).astype(F32)
        xhat0_all, _ = scale_rows(rows_all.astype(F32))
        a0 = (xhat0_all * gains[0] + biases[0]).astype(BF)
        qkv0 = mm(a0, w_qkv0).astype(BF)
        o0, lse0 = attend(qkv0, code_all, live_all)
        h1 = h0 + out_project(o0, w_out0)

        xhat1, inv1 = scale_rows(h1)
        c0 = gather_row((xhat1 * gains[1] + biases[1]).astype(BF))
        u0 = mm(c0, w_mlp_in)
        g0 = gelu(u0).astype(BF)
        h2 = h1 + scatter_row(mm(g0, w_mlp_out))

        xhat2, inv2 = scale_rows(h2)
        a1 = gather_row((xhat2 * gains[2] + biases[2]).astype(BF))
        qkv1 = mm(a1, w_qkv1).astype(BF)
        o1, lse1 = attend(qkv1, code_all, live_all)
        h3 = h2 + out_project(o1, w_out1)

        xhat3, inv3 = scale_rows(h3)
        x = to_experts((xhat3 * gains[3] + biases[3]).astype(BF))
        probs = jax.nn.softmax(mm(x, w_router), axis=-1)
        mine = (jnp.arange(experts) == own_dp % experts).astype(F32)[None]
        prob = jnp.sum(probs * mine, axis=-1, keepdims=True)
        gate = prob.astype(BF).astype(F32)
        ue = mm(x, w_exp_in)
        ge = gelu(ue).astype(BF)
        y = mm(ge, w_exp_out)
        dyx = (gate * dz.astype(F32)).astype(BF)
        due = (mm_nt(dyx, w_exp_out) * gelu_slope(ue)).astype(BF)
        dgate = jnp.sum(dz.astype(F32) * y, axis=-1, keepdims=True)
        dlogits = (dgate * prob * (mine - probs)).astype(BF)
        dx = mm_nt(due, w_exp_in) + mm_nt(dlogits, w_router)
        router_part = mm_tn(x, dlogits)
        exp_in_part = mm_tn(x, due).astype(BF)
        exp_out_part = mm_tn(ge, dyx).astype(BF)

        dc1 = from_experts(dx)
        h4 = h3 + from_experts(gate * y)
        activations = h4.astype(BF)

        if clones == 1:
            got = exchange(exp_in_part.reshape(n_all, rows, n_dp * hid), ALL)
            got = got.reshape(experts, NF, rows, n_dp, hid)
            exp_in_grads = jnp.transpose(got, (0, 2, 3, 1, 4)).reshape(experts, rows, n_dp * NF * hid)
            got = exchange(exp_out_part.reshape(experts, hid, width), "dp")
            exp_out_grads = got.astype(F32)
        else:
            held = lax.psum_scatter(
                exp_in_part.reshape(clones, experts, NF, rows, n_dp * hid), "dp", axis_index_groups=ring
            )
            held = exchange(held, "dp", groups)
            held = exchange(jnp.swapaxes(held, 0, 1), "fsdp")
            got = held.reshape(NF, experts, rows, n_dp, hid)
            exp_in_grads = jnp.transpose(got, (1, 2, 3, 0, 4)).reshape(experts, rows, n_dp * NF * hid)
            held = lax.psum_scatter(
                exp_out_part.reshape(clones, experts, hid, width), "dp", axis_index_groups=ring
            )
            exp_out_grads = exchange(held, "dp", groups).astype(F32)
        exp_in_grads = exp_in_grads.astype(F32)

        def rows_to_owners(grad):
            cols = grad.shape[1]
            got = exchange(grad.astype(BF).reshape(n_all, rows, cols), ALL)
            return got.reshape(n_dp, NF, rows, cols).astype(F32)

        def qkv_layout(total):
            parts = total.reshape(NF, rows, 3, part)
            return jnp.transpose(parts, (1, 2, 0, 3)).reshape(rows, 3 * width)

        def out_to_owners(grad):
            got = exchange(grad.astype(BF).reshape(n_dp, rows, width), "dp")
            total = jnp.sum(got.astype(F32), axis=0)
            route = []
            for d in range(n_dp):
                for f in range(NF):
                    route.append((d * NF + f, f * n_dp + d))
            return lax.ppermute(total, ALL, route)

        def attention_back(grad, qkv, out, lse, a_all, w_qkv, w_out):
            dy = gather_row(grad.astype(BF))
            w_mine = lax.dynamic_slice_in_dim(w_out, own_f * part, part, 0)
            do = (mm_nt(dy, w_mine) * live_all[:, None]).astype(BF)
            out_part = mm_tn(out, dy)
            dqkv = attend_back(qkv, do, lse, code_all)
            return mm_nt(dqkv, w_qkv), mm_tn(a_all, dqkv), out_part

        def sums(out_grad, xhat):
            return jnp.sum(out_grad * xhat, axis=0), jnp.sum(out_grad, axis=0)

        gain3, bias3 = sums(dc1, xhat3)
        grad = top_grad.astype(F32) + norm_back(dc1, xhat3, inv3, gains[3])

        da1, qkv_part1, out_part1 = attention_back(grad, qkv1, o1, lse1, a1, w_qkv1, w_out1)
        proj1 = out_to_owners(out_part1)
        qkv_grad1 = qkv_layout(jnp.sum(rows_to_owners(qkv_part1), axis=0))
        da1 = scatter_row(da1)
        gain2, bias2 = sums(da1, xhat2)
        grad = grad + norm_back(da1, xhat2, inv2, gains[2])

        dm = gather_row(grad.astype(BF))
        du0 = (mm_nt(dm, w_mlp_out) * gelu_slope(u0)).astype(BF)
        mlp_out_part = mm_tn(g0, dm).astype(BF).reshape(n_dp, hid, width)
        mlp_out_grads = jnp.sum(exchange(mlp_out_part, "dp").astype(F32), axis=0)
        mlp_in_part = jnp.sum(rows_to_owners(mm_tn(c0, du0)), axis=0)
        mlp_in_part = mlp_in_part.reshape(NF, rows, n_dp, hid)
        mlp_in_grads = jnp.transpose(mlp_in_part, (1, 2, 0, 3)).reshape(rows, n_dp * NF * hid)
        dc0 = scatter_row(mm_nt(du0, w_mlp_in))
        gain1, bias1 = sums(dc0, xhat1)
        grad = grad + norm_back(dc0, xhat1, inv1, gains[1])

        da0, qkv_part0, out_part0 = attention_back(grad, qkv0, o0, lse0, a0, w_qkv0, w_out0)
        proj0 = out_to_owners(out_part0)
        gain0, bias0 = sums(da0, xhat0_all)
        columns = jnp.stack([gain0, gain1, gain2, gain3, bias0, bias1, bias2, bias3], axis=1)
        columns = jnp.concatenate(
            [columns, router_part, jnp.zeros((width, 128 - 8 - experts), F32), qkv_part0], axis=1
        )
        got = rows_to_owners(columns)
        total = jnp.sum(got, axis=0)
        small_grads = jnp.sum(total[:, :, :128], axis=0)
        qkv_grad0 = qkv_layout(total[:, :, 128:])
        da0 = scatter_row(da0)
        xhat0, inv0 = scale_rows(h0)
        grad = grad + norm_back(da0, xhat0, inv0, gains[0])

        norm_grads = small_grads[:, :8].T
        return (
            activations.reshape(patches.shape),
            grad.reshape(patches.shape),
            norm_grads[:4],
            norm_grads[4:7],
            norm_grads[7],
            jnp.stack([qkv_grad0, qkv_grad1]),
            jnp.stack([proj0, proj1]),
            mlp_in_grads,
            mlp_out_grads,
            small_grads[:, 8 : 8 + experts],
            exp_in_grads,
            exp_out_grads,
        )

    return shards


def solution(mesh):
    by_row = P("dp", "fsdp", None)
    second = P(None, ("dp", "fsdp"), None)
    first = P(("dp", "fsdp"), None)
    pair = P("dp", "fsdp")
    norm = P(None, ("dp", "fsdp"))
    return jax.shard_map(
        make_shards(mesh.shape["dp"]),
        mesh=mesh,
        in_specs=(
            by_row, pair, pair, by_row, by_row, norm, norm, second, second, first, first, first,
            second, second, by_row,
        ),
        out_specs=(
            by_row, by_row, norm, norm, P(("dp", "fsdp")), second, second, first, first, first,
            second, second,
        ),
        check_vma=False,
    )
```

time: 3240 us -> 704 us (0.22)
  waiting for transfers between devices: 2570 us -> 247 us
  blocking collectives: 231 us -> 20.8 us
  starting transfers between devices: 1.55 us -> 133 us
  matrix products: 261 us -> 150 us
  local copies, waits for them, and re-layouts: 105 us -> 69.6 us
    reduce_scatter x8 -> x0, waiting for transfers between devices: 1940 us -> none  [the longest x1 667 us: shards(): lax.psum_scatter(in_grad, ('dp', 'fsdp'), scatter_dimension=1, tiled=True)]
    all_gather x12 -> x3, waiting for transfers between devices: 608 us -> 44.7 us  [the longest x1 21.7 us: shards(): w_out1 = lax.all_gather(attn_out[1], ALL, axis=0, tiled=True)]
    all_gather x5 -> x0, blocking collectives: 186 us -> none  [the longest x2 76.2 us: attn_weights(): lax.all_gather(norm_biases[rows_pick], ('dp', 'fsdp'), axis=1, tiled=True)]
    ppermute x0 -> x47, waiting for transfers between devices: none -> 161 us  [the longest x45 143 us: swap(): return lax.ppermute(value, 'fsdp', [(i, i ^ bits) for i in range(NF)])]
    dot_general x46 -> x49, matrix products: 261 us -> 150 us  [the longest x17 38.8 us: mm(): return jnp.dot(left, right, preferred_element_type=F32)]
    all_to_all x0 -> x16, starting transfers between devices: none -> 81.7 us  [exchange(): lax.all_to_all(value, axes, 0, 0, axis_index_groups=groups, tiled=True)]
    unnamed x234 -> x242, local copies, waits for them, and re-layouts: 83.3 us -> 11.2 us
    ppermute x0 -> x47, starting transfers between devices: none -> 51.2 us  [the longest x45 44.4 us: swap(): return lax.ppermute(value, 'fsdp', [(i, i ^ bits) for i in range(NF)])]
  transfers between devices with their start and end apart: 24 -> 66, of which waited for: 15 -> 30; matrix products, arithmetic and copies ran while one was open for 8% -> 34% of each run, Pallas kernels for 0% -> 0%
where the time goes in v1:
time: 704 us; the launch traced here: 698 us
  waiting for transfers between devices  247 us (35%)
  matrix products  150 us (21%)
  starting transfers between devices  133 us (19%)
  local copies, waits for them, and re-layouts  69.6 us (10%)
  other arithmetic  61.9 us (9%)
  blocking collectives  20.8 us (3%)
  between operations  16.1 us (2%)
    ppermute x45, waiting for transfers between devices, swap(): return lax.ppermute(value, 'fsdp', [(i, i ^ bits) for i in range(NF)])  143 us
    all_to_all x16, starting transfers between devices, exchange(): lax.all_to_all(value, axes, 0, 0, axis_index_groups=groups, tiled=True)  81.7 us
    ppermute x45, starting transfers between devices, swap(): return lax.ppermute(value, 'fsdp', [(i, i ^ bits) for i in range(NF)])  44.4 us
    all_to_all x16, waiting for transfers between devices, exchange(): lax.all_to_all(value, axes, 0, 0, axis_index_groups=groups, tiled=True)  40.9 us
    dot_general x17, matrix products, mm(): return jnp.dot(left, right, preferred_element_type=F32)  38.8 us
    dot_general x11, matrix products, mm_tn(): lax.dot_general(left, right, (((0,), (0,)), ((), ())), preferred_element_...  33.7 us
    dot_general x9, matrix products, mm_nt(): lax.dot_general(left, right, (((1,), (1,)), ((), ())), preferred_element_...  31 us
    all_gather x1, waiting for transfers between devices, shards(): w_out1 = lax.all_gather(attn_out[1], ALL, axis=0, tiled=True)  21.7 us
  transfers between devices with their start and end apart: 66, of which 30 were waited for; matrix products, arithmetic and copies ran while one was open for 34% of the time, Pallas kernels for 0%

profile of v1, /device:TPU:5, one launch (start us, length us, event | category | flops | bytes accessed | tf_op | source)
XLA Modules:
  0.0 698.2 jit_solution(9786903410823661728)
XLA Ops:
  14.3 6.4 all-to-all-start
  23.4 17.2 %collective-permute-done.4 = s32[208]{0:T(256)S(1)} collective-permute-done((s32[208]{0:T(256)S(1)}, s32[208]{0:T(256)S(1)}, u32[]{:S(2)}, u32[]{:S(2)}) %collective-permute-start.4) | collective-permute-done | bytes 864 | tf_op jit(solution)/shard_map/ppermute | solution.py:53
  44.5 6.9 all-to-all-done
  83.8 8.9 %collective-permute-done.10 = bf16[208,768]{1,0:T(8,128)(2,1)S(1)} collective-permute-done((bf16[208,768]{1,0:T(8,128)(2,1)S(1)}, bf16[208,768]{1,0:T(8,128)(2,1)S(1)}, u32[]{:S(2)}, u32[]{:S(2)}) %collective-permute-start.10) | collective-permute-done | bytes 319520 | tf_op jit(solution)/shard_map/ppermute | solution.py:53
  100.0 18.1 %all-gather.6.cloned.1.call-done = bf16[768,768]{1,0:T(8,128)(2,1)} async-done(((bf16[96,768]{1,0:T(8,128)(2,1)}), bf16[768,768]{1,0:T(8,128)(2,1)}) %all-gather.6.cloned.1.call-update) | async-done | bytes 1179664 | tf_op jit(solution)/shard_map/all_gather | solution.py:162
  139.2 11.6 %collective-permute-done.15 = bf16[208,768]{1,0:T(8,128)(2,1)S(1)} collective-permute-done((bf16[208,768]{1,0:T(8,128)(2,1)S(1)}, bf16[208,768]{1,0:T(8,128)(2,1)S(1)}, u32[]{:S(2)}, u32[]{:S(2)}) %collective-permute-start.15) | collective-permute-done | bytes 319520 | tf_op jit(solution)/shard_map/ppermute | solution.py:53
  173.6 21.7 %all-gather.10.cloned.1.call-done = bf16[1,768,768]{2,1,0:T(8,128)(2,1)} async-done(((bf16[1,24,768]{2,1,0:T(8,128)(2,1)}), bf16[1,768,768]{2,1,0:T(8,128)(2,1)}) %all-gather.10.cloned.1.call-update) | async-done | bytes 1179664 | tf_op jit(solution)/shard_map/all_gather | solution.py:158
  229.9 27.0 %collective-permute-done.21 = bf16[448,768]{1,0:T(8,128)(2,1)} collective-permute-done((bf16[448,768]{1,0:T(8,128)(2,1)S(1)}, bf16[448,768]{1,0:T(8,128)(2,1)}, u32[]{:S(2)}, u32[]{:S(2)}) %collective-permute-start.21) | collective-permute-done | bytes 688160 | tf_op jit(solution)/shard_map/ppermute | solution.py:53
  264.5 7.2 %collective-permute-done.26 = bf16[448,768]{1,0:T(8,128)(2,1)} collective-permute-done((bf16[448,768]{1,0:T(8,128)(2,1)}, bf16[448,768]{1,0:T(8,128)(2,1)}, u32[]{:S(2)}, u32[]{:S(2)}) %collective-permute-start.26) | collective-permute-done | bytes 688160 | tf_op jit(solution)/shard_map/ppermute | solution.py:53
  275.2 7.6 %multiply_convert_fusion.2 = (bf16[1792,768]{1,0:T(8,128)(2,1)}, f32[1792,768]{1,0:T(8,128)}) fusion(bf16[768,768]{1,0:T(8,128)(2,1)} %bitcast.44, bf16[448,768]{1,0:T(8,128)(2,1)} %collective-permute-done.22, bf16[448,768]{1,0:T(8,128)(2,1)} %collective-permute-done.21, bf16[448,768]{1,0:T(8,128)(2,1)} %collective-permute-done.20, ...), kind=kOutput, calls=%fused_computation.27 | convolution fusion | flops 2131820544 | bytes 12189696 | tf_op jit(solution)/shard_map/dot_general | solution.py:16
  282.8 9.2 %all-to-all-done.5 = bf16[8,96,768]{2,1,0:T(8,128)(2,1)} async-done(((bf16[8,96,768]{2,1,0:T(8,128)(2,1)}), bf16[8,96,768]{2,1,0:T(8,128)(2,1)}, u32[]{:S(2)}, u32[]{:S(2)}) %all-to-all-start.5) | async-done | bytes 1179680 | tf_op jit(solution)/shard_map/all_to_all | solution.py:72
  292.0 7.9 %fusion.11 = bf16[1792,768]{1,0:T(8,128)(2,1)S(1)} fusion(f32[1792,768]{1,0:T(8,128)} %get-tuple-element.119, bf16[768,768]{1,0:T(8,128)(2,1)} %bitcast.45, f32[1792]{0:T(1024)S(1)} %convert_convert_fusion, bf16[448,768]{1,0:T(8,128)(2,1)} %collective-permute-done.27, bf16[448,768]{1,0:T(8,128)(2,1)} %collective-permute-done.26, ...), kind=kOutput, calls=%fused_computation.26 | convolution fusion | flops 2141454336 | bytes 12196864 | tf_op jit(solution)/shard_map/dot_general | solution.py:24
  304.6 7.3 %fusion.176 = (bf16[1792,768]{1,0:T(8,128)(2,1)}, f32[1792,768]{1,0:T(8,128)}, f32[1792]{0:T(1024)S(1)}) fusion(f32[1792]{0:T(1024)S(1)} %convert_convert_fusion, bf16[448,768]{1,0:T(8,128)(2,1)} %collective-permute-done.27, bf16[448,768]{1,0:T(8,128)(2,1)} %collective-permute-done.26, bf16[448,768]{1,0:T(8,128)(2,1)} %collective-permute-done.25, ...), kind=kOutput, calls=%fused_computation.340 | convolution fusion | flops 2130442496 | bytes 14956544 | tf_op jit(solution)/shard_map/dot_general | solution.py:16
  318.8 16.4 %collective-permute-done.29 = bf16[448,768]{1,0:T(8,128)(2,1)S(1)} collective-permute-done((bf16[448,768]{1,0:T(8,128)(2,1)S(1)}, bf16[448,768]{1,0:T(8,128)(2,1)S(1)}, u32[]{:S(2)}, u32[]{:S(2)}) %collective-permute-start.29) | collective-permute-done | bytes 688160 | tf_op jit(solution)/shard_map/ppermute | solution.py:53
  335.4 20.8 %all_to_all.85 = bf16[8,56,768]{2,1,0:T(8,128)(2,1)S(1)} all-to-all(bf16[8,56,768]{2,1,0:T(8,128)(2,1)S(1)} %bitcast.362), channel_id=1, replica_groups=mesh['dp'=8,'fsdp'=4] {'dp'}, dimensions={0} | all-to-all | bytes 1376256 | tf_op jit(solution)/shard_map/all_to_all | solution.py:72
  392.5 9.9 %multiply_convert_fusion.1 = bf16[3,832,832]{1,2,0:T(8,128)(2,1)} fusion(f32[3,832,832]{1,2,0:T(8,128)} %get-tuple-element.124, f32[3,832,832]{1,2,0:T(8,128)} %copy-done.1, f32[3,832]{1,0:T(4,128)S(1)} %get-tuple-element.123, f32[3,832]{1,0:T(4,128)S(1)} %log_add_fusion.1), kind=kLoop, calls=%fused_computation.3 | loop fusion | flops 8306688 | bytes 20786688 | tf_op jit(solution)/shard_map/convert_element_type | solution.py:102
  421.7 6.7 all-to-all-start.15
  436.6 27.8 %collective-permute-done.36 = bf16[208,768]{1,0:T(8,128)(2,1)} collective-permute-done((bf16[208,768]{1,0:T(8,128)(2,1)S(1)}, bf16[208,768]{1,0:T(8,128)(2,1)}, u32[]{:S(2)}, u32[]{:S(2)}) %collective-permute-start.36) | collective-permute-done | bytes 319520 | tf_op jit(solution)/shard_map/ppermute | solution.py:53
  485.8 7.6 %all-to-all-done.6 = bf16[8,56,768]{2,1,0:T(8,128)(2,1)S(1)} async-done(((bf16[8,56,768]{2,1,0:T(8,128)(2,1)}), bf16[8,56,768]{2,1,0:T(8,128)(2,1)S(1)}, u32[]{:S(2)}, u32[]{:S(2)}) %all-to-all-start.6) | async-done | bytes 688160 | tf_op jit(solution)/shard_map/all_to_all | solution.py:72
  517.5 11.5 %collective-permute-done.39 = bf16[208,768]{1,0:T(8,128)(2,1)S(1)} collective-permute-done((bf16[208,768]{1,0:T(8,128)(2,1)S(1)}, bf16[208,768]{1,0:T(8,128)(2,1)S(1)}, u32[]{:S(2)}, u32[]{:S(2)}) %collective-permute-start.39) | collective-permute-done | bytes 319520 | tf_op jit(solution)/shard_map/ppermute | solution.py:53
  577.9 8.7 %multiply_reduce_fusion = (f32[3,832]{1,0:T(4,128)S(1)}, f32[3,832,832]{1,2,0:T(8,128)}) fusion(f32[3,832,832]{1,2,0:T(8,128)} %copy-done, f32[3,832]{1,0:T(4,128)S(1)} %log_add_fusion, bf16[832,3,64]{0,2,1:T(8,128)(2,1)S(1)} %bitcast.372, bf16[832,3,3,64]{0,3,2,1:T(8,128)(2,1)S(1)} %bitcast.379), kind=kOutput, calls=%fused_computation.1 | convolution fusion | flops 272041536 | bytes 17325824 | tf_op jit(solution)/shard_map/qhd,khd->hqk/dot_general | solution.py:100
  592.3 9.8 %multiply_convert_fusion = bf16[3,832,832]{1,2,0:T(8,128)(2,1)} fusion(f32[3,832,832]{1,2,0:T(8,128)} %get-tuple-element.130, f32[3,832,832]{1,2,0:T(8,128)} %copy-done, f32[3,832]{1,0:T(4,128)S(1)} %get-tuple-element.129, f32[3,832]{1,0:T(4,128)S(1)} %log_add_fusion), kind=kLoop, calls=%fused_computation | loop fusion | flops 8306688 | bytes 20786688 | tf_op jit(solution)/shard_map/convert_element_type | solution.py:102
  606.5 6.3 all-to-all-start.13
  662.4 17.1 %collective-permute-done.46 = f32[24,768]{1,0:T(8,128)S(1)} collective-permute-done((f32[24,768]{1,0:T(8,128)S(1)}, f32[24,768]{1,0:T(8,128)S(1)}, u32[]{:S(2)}, u32[]{:S(2)}) %collective-permute-start.46) | collective-permute-done | bytes 73760 | tf_op jit(solution)/shard_map/ppermute | solution.py:285
  (552 shorter events, 382.6 us)
Async XLA Ops:
  7.2 67.7 %all-gather.8.cloned.1.call-start = ((), (), s32[]{:S(2)}) async-start(), calls=%async_computation.18 | async-start | bytes 1216512 | tf_op jit(solution)/shard_map/all_gather | solution.py:157
  14.3 37.0 %all-to-all-start = ((bf16[32,24,704]{2,1,0:T(8,128)(2,1)}), bf16[32,24,704]{2,1,0:T(8,128)(2,1)S(1)}, u32[]{:S(2)}, u32[]{:S(2)}) async-start(bf16[32,24,704]{2,1,0:T(8,128)(2,1)} %bitcast.4), calls=%async_computation | async-start | bytes 2359296 | tf_op jit(solution)/shard_map/all_to_all | solution.py:72
  20.7 97.4 %all-gather.6.cloned.1.call-start = ((), (), s32[]{:S(2)}) async-start(), calls=%async_computation.17 | async-start | bytes 1327104 | tf_op jit(solution)/shard_map/all_gather | solution.py:162
  52.6 40.6 %all-to-all-start.1 = ((bf16[32,24,768]{2,1,0:T(8,128)(2,1)}), bf16[32,24,768]{2,1,0:T(8,128)(2,1)}, u32[]{:S(2)}, u32[]{:S(2)}) async-start(bf16[32,24,768]{2,1,0:T(8,128)(2,1)} %bitcast.19), calls=%async_computation.1 | async-start | bytes 2359296 | tf_op jit(solution)/shard_map/all_to_all | solution.py:72
  127.7 29.4 %all-to-all-start.2 = ((bf16[32,24,576]{2,1,0:T(8,128)(2,1)}), bf16[32,24,576]{2,1,0:T(8,128)(2,1)}, u32[]{:S(2)}, u32[]{:S(2)}) async-start(bf16[32,24,576]{2,1,0:T(8,128)(2,1)} %bitcast.359), calls=%async_computation.2 | async-start | bytes 1966080 | tf_op jit(solution)/shard_map/all_to_all | solution.py:72
  132.4 62.9 %all-gather.10.cloned.1.call-start = ((), (), s32[]{:S(2)}) async-start(), calls=%async_computation.19 | async-start | bytes 1216512 | tf_op jit(solution)/shard_map/all_gather | solution.py:158
  157.1 43.2 %all-to-all-start.7 = ((bf16[8,56,768]{2,1,0:T(8,128)(2,1)}), bf16[8,56,768]{2,1,0:T(8,128)(2,1)S(1)}, u32[]{:S(2)}, u32[]{:S(2)}) async-start(bf16[8,56,768]{2,1,0:T(8,128)(2,1)} %bitcast.54), calls=%async_computation.7 | async-start | bytes 1376256 | tf_op jit(solution)/shard_map/all_to_all | solution.py:72
  222.9 35.4 %all-to-all-start.4 = ((bf16[32,24,768]{2,1,0:T(8,128)(2,1)}), bf16[32,24,768]{2,1,0:T(8,128)(2,1)}, u32[]{:S(2)}, u32[]{:S(2)}) async-start(bf16[32,24,768]{2,1,0:T(8,128)(2,1)} %reshape.569), calls=%async_computation.4 | async-start | bytes 2359296 | tf_op jit(solution)/shard_map/all_to_all | solution.py:72
  227.4 29.5 %collective-permute-start.21 = (bf16[448,768]{1,0:T(8,128)(2,1)S(1)}, bf16[448,768]{1,0:T(8,128)(2,1)}, u32[]{:S(2)}, u32[]{:S(2)}) collective-permute-start(bf16[448,768]{1,0:T(8,128)(2,1)S(1)} %bitcast.396), channel_id=1, source_target_pairs={{0,2},{1,3},{2,0},{3,1},{4,6},{5,7},{6,4},{7,5},{8,10},{9,11},{10,... | collective-permute-start | bytes 2064392 | tf_op jit(solution)/shard_map/ppermute | solution.py:53
  228.7 43.0 %collective-permute-start.26 = (bf16[448,768]{1,0:T(8,128)(2,1)}, bf16[448,768]{1,0:T(8,128)(2,1)}, u32[]{:S(2)}, u32[]{:S(2)}) collective-permute-start(bf16[448,768]{1,0:T(8,128)(2,1)} %bitcast.402), channel_id=1, source_target_pairs={{0,2},{1,3},{2,0},{3,1},{4,6},{5,7},{6,4},{7,5},{8,10},{9,11},{10,... | collective-permute-start | bytes 2064392 | tf_op jit(solution)/shard_map/ppermute | solution.py:53
  229.0 43.6 %collective-permute-start.20 = (bf16[448,768]{1,0:T(8,128)(2,1)S(1)}, bf16[448,768]{1,0:T(8,128)(2,1)}, u32[]{:S(2)}, u32[]{:S(2)}) collective-permute-start(bf16[448,768]{1,0:T(8,128)(2,1)S(1)} %bitcast.397), channel_id=1, source_target_pairs={{0,1},{1,0},{2,3},{3,2},{4,5},{5,4},{6,7},{7,6},{8,9},{9,8},{10,11... | collective-permute-start | bytes 2064392 | tf_op jit(solution)/shard_map/ppermute | solution.py:53
  258.3 33.7 %all-to-all-start.5 = ((bf16[8,96,768]{2,1,0:T(8,128)(2,1)}), bf16[8,96,768]{2,1,0:T(8,128)(2,1)}, u32[]{:S(2)}, u32[]{:S(2)}) async-start(bf16[8,96,768]{2,1,0:T(8,128)(2,1)} %param.28), calls=%async_computation.5 | async-start | bytes 2359296 | tf_op jit(solution)/shard_map/all_to_all | solution.py:72
  373.8 47.9 %all-to-all-start.16 = ((bf16[8,96,768]{2,1,0:T(8,128)(2,1)}), bf16[8,96,768]{2,1,0:T(8,128)(2,1)}, u32[]{:S(2)}, u32[]{:S(2)}) async-start(bf16[8,96,768]{2,1,0:T(8,128)(2,1)} %bitcast.388), calls=%async_computation.16 | async-start | bytes 2359296 | tf_op jit(solution)/shard_map/all_to_all | solution.py:72
  421.7 48.7 %all-to-all-start.15 = ((bf16[32,24,768]{2,1,0:T(8,128)(2,1)}), bf16[32,24,768]{2,1,0:T(8,128)(2,1)}, u32[]{:S(2)}, u32[]{:S(2)}) async-start(bf16[32,24,768]{2,1,0:T(8,128)(2,1)} %bitcast.389), calls=%async_computation.15 | async-start | bytes 2359296 | tf_op jit(solution)/shard_map/all_to_all | solution.py:72
  430.3 35.0 %collective-permute-start.24 = (bf16[448,768]{1,0:T(8,128)(2,1)S(1)}, bf16[448,768]{1,0:T(8,128)(2,1)S(1)}, u32[]{:S(2)}, u32[]{:S(2)}) collective-permute-start(bf16[448,768]{1,0:T(8,128)(2,1)S(1)} %fusion.40), channel_id=1, source_target_pairs={{0,2},{1,3},{2,0},{3,1},{4,6},{5,7},{6,4},{7,5},{8,10},{9,11},{10,... | collective-permute-start | bytes 2064392 | tf_op jit(solution)/shard_map/ppermute | solution.py:53
  434.9 29.5 %collective-permute-start.36 = (bf16[208,768]{1,0:T(8,128)(2,1)S(1)}, bf16[208,768]{1,0:T(8,128)(2,1)}, u32[]{:S(2)}, u32[]{:S(2)}) collective-permute-start(bf16[208,768]{1,0:T(8,128)(2,1)S(1)} %get-tuple-element.64), channel_id=1, source_target_pairs={{0,2},{1,3},{2,0},{3,1},{4,6},{5,7},{6,4},{7,5},{8,10},{9,11},{10,... | collective-permute-start | bytes 958472 | tf_op jit(solution)/shard_map/ppermute | solution.py:53
  435.6 40.2 %collective-permute-start.35 = (bf16[208,768]{1,0:T(8,128)(2,1)S(1)}, bf16[208,768]{1,0:T(8,128)(2,1)}, u32[]{:S(2)}, u32[]{:S(2)}) collective-permute-start(bf16[208,768]{1,0:T(8,128)(2,1)S(1)} %get-tuple-element.64), channel_id=1, source_target_pairs={{0,1},{1,0},{2,3},{3,2},{4,5},{5,4},{6,7},{7,6},{8,9},{9,8},{10,11... | collective-permute-start | bytes 958472 | tf_op jit(solution)/shard_map/ppermute | solution.py:53
  505.7 29.4 %all-to-all-start.10 = ((bf16[32,24,576]{2,1,0:T(8,128)(2,1)}), bf16[32,24,576]{2,1,0:T(8,128)(2,1)}, u32[]{:S(2)}, u32[]{:S(2)}) async-start(bf16[32,24,576]{2,1,0:T(8,128)(2,1)} %bitcast.358), calls=%async_computation.10 | async-start | bytes 1966080 | tf_op jit(solution)/shard_map/all_to_all | solution.py:72
  532.2 34.4 %collective-permute-start.41 = (bf16[208,768]{1,0:T(8,128)(2,1)}, bf16[208,768]{1,0:T(8,128)(2,1)}, u32[]{:S(2)}, u32[]{:S(2)}) collective-permute-start(bf16[208,768]{1,0:T(8,128)(2,1)} %get-tuple-element.61), channel_id=1, source_target_pairs={{0,2},{1,3},{2,0},{3,1},{4,6},{5,7},{6,4},{7,5},{8,10},{9,11},{10,... | collective-permute-start | bytes 958472 | tf_op jit(solution)/shard_map/ppermute | solution.py:53
  535.2 51.5 %all-to-all-start.14 = ((bf16[8,96,768]{2,1,0:T(8,128)(2,1)}), bf16[8,96,768]{2,1,0:T(8,128)(2,1)S(1)}, u32[]{:S(2)}, u32[]{:S(2)}) async-start(bf16[8,96,768]{2,1,0:T(8,128)(2,1)} %bitcast.386), calls=%async_computation.14 | async-start | bytes 2359296 | tf_op jit(solution)/shard_map/all_to_all | solution.py:72
  606.5 34.4 %all-to-all-start.13 = ((bf16[32,24,768]{2,1,0:T(8,128)(2,1)}), bf16[32,24,768]{2,1,0:T(8,128)(2,1)S(1)}, u32[]{:S(2)}, u32[]{:S(2)}) async-start(bf16[32,24,768]{2,1,0:T(8,128)(2,1)} %bitcast.387), calls=%async_computation.13 | async-start | bytes 2359296 | tf_op jit(solution)/shard_map/all_to_all | solution.py:72
  640.9 44.7 %all-to-all-start.9 = ((bf16[32,24,704]{2,1,0:T(8,128)(2,1)}), bf16[32,24,704]{2,1,0:T(8,128)(2,1)}, u32[]{:S(2)}, u32[]{:S(2)}) async-start(bf16[32,24,704]{2,1,0:T(8,128)(2,1)} %concatenate.86), calls=%async_computation.9 | async-start | bytes 2359296 | tf_op jit(solution)/shard_map/all_to_all | solution.py:72
  645.7 33.8 %collective-permute-start.46 = (f32[24,768]{1,0:T(8,128)S(1)}, f32[24,768]{1,0:T(8,128)S(1)}, u32[]{:S(2)}, u32[]{:S(2)}) collective-permute-start(f32[24,768]{1,0:T(8,128)S(1)} %convert_reduce_fusion.6), channel_id=1, source_target_pairs={{0,0},{1,8},{2,16},{3,24},{4,1},{5,9},{6,17},{7,25},{8,2},{9,10},{... | collective-permute-start | bytes 221192 | tf_op jit(solution)/shard_map/ppermute | solution.py:285
  650.9 29.8 %collective-permute-start.45 = (f32[24,768]{1,0:T(8,128)S(1)}, f32[24,768]{1,0:T(8,128)S(1)}, u32[]{:S(2)}, u32[]{:S(2)}) collective-permute-start(f32[24,768]{1,0:T(8,128)S(1)} %convert_reduce_fusion.7), channel_id=1, source_target_pairs={{0,0},{1,8},{2,16},{3,24},{4,1},{5,9},{6,17},{7,25},{8,2},{9,10},{... | collective-permute-start | bytes 221192 | tf_op jit(solution)/shard_map/ppermute | solution.py:285
  (161 other events, 2334.5 us)
Sparse Core Ops, SparseCore 0:
  11.5 63.3 all-gather.7
  77.0 41.0 all-gather.5
  137.2 58.1 all-gather.9

commit v2 on v1

v2 whole, which is shorter than its diff:
```python
import functools

import jax
import jax.numpy as jnp
from jax import lax
from jax.experimental import pallas as pl
from jax.experimental.pallas import tpu as pltpu
from jax.sharding import PartitionSpec as P

HEADS = 12
HD = 64
EPSILON = 1e-06
NF = 4
ALL = ("dp", "fsdp")
BF = jnp.bfloat16
F32 = jnp.float32


def mm(left, right):
    return jnp.dot(left, right, preferred_element_type=F32)


def mm_tn(left, right):
    return lax.dot_general(left, right, (((0,), (0,)), ((), ())), preferred_element_type=F32)


def mm_nt(left, right):
    return lax.dot_general(left, right, (((1,), (1,)), ((), ())), preferred_element_type=F32)


def gelu(values):
    return 0.5 * values * (1.0 + lax.erf(values * (0.5**0.5)))


def gelu_slope(values):
    cdf = 0.5 * (1.0 + lax.erf(values * (0.5**0.5)))
    return cdf + values * jnp.exp(-0.5 * values * values) * 0.3989422804014327


def scale_rows(rows):
    centre = jnp.mean(rows, axis=-1, keepdims=True)
    centred = rows - centre
    inv_scale = lax.rsqrt(jnp.mean(centred * centred, axis=-1, keepdims=True) + EPSILON)
    return centred * inv_scale, inv_scale


def norm_back(out_grad, scaled, inv_scale, gain):
    weighted = out_grad * gain
    return inv_scale * (
        weighted
        - jnp.mean(weighted, axis=-1, keepdims=True)
        - scaled * jnp.mean(weighted * scaled, axis=-1, keepdims=True)
    )


def swap(value, bits):
    return lax.ppermute(value, "fsdp", [(i, i ^ bits) for i in range(NF)])


def gather_blocks(block):
    across = swap(block, 2)
    beside = swap(block, 1)
    corner = swap(across, 1)
    return [block, beside, across, corner]


def gather_row(block):
    return jnp.concatenate(gather_blocks(block), axis=0)


def scatter_blocks(send, keep):
    got = swap(send, 1).astype(F32)
    far = swap((keep[1] + got[1]).astype(BF), 2).astype(F32)
    return keep[0] + got[0] + far


def scatter_row(partial):
    blocks = partial.reshape((NF, -1) + partial.shape[1:])
    return scatter_blocks(jnp.stack([blocks[1], blocks[3]]).astype(BF), (blocks[0], blocks[2]))


def after(value, *others):
    return lax.optimization_barrier((value,) + others)[0]


def deal(blocks):
    own = lax.axis_index("fsdp")
    got = []
    for k in range(NF):
        block = lax.dynamic_index_in_dim(blocks, own ^ k, 0, keepdims=False)
        got.append(block if k == 0 else swap(block, k))
    odd, far = own % 2 == 1, own >= 2
    got = [jnp.where(odd, got[k ^ 1], got[k]) for k in range(NF)]
    return jnp.stack([jnp.where(far, got[k ^ 2], got[k]) for k in range(NF)])


def exchange(value, axes, groups=None):
    return lax.all_to_all(value, axes, 0, 0, axis_index_groups=groups, tiled=True)


def dot(left, right, left_dim, right_dim):
    dims = (((left_dim,), (right_dim,)), ((), ()))
    return lax.dot_general(left, right, dims, preferred_element_type=F32)


def attend_kernel(qkv_ref, col_ref, row_ref, out_ref, lse_ref, *, heads):
    part = heads * HD
    live = (col_ref[...] % 2).astype(F32)
    for h in range(heads):
        q = qkv_ref[:, h * HD : (h + 1) * HD] * BF(HD**-0.5)
        k = qkv_ref[:, part + h * HD : part + (h + 1) * HD]
        v = qkv_ref[:, 2 * part + h * HD : 2 * part + (h + 1) * HD]
        scores = jnp.where(col_ref[...] == row_ref[...], dot(k, q, 1, 1), -1e30)
        top = jnp.max(scores, axis=0, keepdims=True)
        shifted = jnp.exp(scores - top)
        total = jnp.sum(shifted, axis=0, keepdims=True)
        soft = (shifted * (1.0 / total)).astype(BF)
        out_ref[:, h * HD : (h + 1) * HD] = (dot(soft, v, 0, 0) * live).astype(BF)
        lse_ref[h : h + 1] = top + jnp.log(total)


def attend_back_kernel(qkv_ref, do_ref, lse_ref, col_ref, row_ref, out_ref, *, heads):
    part = heads * HD
    for h in range(heads):
        q = qkv_ref[:, h * HD : (h + 1) * HD] * BF(HD**-0.5)
        k = qkv_ref[:, part + h * HD : part + (h + 1) * HD]
        v = qkv_ref[:, 2 * part + h * HD : 2 * part + (h + 1) * HD]
        do = do_ref[:, h * HD : (h + 1) * HD]
        soft = jnp.exp(dot(k, q, 1, 1) - lse_ref[h : h + 1])
        soft = jnp.where(col_ref[...] == row_ref[...], soft, 0.0)
        soft_grad = dot(v, do, 1, 1)
        row_dot = jnp.sum(soft * soft_grad, axis=0, keepdims=True)
        score_grad = (soft * (soft_grad - row_dot)).astype(BF)
        dq = dot(score_grad, k, 0, 0) * HD**-0.5
        out_ref[:, h * HD : (h + 1) * HD] = dq.astype(BF)
        dk = dot(score_grad, q, 1, 0)
        out_ref[:, part + h * HD : part + (h + 1) * HD] = dk.astype(BF)
        dv = dot(soft.astype(BF), do, 1, 0)
        out_ref[:, 2 * part + h * HD : 2 * part + (h + 1) * HD] = dv.astype(BF)


def whole(kernel, outs, args, flops):
    space = pl.BlockSpec(memory_space=pltpu.VMEM)
    return pl.pallas_call(
        kernel,
        out_shape=outs,
        in_specs=[space] * len(args),
        out_specs=jax.tree.map(lambda _: space, outs),
        compiler_params=pltpu.CompilerParams(vmem_limit_bytes=40 * 2**20),
        cost_estimate=pl.CostEstimate(flops=flops, bytes_accessed=2**21, transcendentals=0),
    )(*args)


def attend(qkv, code_row):
    tokens = qkv.shape[0]
    heads = HEADS // NF
    outs = (
        jax.ShapeDtypeStruct((tokens, heads * HD), BF),
        jax.ShapeDtypeStruct((heads, tokens), F32),
    )
    args = (qkv, code_row[:, None], code_row[None])
    return whole(functools.partial(attend_kernel, heads=heads), outs, args, 5 * 10**9)


def attend_back(qkv, out_grad, lse, code_row):
    heads = HEADS // NF
    outs = jax.ShapeDtypeStruct(qkv.shape, BF)
    args = (qkv, out_grad, lse, code_row[:, None], code_row[None])
    return whole(functools.partial(attend_back_kernel, heads=heads), outs, args, 7 * 10**9)


def expert_kernel(*refs, blocks):
    own_ref, x_refs, dz_refs = refs[0], refs[1 : 1 + blocks], refs[1 + blocks : 1 + 2 * blocks]
    in_ref, out_ref, router_ref = refs[1 + 2 * blocks : 4 + 2 * blocks]
    dx_send, dx_keep, y_send, y_keep, din_ref, dout_ref, drouter_ref = refs[4 + 2 * blocks :][:7]
    din, dout = refs[-2:]
    w_in, w_out, router = in_ref[...], out_ref[...], router_ref[...]
    drouter = None
    for i in range(blocks):
        x, dz = x_refs[i][...], dz_refs[i][...]
        ue = mm(x, w_in)
        cdf = 0.5 * (1.0 + lax.erf(ue * (0.5**0.5)))
        slope = cdf + ue * jnp.exp(-0.5 * ue * ue) * 0.3989422804014327
        ge = (ue * cdf).astype(BF)
        y = mm(ge, w_out)
        logits = mm(x, router)
        lane = lax.broadcasted_iota(jnp.int32, logits.shape, 1)
        shifted = jnp.exp(logits - jnp.max(logits, axis=1, keepdims=True))
        probs = shifted / jnp.sum(shifted, axis=1, keepdims=True)
        mine = (lane == own_ref[0]).astype(F32)
        prob = jnp.sum(probs * mine, axis=1, keepdims=True)
        gate = prob.astype(BF).astype(F32)
        dz_wide = dz.astype(F32)
        dyx = (gate * dz_wide).astype(BF)
        due = (dot(dyx, w_out, 1, 1) * slope).astype(BF)
        dgate = jnp.sum(dz_wide * y, axis=1, keepdims=True)
        dlogits = (dgate * prob * (mine - probs)).astype(BF)
        dx = dot(due, w_in, 1, 1) + dot(dlogits, router, 1, 1)
        y = gate * y
        if i % 2 == 0:
            dx_keep[i // 2], y_keep[i // 2] = dx, y
        else:
            dx_send[i // 2], y_send[i // 2] = dx.astype(BF), y.astype(BF)
        if i == 0:
            din[...], dout[...], drouter = dot(x, due, 0, 0), dot(ge, dyx, 0, 0), dot(x, dlogits, 0, 0)
        else:
            din[...] += dot(x, due, 0, 0)
            dout[...] += dot(ge, dyx, 0, 0)
            drouter += dot(x, dlogits, 0, 0)
    din_ref[...], dout_ref[...], drouter_ref[...] = din[...].astype(BF), dout[...].astype(BF), drouter


def expert_compute(own, x_blocks, dz_blocks, w_in, w_out, router):
    tall, width = x_blocks[0].shape
    hidden = w_in.shape[1]
    count = len(x_blocks)
    send = jax.ShapeDtypeStruct((count // 2, tall, width), BF)
    keep = jax.ShapeDtypeStruct((count // 2, tall, width), F32)
    outs = (
        send, keep, send, keep, jax.ShapeDtypeStruct(w_in.shape, BF), jax.ShapeDtypeStruct(w_out.shape, BF),
        jax.ShapeDtypeStruct(router.shape, F32),
    )
    space = pl.BlockSpec(memory_space=pltpu.VMEM)
    return pl.pallas_call(
        functools.partial(expert_kernel, blocks=count),
        out_shape=outs,
        in_specs=[pl.BlockSpec(memory_space=pltpu.SMEM)] + [space] * (2 * count + 3),
        out_specs=(space,) * len(outs),
        scratch_shapes=[pltpu.VMEM(w_in.shape, F32), pltpu.VMEM(w_out.shape, F32)],
        compiler_params=pltpu.CompilerParams(vmem_limit_bytes=56 * 2**20),
        cost_estimate=pl.CostEstimate(
            flops=16 * count * tall * width * hidden, bytes_accessed=2**24, transcendentals=0
        ),
    )(own.astype(jnp.int32)[None], *x_blocks, *dz_blocks, w_in, w_out, router)


def make_shards(n_dp):
    n_all = n_dp * NF

    def shards(
        patches, segment_ids, live, expert_ids, ranks, norm_gains, norm_biases, attn_qkv, attn_out,
        mlp_in, mlp_out, router, exp_in, exp_out, cotangent,
    ):
        width = patches.shape[-1]
        tokens = patches.shape[0] * patches.shape[1]
        experts = exp_in.shape[0]
        clones = n_dp // experts
        part = width // NF
        rows = attn_qkv.shape[1]
        hid = mlp_out.shape[0]
        own_f = lax.axis_index("fsdp")
        own_dp = lax.axis_index("dp")
        groups = ring = None
        if clones > 1:
            groups = [[g * experts + e for e in range(experts)] for g in range(clones)]
            ring = [[g * experts + e for g in range(clones)] for e in range(experts)]
        capacity = (210 * tokens + 100 * experts - 1) // (100 * experts)
        slots = (capacity + 7) // 8 * 8

        code = (segment_ids * 2 + live).reshape(tokens)
        code_all = gather_row(code)
        live_all = (code_all % 2).astype(F32)
        rows_all = gather_row(patches.reshape(tokens, width))

        def qkv_block(layer):
            weight = attn_qkv[layer].reshape(rows, 3, NF, part)
            return jnp.transpose(weight, (2, 0, 1, 3)).reshape(NF, rows, 3 * part)

        small = jnp.concatenate(
            [norm_gains.T, norm_biases.T, router, jnp.zeros((rows, 128 - 8 - experts), BF)], axis=1
        )
        small = jnp.broadcast_to(small[None], (NF, rows, 128))
        def to_everyone(blocks):
            full = jnp.broadcast_to(blocks[None], (n_dp,) + blocks.shape)
            return exchange(full.reshape((n_all, rows, -1)), ALL).reshape(width, -1)

        first = to_everyone(jnp.concatenate([small, qkv_block(0)], axis=2))
        small_all, w_qkv0 = first[:, :128], first[:, 128:]
        norms = small_all[:, :8].T.astype(F32)
        gains, biases = norms[:4], norms[4:]
        w_router = small_all[:, 8 : 8 + experts]

        mlp_block = jnp.transpose(mlp_in.reshape(rows, n_dp, NF, hid), (2, 0, 1, 3))
        mlp_block = deal(mlp_block.reshape(NF, rows, n_dp * hid)).reshape(NF * rows, width)
        mlp_all = lax.all_gather(jnp.concatenate([mlp_block, mlp_out], axis=0), "dp")
        w_mlp_in = mlp_all[:, : NF * rows].reshape(width, n_dp * hid)
        w_mlp_out = mlp_all[:, NF * rows :].reshape(n_dp * hid, width)

        to_heads = [(j, j % n_dp * NF + j // n_dp) for j in range(n_all)]
        to_owner = [(b, a) for a, b in to_heads]
        held = lax.ppermute(jnp.concatenate([attn_out[0], attn_out[1]], axis=0), ALL, to_heads)
        held = exchange(jnp.broadcast_to(after(held, first)[None], (n_dp,) + held.shape), "dp")
        w_out0, w_out1 = held[:, :rows].reshape(part, width), held[:, rows:].reshape(part, width)

        in_block = jnp.transpose(exp_in.reshape(experts, rows, n_dp, NF, hid), (0, 3, 1, 2, 4))
        in_block = in_block.reshape(experts * NF, rows, n_dp * hid)
        if clones == 1:
            held = jnp.broadcast_to(qkv_block(1)[None], (n_dp, NF, rows, 3 * part)).reshape(n_all, rows, -1)
            held = exchange(after(jnp.concatenate([in_block, held], axis=2), w_out0), ALL).reshape(width, -1)
            w_exp_in, w_qkv1 = held[:, : n_dp * hid], held[:, n_dp * hid :]
        else:
            held = in_block.reshape(experts, NF, rows, n_dp * hid)
            held = exchange(jnp.swapaxes(held, 0, 1), "fsdp")
            held = exchange(jnp.swapaxes(held, 0, 1), "dp", groups)
            w_exp_in = lax.all_gather(held, "dp", axis_index_groups=ring).reshape(width, n_dp * hid)
            w_qkv1 = to_everyone(qkv_block(1))
        choice = expert_ids.reshape(tokens, 2)
        rank = ranks.reshape(tokens, 2)
        place = jnp.where(rank < capacity, choice * slots + rank, -1)
        slot_index = jnp.arange(experts * slots, dtype=jnp.int32)[:, None]
        pick = (place[:, 0][None] == slot_index) | (place[:, 1][None] == slot_index)
        pick = pick.astype(BF)

        def to_experts(block):
            held = mm(pick, block).astype(BF).reshape(experts, slots, width)
            return exchange(held, "dp", groups).reshape(experts * slots, width)

        top_grad = cotangent.reshape(tokens, width)
        dz = to_experts(after(top_grad, w_exp_in))

        h0 = patches.reshape(tokens, width).astype(F32)
        xhat0_all, _ = scale_rows(rows_all.astype(F32))
        a0 = (xhat0_all * gains[0] + biases[0]).astype(BF)
        qkv0 = mm(a0, w_qkv0).astype(BF)
        o0, lse0 = attend(qkv0, code_all)
        h1 = h0 + scatter_row(mm(o0, w_out0))

        xhat1, inv1 = scale_rows(h1)
        c0 = gather_row((xhat1 * gains[1] + biases[1]).astype(BF))
        u0 = mm(c0, w_mlp_in)
        g0 = after(gelu(u0).astype(BF), w_qkv1)
        h2 = h1 + scatter_row(mm(g0, w_mlp_out))

        xhat2, inv2 = scale_rows(h2)
        a1 = after(gather_row((xhat2 * gains[2] + biases[2]).astype(BF)), w_exp_in)
        qkv1 = mm(a1, w_qkv1).astype(BF)
        o1, lse1 = attend(qkv1, code_all)
        h3 = h2 + scatter_row(mm(o1, w_out1))

        xhat3, inv3 = scale_rows(h3)
        c1 = after((xhat3 * gains[3] + biases[3]).astype(BF), dz)
        dz = gather_blocks(after(dz, c1))
        x = to_experts(c1)
        w_exp_out = exchange(after(exp_out, x, dz[2]), "dp", groups)
        if clones > 1:
            w_exp_out = lax.all_gather(w_exp_out, "dp", axis_index_groups=ring)
        w_exp_out = w_exp_out.reshape(n_dp * hid, width)
        x = gather_blocks(x)
        dx_send, dx_keep, y_send, y_keep, exp_in_part, exp_out_part, router_part = expert_compute(
            own_dp % experts, x, dz, w_exp_in, w_exp_out, w_router
        )
        dx = scatter_blocks(dx_send, dx_keep).astype(BF)
        y = scatter_blocks(after(y_send, dx), y_keep).astype(BF)
        dx = exchange(dx.reshape(experts, slots, width), "dp", groups)

        if clones == 1:
            back = exp_out_part.reshape(experts, hid, width)
            in_got = exchange(after(exp_in_part.reshape(n_all, rows, n_dp * hid), dx), ALL)
            got = exchange(after(back, in_got), "dp")
            exp_out_grads = got.astype(F32)
            in_got = in_got.reshape(experts, NF, rows, n_dp, hid)
            exp_in_grads = jnp.transpose(in_got, (0, 2, 3, 1, 4))
        else:
            back = lax.psum_scatter(
                exp_out_part.reshape(clones, experts, hid, width), "dp", axis_index_groups=ring
            )
            exp_out_grads = exchange(back, "dp", groups).astype(F32)
            got = exp_out_grads
            held = lax.psum_scatter(
                exp_in_part.reshape(clones, experts, NF, rows, n_dp * hid), "dp", axis_index_groups=ring
            )
            held = exchange(held, "dp", groups)
            held = exchange(jnp.swapaxes(held, 0, 1), "fsdp")
            in_got = held.reshape(NF, experts, rows, n_dp, hid)
            exp_in_grads = jnp.transpose(in_got, (1, 2, 3, 0, 4))
        exp_in_grads = exp_in_grads.reshape(experts, rows, n_dp * NF * hid).astype(F32)
        dc1 = mm_tn(pick, after(dx, exp_in_part).reshape(experts * slots, width))

        def rows_to_owners(grad):
            cols = grad.shape[1]
            got = exchange(grad.astype(BF).reshape(n_all, rows, cols), ALL)
            return got.reshape(n_dp, NF, rows, cols).astype(F32)

        def qkv_layout(total):
            parts = total.reshape(NF, rows, 3, part)
            return jnp.transpose(parts, (1, 2, 0, 3)).reshape(rows, 3 * width)

        def sums(out_grad, xhat):
            return jnp.sum(out_grad * xhat, axis=0), jnp.sum(out_grad, axis=0)

        gain3, bias3 = sums(dc1, xhat3)
        grad = top_grad.astype(F32) + norm_back(dc1, xhat3, inv3, gains[3])

        dy1 = gather_row(grad.astype(BF))
        do1 = (mm_nt(dy1, w_out1) * live_all[:, None]).astype(BF)
        dqkv1 = attend_back(qkv1, do1, lse1, code_all)
        da1 = scatter_row(mm_nt(after(dqkv1, in_got), w_qkv1))
        out_part1 = mm_tn(o1, dy1).astype(BF)
        qkv_part1 = mm_tn(a1, dqkv1).astype(BF)
        gain2, bias2 = sums(da1, xhat2)
        grad = grad + norm_back(da1, xhat2, inv2, gains[2])

        dm = gather_row(grad.astype(BF))
        du0 = (mm_nt(after(dm, qkv_part1, got), w_mlp_out) * gelu_slope(u0)).astype(BF)
        dc0 = scatter_row(mm_nt(du0, w_mlp_in))
        mlp_in_part = mm_tn(c0, du0).astype(BF)
        dense_part = jnp.concatenate(
            [
                mlp_in_part.reshape(n_dp, NF * rows, width),
                mm_tn(g0, dm).astype(BF).reshape(n_dp, NF * rows, width),
                qkv_part1.reshape(n_dp, NF * rows, 3 * part),
                out_part1.reshape(n_dp, NF * rows, part),
            ],
            axis=2,
        )
        dense_sum = lax.psum_scatter(dense_part, "dp")
        gain1, bias1 = sums(dc0, xhat1)
        grad = grad + norm_back(dc0, xhat1, inv1, gains[1])

        dy0 = gather_row(grad.astype(BF))
        do0 = (mm_nt(after(dy0, dense_part), w_out0) * live_all[:, None]).astype(BF)
        out_part0 = mm_tn(o0, dy0).astype(BF).reshape(n_dp, rows, width)
        y = y.reshape(experts, slots, width)
        if clones == 1:
            held = exchange(after(jnp.concatenate([y, out_part0], axis=1), got), "dp")
            y, out_got0 = held[:, :slots], held[:, slots:]
        else:
            y, out_got0 = exchange(y, "dp", groups), exchange(out_part0, "dp")
        h4 = h3 + mm_tn(pick, y.reshape(experts * slots, width))
        activations = h4.astype(BF)
        dqkv0 = attend_back(qkv0, do0, lse0, code_all)
        da0 = mm_nt(dqkv0, w_qkv0)
        qkv_part0 = mm_tn(a0, dqkv0)
        gain0, bias0 = sums(da0, xhat0_all)
        columns = jnp.stack([gain0, gain1, gain2, gain3, bias0, bias1, bias2, bias3], axis=1)
        columns = jnp.concatenate(
            [columns, router_part, jnp.zeros((width, 128 - 8 - experts), F32), qkv_part0], axis=1
        )
        tail = rows_to_owners(after(columns, y))
        total = jnp.sum(tail, axis=0)
        small_grads = jnp.sum(total[:, :, :128], axis=0)
        qkv_grad0 = qkv_layout(total[:, :, 128:])
        held = jnp.concatenate([dense_sum[:, :width], dense_sum[:, 2 * width : 2 * width + 3 * part]], axis=1)
        held = exchange(held.reshape(NF, rows, -1), "fsdp").astype(F32)
        mlp_in_grads = held[..., :width].reshape(NF, rows, n_dp, hid)
        mlp_in_grads = jnp.transpose(mlp_in_grads, (1, 2, 0, 3)).reshape(rows, n_dp * NF * hid)
        qkv_grad1 = qkv_layout(held[..., width:])
        mlp_out_grads = dense_sum[:, width : 2 * width].astype(F32)
        out_sum1 = dense_sum[:, 2 * width + 3 * part :].reshape(rows, width).astype(F32)
        out_sums = jnp.stack([jnp.sum(out_got0.astype(F32), axis=0), out_sum1])
        proj_grads = lax.ppermute(out_sums, ALL, to_owner)
        da0 = scatter_row(da0)
        xhat0, inv0 = scale_rows(h0)
        grad = grad + norm_back(da0, xhat0, inv0, gains[0])

        norm_grads = small_grads[:, :8].T
        return (
            activations.reshape(patches.shape),
            grad.reshape(patches.shape),
            norm_grads[:4],
            norm_grads[4:7],
            norm_grads[7],
            jnp.stack([qkv_grad0, qkv_grad1]),
            proj_grads,
            mlp_in_grads,
            mlp_out_grads,
            small_grads[:, 8 : 8 + experts],
            exp_in_grads,
            exp_out_grads,
        )

    return shards


def solution(mesh):
    by_row = P("dp", "fsdp", None)
    second = P(None, ("dp", "fsdp"), None)
    first = P(("dp", "fsdp"), None)
    pair = P("dp", "fsdp")
    norm = P(None, ("dp", "fsdp"))
    return jax.shard_map(
        make_shards(mesh.shape["dp"]),
        mesh=mesh,
        in_specs=(
            by_row, pair, pair, by_row, by_row, norm, norm, second, second, first, first, first,
            second, second, by_row,
        ),
        out_specs=(
            by_row, by_row, norm, norm, P(("dp", "fsdp")), second, second, first, first, first,
            second, second,
        ),
        check_vma=False,
    )
```

time: 704 us -> 587 us (0.83)
  matrix products: 150 us -> 45.4 us
  Pallas kernels: 0 us -> 49.2 us
  starting transfers between devices: 133 us -> 109 us
  waiting for transfers between devices: 247 us -> 229 us
  other arithmetic: 61.9 us -> 45.5 us
    pallas_call x0 -> x5, Pallas kernels: none -> 49.2 us  [the longest x4 25.8 us: whole(): pl.pallas_call(kernel, out_shape=outs, in_specs=[space] * len(args), out_...]
    all_to_all x16 -> x11, waiting for transfers between devices: 40.9 us -> 88.3 us  [exchange(): lax.all_to_all(value, axes, 0, 0, axis_index_groups=groups, tiled=True)]
    dot_general x12 -> x0, matrix products: 46.4 us -> none  [the longest x2 15 us: attend_back(): jnp.einsum('qhd,khd->hqk', out_grad, parts[:, 2], preferred_element_type=...]
    all_gather x3 -> x1, waiting for transfers between devices: 44.7 us -> 0.02 us  [shards(): lax.all_gather(jnp.concatenate([mlp_block, mlp_out], axis=0), 'dp')]
    all_to_all x16 -> x11, starting transfers between devices: 81.7 us -> 57.1 us  [exchange(): lax.all_to_all(value, axes, 0, 0, axis_index_groups=groups, tiled=True)]
    dot_general x17 -> x8, matrix products: 38.8 us -> 14.2 us  [mm(): return jnp.dot(left, right, preferred_element_type=F32)]
    ppermute x2, waiting for transfers between devices: 18.2 us -> 0.01 us  [the longest x1 0.01 us: shards(): lax.ppermute(jnp.concatenate([attn_out[0], attn_out[1]], axis=0), ALL, to...]
    convert_element_type x26 -> x25, other arithmetic: 34.1 us -> 16.4 us  [the longest x8 6.8 us: scatter_blocks(): far = swap((keep[1] + got[1]).astype(BF), 2).astype(F32)]
  transfers between devices with their start and end apart: 66 -> 61, of which waited for: 30 -> 33; matrix products, arithmetic and copies ran while one was open for 34% -> 20% of each run, Pallas kernels for 0% -> 4%
where the time goes in v2:
time: 587 us; the launch traced here: 579 us
  waiting for transfers between devices  229 us (39%)
  starting transfers between devices  109 us (19%)
  local copies, waits for them, and re-layouts  64.9 us (11%)
  Pallas kernels  49.2 us (8%)
  other arithmetic  45.5 us (8%)
  matrix products  45.4 us (8%)
  blocking collectives  20.6 us (4%)
  between operations  15.9 us (3%)
    ppermute x46, waiting for transfers between devices, swap(): return lax.ppermute(value, 'fsdp', [(i, i ^ bits) for i in range(NF)])  141 us
    all_to_all x11, waiting for transfers between devices, exchange(): lax.all_to_all(value, axes, 0, 0, axis_index_groups=groups, tiled=True)  88.3 us
    all_to_all x11, starting transfers between devices, exchange(): lax.all_to_all(value, axes, 0, 0, axis_index_groups=groups, tiled=True)  57.1 us
    ppermute x46, starting transfers between devices, swap(): return lax.ppermute(value, 'fsdp', [(i, i ^ bits) for i in range(NF)])  44.2 us
    pallas_call x4, Pallas kernels, whole(): pl.pallas_call(kernel, out_shape=outs, in_specs=[space] * len(args), out_...  25.8 us
    pallas_call x1, Pallas kernels, expert_compute(): pl.pallas_call(functools.partial(expert_kernel, blocks=count), out_shape=...  23.4 us
    all_to_all x1, blocking collectives, exchange(): lax.all_to_all(value, axes, 0, 0, axis_index_groups=groups, tiled=True)  20.6 us
    dot_general x8, matrix products, mm_tn(): lax.dot_general(left, right, (((0,), (0,)), ((), ())), preferred_element_...  16.7 us
  transfers between devices with their start and end apart: 61, of which 33 were waited for; matrix products, arithmetic and copies ran while one was open for 20% of the time, Pallas kernels for 4%

profile of v2, /device:TPU:5, one launch (start us, length us, event | category | flops | bytes accessed | tf_op | source)
XLA Modules:
  0.0 579.5 jit_solution(15387296361956115185)
XLA Ops:
  37.2 13.2 %all-to-all-done = bf16[32,24,704]{2,1,0:T(8,128)(2,1)S(1)} async-done(((bf16[32,24,704]{2,1,0:T(8,128)(2,1)}), bf16[32,24,704]{2,1,0:T(8,128)(2,1)S(1)}, u32[]{:S(2)}, u32[]{:S(2)}) %all-to-all-start) | async-done | bytes 1081376 | tf_op jit(solution)/shard_map/all_to_all | solution.py:98
  53.0 10.5 %all-to-all-start.1 = ((bf16[8,48,768]{2,1,0:T(8,128)(2,1)}), bf16[8,48,768]{2,1,0:T(8,128)(2,1)S(1)}, u32[]{:S(2)}, u32[]{:S(2)}) async-start(bf16[8,48,768]{2,1,0:T(8,128)(2,1)} %broadcast_in_dim.29), calls=%async_computation.1 | async-start | bytes 1179648 | tf_op jit(solution)/shard_map/all_to_all | solution.py:98
  74.1 17.7 %all-to-all-done.1 = bf16[8,48,768]{2,1,0:T(8,128)(2,1)S(1)} async-done(((bf16[8,48,768]{2,1,0:T(8,128)(2,1)}), bf16[8,48,768]{2,1,0:T(8,128)(2,1)S(1)}, u32[]{:S(2)}, u32[]{:S(2)}) %all-to-all-start.1) | async-done | bytes 589856 | tf_op jit(solution)/shard_map/all_to_all | solution.py:98
  95.9 8.8 %collective-permute-done.8 = bf16[208,768]{1,0:T(8,128)(2,1)S(1)} collective-permute-done((bf16[208,768]{1,0:T(8,128)(2,1)S(1)}, bf16[208,768]{1,0:T(8,128)(2,1)S(1)}, u32[]{:S(2)}, u32[]{:S(2)}) %collective-permute-start.8) | collective-permute-done | bytes 319520 | tf_op jit(solution)/shard_map/ppermute | solution.py:57
  137.3 16.2 %collective-permute-done.16 = bf16[208,768]{1,0:T(8,128)(2,1)S(1)} collective-permute-done((bf16[208,768]{1,0:T(8,128)(2,1)S(1)}, bf16[208,768]{1,0:T(8,128)(2,1)S(1)}, u32[]{:S(2)}, u32[]{:S(2)}) %collective-permute-start.16) | collective-permute-done | bytes 319520 | tf_op jit(solution)/shard_map/ppermute | solution.py:57
  156.0 6.7 %collective-permute-done.18 = bf16[208,768]{1,0:T(8,128)(2,1)S(1)} collective-permute-done((bf16[208,768]{1,0:T(8,128)(2,1)S(1)}, bf16[208,768]{1,0:T(8,128)(2,1)S(1)}, u32[]{:S(2)}, u32[]{:S(2)}) %collective-permute-start.18) | collective-permute-done | bytes 319520 | tf_op jit(solution)/shard_map/ppermute | solution.py:57
  166.7 8.5 %all-to-all-done.2 = bf16[32,24,1344]{2,1,0:T(8,128)(2,1)} async-done(((bf16[32,24,1344]{2,1,0:T(8,128)(2,1)}), bf16[32,24,1344]{2,1,0:T(8,128)(2,1)}, u32[]{:S(2)}, u32[]{:S(2)}) %all-to-all-start.2) | async-done | bytes 2064416 | tf_op jit(solution)/shard_map/all_to_all | solution.py:98
  180.1 5.1 shard_map.239
  201.4 12.6 %all-to-all-done.3 = bf16[8,56,768]{2,1,0:T(8,128)(2,1)} async-done(((bf16[8,56,768]{2,1,0:T(8,128)(2,1)}), bf16[8,56,768]{2,1,0:T(8,128)(2,1)}, u32[]{:S(2)}, u32[]{:S(2)}) %all-to-all-start.3) | async-done | bytes 688160 | tf_op jit(solution)/shard_map/all_to_all | solution.py:98
  220.2 15.2 %collective-permute-done.26.refs_7_ = bf16[448,768]{1,0:T(8,128)(2,1)} collective-permute-done((bf16[448,768]{1,0:T(8,128)(2,1)}, bf16[448,768]{1,0:T(8,128)(2,1)}, u32[]{:S(2)}, u32[]{:S(2)}) %collective-permute-start.26) | collective-permute-done | bytes 688160 | tf_op jit(solution)/shard_map/ppermute | solution.py:57
  245.4 11.4 %collective-permute-done.23.refs_3_ = bf16[448,768]{1,0:T(8,128)(2,1)} collective-permute-done((bf16[448,768]{1,0:T(8,128)(2,1)}, bf16[448,768]{1,0:T(8,128)(2,1)}, u32[]{:S(2)}, u32[]{:S(2)}) %collective-permute-start.23) | collective-permute-done | bytes 688160 | tf_op jit(solution)/shard_map/ppermute | solution.py:57
  262.1 7.3 %all-to-all-done.5 = bf16[8,96,768]{2,1,0:T(8,128)(2,1)} async-done(((bf16[8,96,768]{2,1,0:T(8,128)(2,1)}), bf16[8,96,768]{2,1,0:T(8,128)(2,1)}, u32[]{:S(2)}, u32[]{:S(2)}) %all-to-all-start.5) | async-done | bytes 1179680 | tf_op jit(solution)/shard_map/all_to_all | solution.py:98
  269.5 23.4 %shard_map.240 = (bf16[2,448,768]{2,1,0:T(8,128)(2,1)}, f32[2,448,768]{2,1,0:T(8,128)}, bf16[2,448,768]{2,1,0:T(8,128)(2,1)}, f32[2,448,768]{2,1,0:T(8,128)}, bf...) custom-call(s32[1]{0:T(128)} %bitcast.44.refs_0_, bf16[448,768]{1,0:T(8,128)(2,1)} %bitcast.49.refs_1_, ...), custom_call_target="tpu_custom_call" | custom-call | flops 16911433728 | bytes 16777216 | tf_op jit(solution)/shard_map/pallas_call | solution.py:224
  298.3 16.1 %collective-permute-done.29 = bf16[448,768]{1,0:T(8,128)(2,1)S(1)} collective-permute-done((bf16[448,768]{1,0:T(8,128)(2,1)S(1)}, bf16[448,768]{1,0:T(8,128)(2,1)S(1)}, u32[]{:S(2)}, u32[]{:S(2)}) %collective-permute-start.29) | collective-permute-done | bytes 688160 | tf_op jit(solution)/shard_map/ppermute | solution.py:57
  314.6 20.6 %all_to_all.60 = bf16[8,56,768]{2,1,0:T(8,128)(2,1)} all-to-all(bf16[8,56,768]{2,1,0:T(8,128)(2,1)S(1)} %bitcast.275), channel_id=1, replica_groups=mesh['dp'=8,'fsdp'=4] {'dp'}, dimensions={0} | all-to-all | bytes 1376256 | tf_op jit(solution)/shard_map/all_to_all | solution.py:98
  335.3 5.2 all-to-all-start.7
  345.2 14.8 %collective-permute-done.33 = bf16[208,768]{1,0:T(8,128)(2,1)S(1)} collective-permute-done((bf16[208,768]{1,0:T(8,128)(2,1)S(1)}, bf16[208,768]{1,0:T(8,128)(2,1)S(1)}, u32[]{:S(2)}, u32[]{:S(2)}) %collective-permute-start.33) | collective-permute-done | bytes 319520 | tf_op jit(solution)/shard_map/ppermute | solution.py:57
  362.9 7.9 %shard_map.241 = bf16[832,576]{1,0:T(8,128)(2,1)S(1)} custom-call(bf16[832,576]{1,0:T(8,128)(2,1)S(1)} %convolution_convert_fusion.2.qkv_ref, bf16[832,192]{1,0:T(8,128)(2,1)S(1)} %fusion.22.do_ref, f32[3,832]{1,0:T(4,128)S(1)} %get-tuple-element.57.lse_ref, s32[832,1]{1,0:T(8,128)S(1)} %broadcast_in_dim.35.col_ref, s32[1,832]{1,0:T(1,128)S(1)} %broadcast_in_dim.28.row_ref), custom_call_target="tpu_custom_call" | custom-call | flops 7000000000 | bytes 2097152 | tf_op jit(solution)/shard_map/pallas_call | solution.py:144
  381.3 5.6 all-to-all-start.8
  394.6 5.8 collective-permute-done.38
  437.9 6.4 %concatenate.71 = bf16[8,96,2304]{2,1,0:T(8,128)(2,1)} concatenate(bf16[8,96,768]{2,1,0:T(8,128)(2,1)} %bitcast.286, bf16[8,96,768]{2,1,0:T(8,128)(2,1)} %bitcast.285, bf16[8,96,576]{2,1,0:T(8,128)(2,1)S(1)} %bitcast.271, bf16[8,96,192]{2,1,0:T(8,128)(2,1)S(1)} %reshape.460), dimensions={2} | concatenate | bytes 7077888 | tf_op jit(solution)/shard_map/concatenate | solution.py:407
  452.3 17.4 %collective-permute-done.43 = bf16[208,768]{1,0:T(8,128)(2,1)S(1)} collective-permute-done((bf16[208,768]{1,0:T(8,128)(2,1)S(1)}, bf16[208,768]{1,0:T(8,128)(2,1)S(1)}, u32[]{:S(2)}, u32[]{:S(2)}) %collective-permute-start.43) | collective-permute-done | bytes 319520 | tf_op jit(solution)/shard_map/ppermute | solution.py:57
  480.1 7.8 %shard_map.242 = bf16[832,576]{1,0:T(8,128)(2,1)S(1)} custom-call(bf16[832,576]{1,0:T(8,128)(2,1)S(1)} %copy-done.1, bf16[832,192]{1,0:T(8,128)(2,1)S(1)} %fusion.23.do_ref, f32[3,832]{1,0:T(4,128)S(1)} %get-tuple-element.65.lse_ref, s32[832,1]{1,0:T(8,128)S(1)} %broadcast_in_dim.35.col_ref, s32[1,832]{1,0:T(1,128)S(1)} %broadcast_in_dim.28.row_ref), custom_call_target="tpu_custom_call" | custom-call | flops 7000000000 | bytes 2097152 | tf_op jit(solution)/shard_map/pallas_call | solution.py:144
  531.1 19.9 %all-to-all-done.10 = bf16[32,24,704]{2,1,0:T(8,128)(2,1)} async-done(((bf16[32,24,704]{2,1,0:T(8,128)(2,1)}), bf16[32,24,704]{2,1,0:T(8,128)(2,1)}, u32[]{:S(2)}, u32[]{:S(2)}) %all-to-all-start.10) | async-done | bytes 1081376 | tf_op jit(solution)/shard_map/all_to_all | solution.py:98
  (447 shorter events, 279.3 us)
Async XLA Ops:
  7.2 27.5 %collective-permute-start.1 = (bf16[208,768]{1,0:T(8,128)(2,1)}, bf16[208,768]{1,0:T(8,128)(2,1)S(1)}, u32[]{:S(2)}, u32[]{:S(2)}) collective-permute-start(bf16[208,768]{1,0:T(8,128)(2,1)} %bitcast.263), channel_id=1, source_target_pairs={{0,2},{1,3},{2,0},{3,1},{4,6},{5,7},{6,4},{7,5},{8,10},{9,11},{10,... | collective-permute-start | bytes 958472 | tf_op jit(solution)/shard_map/ppermute | solution.py:57
  8.5 27.1 %collective-permute-start = (bf16[208,768]{1,0:T(8,128)(2,1)}, bf16[208,768]{1,0:T(8,128)(2,1)S(1)}, u32[]{:S(2)}, u32[]{:S(2)}) collective-permute-start(bf16[208,768]{1,0:T(8,128)(2,1)} %bitcast.264), channel_id=1, source_target_pairs={{0,1},{1,0},{2,3},{3,2},{4,5},{5,4},{6,7},{7,6},{8,9},{9,8},{10,11... | collective-permute-start | bytes 958472 | tf_op jit(solution)/shard_map/ppermute | solution.py:57
  13.7 36.6 %all-to-all-start = ((bf16[32,24,704]{2,1,0:T(8,128)(2,1)}), bf16[32,24,704]{2,1,0:T(8,128)(2,1)S(1)}, u32[]{:S(2)}, u32[]{:S(2)}) async-start(bf16[32,24,704]{2,1,0:T(8,128)(2,1)} %bitcast.4), calls=%async_computation | async-start | bytes 2359296 | tf_op jit(solution)/shard_map/all_to_all | solution.py:98
  18.7 107.4 %all-gather.3.cloned.1.call-start = ((), (), s32[]{:S(2)}) async-start(), calls=%async_computation.14 | async-start | bytes 2654208 | tf_op jit(solution)/shard_map/all_gather | solution.py:285
  30.4 20.9 %collective-permute-start.6 = (bf16[48,768]{1,0:T(8,128)(2,1)}, bf16[48,768]{1,0:T(8,128)(2,1)}, u32[]{:S(2)}, u32[]{:S(2)}) collective-permute-start(bf16[48,768]{1,0:T(8,128)(2,1)} %pad_maximum_fusion.24), channel_id=1, source_target_pairs={{0,0},{1,4},{2,8},{3,12},{4,16},{5,20},{6,24},{7,28},{8,1},{9,5},{... | collective-permute-start | bytes 221192 | tf_op jit(solution)/shard_map/ppermute | solution.py:291
  53.0 38.7 %all-to-all-start.1 = ((bf16[8,48,768]{2,1,0:T(8,128)(2,1)}), bf16[8,48,768]{2,1,0:T(8,128)(2,1)S(1)}, u32[]{:S(2)}, u32[]{:S(2)}) async-start(bf16[8,48,768]{2,1,0:T(8,128)(2,1)} %broadcast_in_dim.29), calls=%async_computation.1 | async-start | bytes 1179648 | tf_op jit(solution)/shard_map/all_to_all | solution.py:98
  121.4 53.8 %all-to-all-start.2 = ((bf16[32,24,1344]{2,1,0:T(8,128)(2,1)}), bf16[32,24,1344]{2,1,0:T(8,128)(2,1)}, u32[]{:S(2)}, u32[]{:S(2)}) async-start(bf16[32,24,1344]{2,1,0:T(8,128)(2,1)} %pad_maximum_fusion), calls=%async_computation.2 | async-start | bytes 4325376 | tf_op jit(solution)/shard_map/all_to_all | solution.py:98
  136.1 17.5 %collective-permute-start.16 = (bf16[208,768]{1,0:T(8,128)(2,1)S(1)}, bf16[208,768]{1,0:T(8,128)(2,1)S(1)}, u32[]{:S(2)}, u32[]{:S(2)}) collective-permute-start(bf16[208,768]{1,0:T(8,128)(2,1)S(1)} %fusion.60), channel_id=1, source_target_pairs={{0,2},{1,3},{2,0},{3,1},{4,6},{5,7},{6,4},{7,5},{8,10},{9,11},{10,... | collective-permute-start | bytes 958472 | tf_op jit(solution)/shard_map/ppermute | solution.py:57
  192.2 21.8 %all-to-all-start.3 = ((bf16[8,56,768]{2,1,0:T(8,128)(2,1)}), bf16[8,56,768]{2,1,0:T(8,128)(2,1)}, u32[]{:S(2)}, u32[]{:S(2)}) async-start(bf16[8,56,768]{2,1,0:T(8,128)(2,1)} %bitcast.274), calls=%async_computation.3 | async-start | bytes 1376256 | tf_op jit(solution)/shard_map/all_to_all | solution.py:98
  215.1 21.9 %all-to-all-start.4 = ((bf16[8,56,768]{2,1,0:T(8,128)(2,1)}), bf16[8,56,768]{2,1,0:T(8,128)(2,1)}, u32[]{:S(2)}, u32[]{:S(2)}) async-start(bf16[8,56,768]{2,1,0:T(8,128)(2,1)} %bitcast.48), calls=%async_computation.4 | async-start | bytes 1376256 | tf_op jit(solution)/shard_map/all_to_all | solution.py:98
  219.7 15.7 %collective-permute-start.26 = (bf16[448,768]{1,0:T(8,128)(2,1)}, bf16[448,768]{1,0:T(8,128)(2,1)}, u32[]{:S(2)}, u32[]{:S(2)}) collective-permute-start(bf16[448,768]{1,0:T(8,128)(2,1)} %bitcast.47.refs_5_), channel_id=1, source_target_pairs={{0,2},{1,3},{2,0},{3,1},{4,6},{5,7},{6,4},{7,5},{8,10},{9,11},{10,... | collective-permute-start | bytes 2064392 | tf_op jit(solution)/shard_map/ppermute | solution.py:57
  237.0 32.5 %all-to-all-start.5 = ((bf16[8,96,768]{2,1,0:T(8,128)(2,1)}), bf16[8,96,768]{2,1,0:T(8,128)(2,1)}, u32[]{:S(2)}, u32[]{:S(2)}) async-start(bf16[8,96,768]{2,1,0:T(8,128)(2,1)} %param.28), calls=%async_computation.5 | async-start | bytes 2359296 | tf_op jit(solution)/shard_map/all_to_all | solution.py:98
  242.4 17.6 %collective-permute-start.25 = (bf16[448,768]{1,0:T(8,128)(2,1)}, bf16[448,768]{1,0:T(8,128)(2,1)}, u32[]{:S(2)}, u32[]{:S(2)}) collective-permute-start(bf16[448,768]{1,0:T(8,128)(2,1)} %bitcast.47.refs_5_), channel_id=1, source_target_pairs={{0,1},{1,0},{2,3},{3,2},{4,5},{5,4},{6,7},{7,6},{8,9},{9,8},{10,11... | collective-permute-start | bytes 2064392 | tf_op jit(solution)/shard_map/ppermute | solution.py:57
  297.7 16.7 %collective-permute-start.29 = (bf16[448,768]{1,0:T(8,128)(2,1)S(1)}, bf16[448,768]{1,0:T(8,128)(2,1)S(1)}, u32[]{:S(2)}, u32[]{:S(2)}) collective-permute-start(bf16[448,768]{1,0:T(8,128)(2,1)S(1)} %fusion.33), channel_id=1, source_target_pairs={{0,2},{1,3},{2,0},{3,1},{4,6},{5,7},{6,4},{7,5},{8,10},{9,11},{10,... | collective-permute-start | bytes 2064392 | tf_op jit(solution)/shard_map/ppermute | solution.py:57
  335.3 35.5 %all-to-all-start.7 = ((bf16[32,24,768]{2,1,0:T(8,128)(2,1)}), bf16[32,24,768]{2,1,0:T(8,128)(2,1)}, u32[]{:S(2)}, u32[]{:S(2)}) async-start(bf16[32,24,768]{2,1,0:T(8,128)(2,1)} %bitcast.292), calls=%async_computation.7 | async-start | bytes 2359296 | tf_op jit(solution)/shard_map/all_to_all | solution.py:98
  343.4 16.7 %collective-permute-start.33 = (bf16[208,768]{1,0:T(8,128)(2,1)S(1)}, bf16[208,768]{1,0:T(8,128)(2,1)S(1)}, u32[]{:S(2)}, u32[]{:S(2)}) collective-permute-start(bf16[208,768]{1,0:T(8,128)(2,1)S(1)} %get-tuple-element.147), channel_id=1, source_target_pairs={{0,2},{1,3},{2,0},{3,1},{4,6},{5,7},{6,4},{7,5},{8,10},{9,11},{10,... | collective-permute-start | bytes 958472 | tf_op jit(solution)/shard_map/ppermute | solution.py:57
  344.6 16.3 %collective-permute-start.32 = (bf16[208,768]{1,0:T(8,128)(2,1)S(1)}, bf16[208,768]{1,0:T(8,128)(2,1)S(1)}, u32[]{:S(2)}, u32[]{:S(2)}) collective-permute-start(bf16[208,768]{1,0:T(8,128)(2,1)S(1)} %get-tuple-element.147), channel_id=1, source_target_pairs={{0,1},{1,0},{2,3},{3,2},{4,5},{5,4},{6,7},{7,6},{8,9},{9,8},{10,11... | collective-permute-start | bytes 958472 | tf_op jit(solution)/shard_map/ppermute | solution.py:57
  381.3 33.4 %all-to-all-start.8 = ((bf16[8,96,768]{2,1,0:T(8,128)(2,1)}), bf16[8,96,768]{2,1,0:T(8,128)(2,1)}, u32[]{:S(2)}, u32[]{:S(2)}) async-start(bf16[8,96,768]{2,1,0:T(8,128)(2,1)} %bitcast.291), calls=%async_computation.8 | async-start | bytes 2359296 | tf_op jit(solution)/shard_map/all_to_all | solution.py:98
  386.9 165.7 %reduce-scatter.2.cloned.1.call-start = ((), (), s32[]{:S(2)}) async-start(), calls=%async_computation.13 | async-start | bytes 3981312 | tf_op jit(solution)/shard_map/reduce_scatter | solution.py:416
  446.4 24.8 %collective-permute-start.31 = (bf16[448,768]{1,0:T(8,128)(2,1)S(1)}, bf16[448,768]{1,0:T(8,128)(2,1)S(1)}, u32[]{:S(2)}, u32[]{:S(2)}) collective-permute-start(bf16[448,768]{1,0:T(8,128)(2,1)S(1)} %fusion.34), channel_id=1, source_target_pairs={{0,2},{1,3},{2,0},{3,1},{4,6},{5,7},{6,4},{7,5},{8,10},{9,11},{10,... | collective-permute-start | bytes 2064392 | tf_op jit(solution)/shard_map/ppermute | solution.py:57
  449.7 19.9 %collective-permute-start.43 = (bf16[208,768]{1,0:T(8,128)(2,1)S(1)}, bf16[208,768]{1,0:T(8,128)(2,1)S(1)}, u32[]{:S(2)}, u32[]{:S(2)}) collective-permute-start(bf16[208,768]{1,0:T(8,128)(2,1)S(1)} %get-tuple-element.141), channel_id=1, source_target_pairs={{0,2},{1,3},{2,0},{3,1},{4,6},{5,7},{6,4},{7,5},{8,10},{9,11},{10,... | collective-permute-start | bytes 958472 | tf_op jit(solution)/shard_map/ppermute | solution.py:57
  450.9 20.5 %collective-permute-start.42 = (bf16[208,768]{1,0:T(8,128)(2,1)S(1)}, bf16[208,768]{1,0:T(8,128)(2,1)S(1)}, u32[]{:S(2)}, u32[]{:S(2)}) collective-permute-start(bf16[208,768]{1,0:T(8,128)(2,1)S(1)} %get-tuple-element.141), channel_id=1, source_target_pairs={{0,1},{1,0},{2,3},{3,2},{4,5},{5,4},{6,7},{7,6},{8,9},{9,8},{10,11... | collective-permute-start | bytes 958472 | tf_op jit(solution)/shard_map/ppermute | solution.py:57
  474.6 27.8 %all-to-all-start.9 = ((bf16[8,80,768]{2,1,0:T(8,128)(2,1)}), bf16[8,80,768]{2,1,0:T(8,128)(2,1)S(1)}, u32[]{:S(2)}, u32[]{:S(2)}) async-start(bf16[8,80,768]{2,1,0:T(8,128)(2,1)} %pad_maximum_fusion.7), calls=%async_computation.9 | async-start | bytes 1966080 | tf_op jit(solution)/shard_map/all_to_all | solution.py:98
  503.9 47.2 %all-to-all-start.10 = ((bf16[32,24,704]{2,1,0:T(8,128)(2,1)}), bf16[32,24,704]{2,1,0:T(8,128)(2,1)}, u32[]{:S(2)}, u32[]{:S(2)}) async-start(bf16[32,24,704]{2,1,0:T(8,128)(2,1)} %bitcast.79), calls=%async_computation.10 | async-start | bytes 2359296 | tf_op jit(solution)/shard_map/all_to_all | solution.py:98
  (116 other events, 861.5 us)
Sparse Core Ops, SparseCore 0:
  35.7 61.1 all-gather.2
  444.5 105.4 reduce-scatter.1

commit v3 on v2

--- a/solution.py
+++ b/solution.py
@@ -103,7 +103,30 @@
     return lax.dot_general(left, right, dims, preferred_element_type=F32)
 
 
-def attend_kernel(qkv_ref, col_ref, row_ref, out_ref, lse_ref, *, heads):
+def put_partial(partial, send_ref, keep_ref):
+    tall = partial.shape[0] // NF
+    for k in range(NF):
+        block = partial[k * tall : (k + 1) * tall]
+        if k % 2 == 0:
+            keep_ref[k // 2] = block
+        else:
+            send_ref[k // 2] = block.astype(BF)
+
+
+def partial_shapes(tokens, width):
+    tall = tokens // NF
+    return (
+        jax.ShapeDtypeStruct((NF // 2, tall, width), BF),
+        jax.ShapeDtypeStruct((NF // 2, tall, width), F32),
+    )
+
+
+def attend_kernel(*refs, count, heads):
+    a_refs, (w_ref, wo_ref, col_ref, row_ref) = refs[:count], refs[count : count + 4]
+    qkv_ref, out_ref, lse_ref, send_ref, keep_ref = refs[count + 4 :]
+    tall = a_refs[0].shape[0]
+    for k in range(count):
+        qkv_ref[k * tall : (k + 1) * tall] = mm(a_refs[k][...], w_ref[...]).astype(BF)
     part = heads * HD
     live = (col_ref[...] % 2).astype(F32)
     for h in range(heads):
@@ -117,10 +140,17 @@
         soft = (shifted * (1.0 / total)).astype(BF)
         out_ref[:, h * HD : (h + 1) * HD] = (dot(soft, v, 0, 0) * live).astype(BF)
         lse_ref[h : h + 1] = top + jnp.log(total)
-
-
-def attend_back_kernel(qkv_ref, do_ref, lse_ref, col_ref, row_ref, out_ref, *, heads):
+    put_partial(mm(out_ref[...], wo_ref[...]), send_ref, keep_ref)
+
+
+def attend_back_kernel(*refs, count, heads):
+    dy_refs, (w_ref, wo_ref, qkv_ref, lse_ref, col_ref, row_ref) = refs[:count], refs[count : count + 6]
+    dqkv_ref, send_ref, keep_ref, do_ref = refs[count + 6 :]
+    tall = dy_refs[0].shape[0]
     part = heads * HD
+    for k in range(count):
+        live = (col_ref[k * tall : (k + 1) * tall] % 2).astype(F32)
+        do_ref[k * tall : (k + 1) * tall] = (dot(dy_refs[k][...], wo_ref[...], 1, 1) * live).astype(BF)
     for h in range(heads):
         q = qkv_ref[:, h * HD : (h + 1) * HD] * BF(HD**-0.5)
         k = qkv_ref[:, part + h * HD : part + (h + 1) * HD]
@@ -132,41 +162,121 @@
         row_dot = jnp.sum(soft * soft_grad, axis=0, keepdims=True)
         score_grad = (soft * (soft_grad - row_dot)).astype(BF)
         dq = dot(score_grad, k, 0, 0) * HD**-0.5
-        out_ref[:, h * HD : (h + 1) * HD] = dq.astype(BF)
+        dqkv_ref[:, h * HD : (h + 1) * HD] = dq.astype(BF)
         dk = dot(score_grad, q, 1, 0)
-        out_ref[:, part + h * HD : part + (h + 1) * HD] = dk.astype(BF)
+        dqkv_ref[:, part + h * HD : part + (h + 1) * HD] = dk.astype(BF)
         dv = dot(soft.astype(BF), do, 1, 0)
-        out_ref[:, 2 * part + h * HD : 2 * part + (h + 1) * HD] = dv.astype(BF)
-
-
-def whole(kernel, outs, args, flops):
+        dqkv_ref[:, 2 * part + h * HD : 2 * part + (h + 1) * HD] = dv.astype(BF)
+    put_partial(dot(dqkv_ref[...], w_ref[...], 1, 1), send_ref, keep_ref)
+
+
+def mlp_kernel(*refs):
+    c_refs, (in_ref, out_ref, u_ref, g_ref, send_ref, keep_ref) = refs[:NF], refs[NF:]
+    for k in range(NF):
+        u = mm(c_refs[k][...], in_ref[...])
+        u_ref[k] = u
+        g = gelu(u).astype(BF)
+        g_ref[k] = g
+        partial = mm(g, out_ref[...])
+        if k % 2 == 0:
+            keep_ref[k // 2] = partial
+        else:
+            send_ref[k // 2] = partial.astype(BF)
+
+
+def mlp_back_kernel(*refs):
+    dm_refs, (u_ref, in_ref, out_ref, du_ref, send_ref, keep_ref) = refs[:NF], refs[NF:]
+    for k in range(NF):
+        du = (dot(dm_refs[k][...], out_ref[...], 1, 1) * gelu_slope(u_ref[k])).astype(BF)
+        du_ref[k] = du
+        partial = dot(du, in_ref[...], 1, 1)
+        if k % 2 == 0:
+            keep_ref[k // 2] = partial
+        else:
+            send_ref[k // 2] = partial.astype(BF)
+
+
+def mlp_weights_kernel(*refs):
+    c_refs, dm_refs = refs[:NF], refs[NF : 2 * NF]
+    du_ref, g_ref, rest_ref, out_ref, sum_ref = refs[2 * NF :]
+    groups, rows, width = rest_ref.shape
+    for step in range(2):
+        for k in range(NF):
+            if step == 0:
+                term = dot(c_refs[k][...], du_ref[k], 0, 0)
+            else:
+                term = dot(g_ref[k], dm_refs[k][...], 0, 0)
+            if k == 0:
+                sum_ref[...] = term
+            else:
+                sum_ref[...] += term
+        for d in range(groups):
+            out_ref[d, :, step * width : (step + 1) * width] = sum_ref[d * rows : (d + 1) * rows].astype(BF)
+    for d in range(groups):
+        out_ref[d, :, 2 * width :] = rest_ref[d]
+
+
+def whole(kernel, outs, args, flops, scratch=()):
     space = pl.BlockSpec(memory_space=pltpu.VMEM)
     return pl.pallas_call(
         kernel,
         out_shape=outs,
         in_specs=[space] * len(args),
         out_specs=jax.tree.map(lambda _: space, outs),
-        compiler_params=pltpu.CompilerParams(vmem_limit_bytes=40 * 2**20),
+        scratch_shapes=scratch,
+        compiler_params=pltpu.CompilerParams(vmem_limit_bytes=48 * 2**20),
         cost_estimate=pl.CostEstimate(flops=flops, bytes_accessed=2**21, transcendentals=0),
     )(*args)
 
 
-def attend(qkv, code_row):
-    tokens = qkv.shape[0]
+def attend(a_blocks, w_qkv, w_out, code_row):
+    tokens, width = code_row.shape[0], w_qkv.shape[0]
     heads = HEADS // NF
+    part = heads * HD
     outs = (
-        jax.ShapeDtypeStruct((tokens, heads * HD), BF),
+        jax.ShapeDtypeStruct((tokens, 3 * part), BF),
+        jax.ShapeDtypeStruct((tokens, part), BF),
         jax.ShapeDtypeStruct((heads, tokens), F32),
-    )
-    args = (qkv, code_row[:, None], code_row[None])
-    return whole(functools.partial(attend_kernel, heads=heads), outs, args, 5 * 10**9)
-
-
-def attend_back(qkv, out_grad, lse, code_row):
+    ) + partial_shapes(tokens, width)
+    kernel = functools.partial(attend_kernel, count=len(a_blocks), heads=heads)
+    args = (*a_blocks, w_qkv, w_out, code_row[:, None], code_row[None])
+    return whole(kernel, outs, args, 8 * 10**9)
+
+
+def attend_back(dy_blocks, w_qkv, w_out, qkv, lse, code_row):
+    tokens, width = code_row.shape[0], w_qkv.shape[0]
     heads = HEADS // NF
-    outs = jax.ShapeDtypeStruct(qkv.shape, BF)
-    args = (qkv, out_grad, lse, code_row[:, None], code_row[None])
-    return whole(functools.partial(attend_back_kernel, heads=heads), outs, args, 7 * 10**9)
+    outs = (jax.ShapeDtypeStruct(qkv.shape, BF),) + partial_shapes(tokens, width)
+    kernel = functools.partial(attend_back_kernel, count=len(dy_blocks), heads=heads)
+    args = (*dy_blocks, w_qkv, w_out, qkv, lse, code_row[:, None], code_row[None])
+    return whole(kernel, outs, args, 11 * 10**9, (pltpu.VMEM((tokens, heads * HD), BF),))
+
+
+def mlp(c_blocks, w_in, w_out):
+    tall, width = c_blocks[0].shape
+    outs = (
+        jax.ShapeDtypeStruct((NF, tall, w_in.shape[1]), F32),
+        jax.ShapeDtypeStruct((NF, tall, w_in.shape[1]), BF),
+    ) + partial_shapes(NF * tall, width)
+    return whole(mlp_kernel, outs, (*c_blocks, w_in, w_out), 5 * 10**9)
+
+
+def mlp_back(dm_blocks, u, w_in, w_out):
+    tall, width = dm_blocks[0].shape
+    outs = (jax.ShapeDtypeStruct(u.shape, BF),) + partial_shapes(NF * tall, width)
+    return whole(mlp_back_kernel, outs, (*dm_blocks, u, w_in, w_out), 6 * 10**9)
+
+
+def mlp_weights(c_blocks, dm_blocks, du, g, rest):
+    groups, rows, width = rest.shape
+    if rows % 16 == 0:
+        outs = jax.ShapeDtypeStruct((groups, rows, 3 * width), BF)
+        args = (*c_blocks, *dm_blocks, du, g, rest)
+        return whole(mlp_weights_kernel, outs, args, 5 * 10**9, (pltpu.VMEM((width, width), F32),))
+    parts = [mm_tn(jnp.concatenate(c_blocks, axis=0), du.reshape(-1, width))]
+    parts.append(mm_tn(g.reshape(-1, width), jnp.concatenate(dm_blocks, axis=0)))
+    parts = [value.astype(BF).reshape(groups, rows, width) for value in parts]
+    return jnp.concatenate(parts + [rest], axis=2)
 
 
 def expert_kernel(*refs, blocks):
@@ -296,7 +406,9 @@
         in_block = in_block.reshape(experts * NF, rows, n_dp * hid)
         if clones == 1:
             held = jnp.broadcast_to(qkv_block(1)[None], (n_dp, NF, rows, 3 * part)).reshape(n_all, rows, -1)
-            held = exchange(after(jnp.concatenate([in_block, held], axis=2), w_out0), ALL).reshape(width, -1)
+            in_block = jnp.concatenate([in_block, held], axis=2)
+            w_qkv0 = after(w_qkv0, in_block)
+            held = exchange(after(in_block, w_out0), ALL).reshape(width, -1)
             w_exp_in, w_qkv1 = held[:, : n_dp * hid], held[:, n_dp * hid :]
         else:
             held = in_block.reshape(experts, NF, rows, n_dp * hid)
@@ -316,48 +428,51 @@
             return exchange(held, "dp", groups).reshape(experts * slots, width)
 
         top_grad = cotangent.reshape(tokens, width)
-        dz = to_experts(after(top_grad, w_exp_in))
+        if clones == 1:
+            dz = mm(pick, top_grad).astype(BF).reshape(experts, slots, width)
+            held = exchange(after(jnp.concatenate([dz, exp_out], axis=1), w_exp_in), "dp")
+            dz, w_exp_out = held[:, :slots].reshape(experts * slots, width), held[:, slots:]
+        else:
+            dz = to_experts(top_grad)
+            w_exp_out = exchange(exp_out, "dp", groups)
+            w_exp_out = lax.all_gather(w_exp_out, "dp", axis_index_groups=ring)
+        w_exp_out = w_exp_out.reshape(n_dp * hid, width)
 
         h0 = patches.reshape(tokens, width).astype(F32)
         xhat0_all, _ = scale_rows(rows_all.astype(F32))
         a0 = (xhat0_all * gains[0] + biases[0]).astype(BF)
-        qkv0 = mm(a0, w_qkv0).astype(BF)
-        o0, lse0 = attend(qkv0, code_all)
-        h1 = h0 + scatter_row(mm(o0, w_out0))
+        qkv0, o0, lse0, send, keep = attend([a0], w_qkv0, w_out0, code_all)
+        h1 = h0 + scatter_blocks(send, keep)
 
         xhat1, inv1 = scale_rows(h1)
-        c0 = gather_row((xhat1 * gains[1] + biases[1]).astype(BF))
-        u0 = mm(c0, w_mlp_in)
-        g0 = after(gelu(u0).astype(BF), w_qkv1)
-        h2 = h1 + scatter_row(mm(g0, w_mlp_out))
+        c0 = gather_blocks((xhat1 * gains[1] + biases[1]).astype(BF))
+        u0, g0, send, keep = mlp(c0, w_mlp_in, w_mlp_out)
+        h2 = h1 + scatter_blocks(send, keep)
 
         xhat2, inv2 = scale_rows(h2)
-        a1 = after(gather_row((xhat2 * gains[2] + biases[2]).astype(BF)), w_exp_in)
-        qkv1 = mm(a1, w_qkv1).astype(BF)
-        o1, lse1 = attend(qkv1, code_all)
-        h3 = h2 + scatter_row(mm(o1, w_out1))
+        a1 = gather_blocks(after((xhat2 * gains[2] + biases[2]).astype(BF), w_exp_in))
+        qkv1, o1, lse1, send, keep = attend(a1, w_qkv1, w_out1, code_all)
+        h3 = h2 + scatter_blocks(send, keep)
 
         xhat3, inv3 = scale_rows(h3)
-        c1 = after((xhat3 * gains[3] + biases[3]).astype(BF), dz)
+        c1 = after((xhat3 * gains[3] + biases[3]).astype(BF), dz, w_exp_out)
         dz = gather_blocks(after(dz, c1))
         x = to_experts(c1)
-        w_exp_out = exchange(after(exp_out, x, dz[2]), "dp", groups)
-        if clones > 1:
-            w_exp_out = lax.all_gather(w_exp_out, "dp", axis_index_groups=ring)
-        w_exp_out = w_exp_out.reshape(n_dp * hid, width)
         x = gather_blocks(x)
         dx_send, dx_keep, y_send, y_keep, exp_in_part, exp_out_part, router_part = expert_compute(
             own_dp % experts, x, dz, w_exp_in, w_exp_out, w_router
         )
         dx = scatter_blocks(dx_send, dx_keep).astype(BF)
         y = scatter_blocks(after(y_send, dx), y_keep).astype(BF)
+        y_summed = y
         dx = exchange(dx.reshape(experts, slots, width), "dp", groups)
 
         if clones == 1:
             back = exp_out_part.reshape(experts, hid, width)
+            back = jnp.concatenate([y.reshape(experts, slots, width), back], axis=1)
             in_got = exchange(after(exp_in_part.reshape(n_all, rows, n_dp * hid), dx), ALL)
             got = exchange(after(back, in_got), "dp")
-            exp_out_grads = got.astype(F32)
+            y, exp_out_grads = got[:, :slots], got[:, slots:].astype(F32)
             in_got = in_got.reshape(experts, NF, rows, n_dp, hid)
             exp_in_grads = jnp.transpose(in_got, (0, 2, 3, 1, 4))
         else:
@@ -366,6 +481,7 @@
             )
             exp_out_grads = exchange(back, "dp", groups).astype(F32)
             got = exp_out_grads
+            y = exchange(y.reshape(experts, slots, width), "dp", groups)
             held = lax.psum_scatter(
                 exp_in_part.reshape(clones, experts, NF, rows, n_dp * hid), "dp", axis_index_groups=ring
             )
@@ -374,7 +490,7 @@
             in_got = held.reshape(NF, experts, rows, n_dp, hid)
             exp_in_grads = jnp.transpose(in_got, (1, 2, 3, 0, 4))
         exp_in_grads = exp_in_grads.reshape(experts, rows, n_dp * NF * hid).astype(F32)
-        dc1 = mm_tn(pick, after(dx, exp_in_part).reshape(experts * slots, width))
+        dc1 = mm_tn(pick, after(dx, exp_in_part, y_summed).reshape(experts * slots, width))
 
         def rows_to_owners(grad):
             cols = grad.shape[1]
@@ -391,55 +507,48 @@
         gain3, bias3 = sums(dc1, xhat3)
         grad = top_grad.astype(F32) + norm_back(dc1, xhat3, inv3, gains[3])
 
-        dy1 = gather_row(grad.astype(BF))
-        do1 = (mm_nt(dy1, w_out1) * live_all[:, None]).astype(BF)
-        dqkv1 = attend_back(qkv1, do1, lse1, code_all)
-        da1 = scatter_row(mm_nt(after(dqkv1, in_got), w_qkv1))
-        out_part1 = mm_tn(o1, dy1).astype(BF)
-        qkv_part1 = mm_tn(a1, dqkv1).astype(BF)
+        dy1 = gather_blocks(grad.astype(BF))
+        dqkv1, send, keep = attend_back(dy1, w_qkv1, w_out1, qkv1, lse1, code_all)
+        da1 = scatter_blocks(after(send, in_got), keep)
+        attn_part = [
+            mm_tn(jnp.concatenate(a1, axis=0), dqkv1).astype(BF).reshape(n_dp, NF * rows, 3 * part),
+            mm_tn(o1, jnp.concatenate(dy1, axis=0)).astype(BF).reshape(n_dp, NF * rows, part),
+        ]
+        attn_part = jnp.concatenate(attn_part, axis=2)
         gain2, bias2 = sums(da1, xhat2)
         grad = grad + norm_back(da1, xhat2, inv2, gains[2])
 
-        dm = gather_row(grad.astype(BF))
-        du0 = (mm_nt(after(dm, qkv_part1, got), w_mlp_out) * gelu_slope(u0)).astype(BF)
-        dc0 = scatter_row(mm_nt(du0, w_mlp_in))
-        mlp_in_part = mm_tn(c0, du0).astype(BF)
-        dense_part = jnp.concatenate(
-            [
-                mlp_in_part.reshape(n_dp, NF * rows, width),
-                mm_tn(g0, dm).astype(BF).reshape(n_dp, NF * rows, width),
-                qkv_part1.reshape(n_dp, NF * rows, 3 * part),
-                out_part1.reshape(n_dp, NF * rows, part),
-            ],
-            axis=2,
-        )
+        dm = gather_blocks(grad.astype(BF))
+        du0, send, keep = mlp_back(dm, after(u0, attn_part), w_mlp_in, w_mlp_out)
+        dc0 = scatter_blocks(send, keep)
+        dense_part = mlp_weights(c0, dm, du0, after(g0, got), attn_part)
         dense_sum = lax.psum_scatter(dense_part, "dp")
         gain1, bias1 = sums(dc0, xhat1)
         grad = grad + norm_back(dc0, xhat1, inv1, gains[1])
 
-        dy0 = gather_row(grad.astype(BF))
-        do0 = (mm_nt(after(dy0, dense_part), w_out0) * live_all[:, None]).astype(BF)
-        out_part0 = mm_tn(o0, dy0).astype(BF).reshape(n_dp, rows, width)
-        y = y.reshape(experts, slots, width)
-        if clones == 1:
-            held = exchange(after(jnp.concatenate([y, out_part0], axis=1), got), "dp")
-            y, out_got0 = held[:, :slots], held[:, slots:]
-        else:
-            y, out_got0 = exchange(y, "dp", groups), exchange(out_part0, "dp")
+        dy0 = gather_blocks(grad.astype(BF))
+        dqkv0, send, keep = attend_back([after(dy0[0], dense_part), *dy0[1:]], w_qkv0, w_out0, qkv0, lse0, code_all)
+        out_part0 = mm_tn(o0, jnp.concatenate(dy0, axis=0)).astype(BF).reshape(n_dp, rows, width)
+        out_got0 = exchange(after(out_part0, got), "dp")
+        qkv_part0 = mm_tn(a0, dqkv0)
         h4 = h3 + mm_tn(pick, y.reshape(experts * slots, width))
         activations = h4.astype(BF)
-        dqkv0 = attend_back(qkv0, do0, lse0, code_all)
-        da0 = mm_nt(dqkv0, w_qkv0)
-        qkv_part0 = mm_tn(a0, dqkv0)
-        gain0, bias0 = sums(da0, xhat0_all)
+        da0 = scatter_blocks(send, keep)
+        xhat0_blocks = xhat0_all.reshape(NF, tokens, width)
+        gain0 = bias0 = 0.0
+        for k in range(NF):
+            block = keep[k // 2] if k % 2 == 0 else send[k // 2].astype(F32)
+            block_gain, block_bias = sums(block, xhat0_blocks[k])
+            gain0, bias0 = gain0 + block_gain, bias0 + block_bias
         columns = jnp.stack([gain0, gain1, gain2, gain3, bias0, bias1, bias2, bias3], axis=1)
         columns = jnp.concatenate(
             [columns, router_part, jnp.zeros((width, 128 - 8 - experts), F32), qkv_part0], axis=1
         )
-        tail = rows_to_owners(after(columns, y))
+        tail = rows_to_owners(after(columns, out_got0))
         total = jnp.sum(tail, axis=0)
         small_grads = jnp.sum(total[:, :, :128], axis=0)
         qkv_grad0 = qkv_layout(total[:, :, 128:])
+        dense_sum = after(dense_sum, tail)
         held = jnp.concatenate([dense_sum[:, :width], dense_sum[:, 2 * width : 2 * width + 3 * part]], axis=1)
         held = exchange(held.reshape(NF, rows, -1), "fsdp").astype(F32)
         mlp_in_grads = held[..., :width].reshape(NF, rows, n_dp, hid)
@@ -449,7 +558,6 @@
         out_sum1 = dense_sum[:, 2 * width + 3 * part :].reshape(rows, width).astype(F32)
         out_sums = jnp.stack([jnp.sum(out_got0.astype(F32), axis=0), out_sum1])
         proj_grads = lax.ppermute(out_sums, ALL, to_owner)
-        da0 = scatter_row(da0)
         xhat0, inv0 = scale_rows(h0)
         grad = grad + norm_back(da0, xhat0, inv0, gains[0])
 

time: 587 us -> 565 us (0.963)
  matrix products: 45.4 us -> 13.1 us
  Pallas kernels: 49.2 us -> 77.8 us
  blocking collectives: 20.6 us -> 0 us
  waiting for transfers between devices: 229 us -> 223 us
    pallas_call x4 -> x7, Pallas kernels: 25.8 us -> 54.6 us  [whole(): pl.pallas_call(kernel, out_shape=outs, in_specs=[space] * len(args), out_...]
    all_to_all x1 -> x0, blocking collectives: 20.6 us -> none  [exchange(): lax.all_to_all(value, axes, 0, 0, axis_index_groups=groups, tiled=True)]
    ppermute x46, waiting for transfers between devices: 141 us -> 123 us  [swap(): return lax.ppermute(value, 'fsdp', [(i, i ^ bits) for i in range(NF)])]
    reduce_scatter x1, waiting for transfers between devices: 0.02 us -> 15.2 us  [shards(): dense_sum = lax.psum_scatter(dense_part, 'dp')]
    dot_general x6 -> x0, matrix products: 14.5 us -> none  [mm_nt(): lax.dot_general(left, right, (((1,), (1,)), ((), ())), preferred_element_...]
    dot_general x8 -> x2, matrix products: 14.2 us -> 1.55 us  [mm(): return jnp.dot(left, right, preferred_element_type=F32)]
    unnamed x161 -> x221, local copies, waits for them, and re-layouts: 9.19 us -> 21.2 us
    all_to_all x11, waiting for transfers between devices: 88.3 us -> 79.5 us  [exchange(): lax.all_to_all(value, axes, 0, 0, axis_index_groups=groups, tiled=True)]
  transfers between devices with their start and end apart: 61 -> 61, of which waited for: 33 -> 34; matrix products, arithmetic and copies ran while one was open for 20% -> 16% of each run, Pallas kernels for 4% -> 10%
where the time goes in v3:
time: 565 us; the launch traced here: 556 us
  waiting for transfers between devices  223 us (39%)
  starting transfers between devices  108 us (19%)
  Pallas kernels  77.8 us (14%)
  local copies, waits for them, and re-layouts  70.6 us (12%)
  other arithmetic  47.8 us (8%)
  between operations  15.9 us (3%)
  matrix products  13.1 us (2%)
    ppermute x46, waiting for transfers between devices, swap(): return lax.ppermute(value, 'fsdp', [(i, i ^ bits) for i in range(NF)])  123 us
    all_to_all x11, waiting for transfers between devices, exchange(): lax.all_to_all(value, axes, 0, 0, axis_index_groups=groups, tiled=True)  79.5 us
    pallas_call x7, Pallas kernels, whole(): pl.pallas_call(kernel, out_shape=outs, in_specs=[space] * len(args), out_...  54.6 us
    all_to_all x11, starting transfers between devices, exchange(): lax.all_to_all(value, axes, 0, 0, axis_index_groups=groups, tiled=True)  53.8 us
    ppermute x46, starting transfers between devices, swap(): return lax.ppermute(value, 'fsdp', [(i, i ^ bits) for i in range(NF)])  46.9 us
    pallas_call x1, Pallas kernels, expert_compute(): pl.pallas_call(functools.partial(expert_kernel, blocks=count), out_shape=...  23.2 us
    unnamed x221, local copies, waits for them, and re-layouts  21.2 us
    reduce_scatter x1, waiting for transfers between devices, shards(): dense_sum = lax.psum_scatter(dense_part, 'dp')  15.2 us
  transfers between devices with their start and end apart: 61, of which 34 were waited for; matrix products, arithmetic and copies ran while one was open for 16% of the time, Pallas kernels for 10%

profile of v3, /device:TPU:5, one launch (start us, length us, event | category | flops | bytes accessed | tf_op | source)
XLA Modules:
  0.0 556.1 jit_solution(9625063154783385386)
XLA Ops:
  10.9 6.5 %all-to-all-start = ((bf16[32,24,704]{2,1,0:T(8,128)(2,1)}), bf16[32,24,704]{2,1,0:T(8,128)(2,1)}, u32[]{:S(2)}, u32[]{:S(2)}) async-start(bf16[32,24,704]{2,1,0:T(8,128)(2,1)} %bitcast.4), calls=%async_computation | async-start | bytes 2359296 | tf_op jit(solution)/shard_map/all_to_all | solution.py:98
  65.1 13.5 %all-to-all-done.1 = bf16[8,48,768]{2,1,0:T(8,128)(2,1)} async-done(((bf16[8,48,768]{2,1,0:T(8,128)(2,1)}), bf16[8,48,768]{2,1,0:T(8,128)(2,1)}, u32[]{:S(2)}, u32[]{:S(2)}) %all-to-all-start.1) | async-done | bytes 589856 | tf_op jit(solution)/shard_map/all_to_all | solution.py:98
  80.4 8.5 %shard_map.238 = (bf16[832,576]{1,0:T(8,128)(2,1)S(1)}, bf16[832,192]{1,0:T(8,128)(2,1)S(1)}, f32[3,832]{1,0:T(4,128)S(1)}, bf16[2,208,768]{2,1,0:T(8,128)(2,1)S(1)}, f32[2,208,768]{2,1,0:T(8,128)S(1)}) custom-call(bf16[832,768]{1,0:T(8,128)(2,1)} %get-tuple-element.203.refs_0_, bf16[768,576]{1,0:T(8,128)(2,1)S(1)} %slice.338.refs_1_.refs_4_, ...), custom_call_target="tpu_custom_call" | custom-call | flops 8000000000 | bytes 2097152 | tf_op jit(solution)/shard_map/pallas_call | solution.py:221
  105.9 18.1 %collective-permute-done.10.refs_2_ = bf16[208,768]{1,0:T(8,128)(2,1)S(1)} collective-permute-done((bf16[208,768]{1,0:T(8,128)(2,1)S(1)}, bf16[208,768]{1,0:T(8,128)(2,1)S(1)}, u32[]{:S(2)}, u32[]{:S(2)}) %collective-permute-start.10) | collective-permute-done | bytes 319520 | tf_op jit(solution)/shard_map/ppermute | solution.py:57
  139.2 11.5 %collective-permute-done.16 = bf16[208,768]{1,0:T(8,128)(2,1)S(1)} collective-permute-done((bf16[208,768]{1,0:T(8,128)(2,1)S(1)}, bf16[208,768]{1,0:T(8,128)(2,1)S(1)}, u32[]{:S(2)}, u32[]{:S(2)}) %collective-permute-start.16) | collective-permute-done | bytes 319520 | tf_op jit(solution)/shard_map/ppermute | solution.py:57
  157.1 6.8 %collective-permute-done.18.refs_2_ = bf16[208,768]{1,0:T(8,128)(2,1)} collective-permute-done((bf16[208,768]{1,0:T(8,128)(2,1)}, bf16[208,768]{1,0:T(8,128)(2,1)}, u32[]{:S(2)}, u32[]{:S(2)}) %collective-permute-start.18) | collective-permute-done | bytes 319520 | tf_op jit(solution)/shard_map/ppermute | solution.py:57
  172.5 9.3 %shard_map.240 = (bf16[832,576]{1,0:T(8,128)(2,1)S(1)}, bf16[832,192]{1,0:T(8,128)(2,1)S(1)}, f32[3,832]{1,0:T(4,128)S(1)}, bf16[2,208,768]{2,1,0:T(8,128)(2,1)S(1)}, f32[2,208,768]{2,1,0:T(8,128)}) custom-call(bf16[208,768]{1,0:T(8,128)(2,1)} %add_convert_fusion.2.refs_0_, bf16[208,768]{1,0:T(8,128)(2,1)} %collective-permute-done.17.refs_1_, ...), custom_call_target="tpu_custom_call" | custom-call | flops 8000000000 | bytes 2097152 | tf_op jit(solution)/shard_map/pallas_call | solution.py:221
  184.8 8.5 %collective-permute-done.21 = bf16[208,768]{1,0:T(8,128)(2,1)S(1)} collective-permute-done((bf16[208,768]{1,0:T(8,128)(2,1)S(1)}, bf16[208,768]{1,0:T(8,128)(2,1)S(1)}, u32[]{:S(2)}, u32[]{:S(2)}) %collective-permute-start.21) | collective-permute-done | bytes 319520 | tf_op jit(solution)/shard_map/ppermute | solution.py:57
  195.2 18.2 %all-to-all-done.3 = bf16[8,152,768]{2,1,0:T(8,128)(2,1)} async-done(((bf16[8,152,768]{2,1,0:T(8,128)(2,1)}), bf16[8,152,768]{2,1,0:T(8,128)(2,1)}, u32[]{:S(2)}, u32[]{:S(2)}) %all-to-all-start.3) | async-done | bytes 1867808 | tf_op jit(solution)/shard_map/all_to_all | solution.py:98
  224.9 15.8 %all-to-all-done.4 = bf16[8,56,768]{2,1,0:T(8,128)(2,1)} async-done(((bf16[8,56,768]{2,1,0:T(8,128)(2,1)}), bf16[8,56,768]{2,1,0:T(8,128)(2,1)}, u32[]{:S(2)}, u32[]{:S(2)}) %all-to-all-start.4) | async-done | bytes 688160 | tf_op jit(solution)/shard_map/all_to_all | solution.py:98
  244.1 12.5 %collective-permute-done.23.refs_3_ = bf16[448,768]{1,0:T(8,128)(2,1)} collective-permute-done((bf16[448,768]{1,0:T(8,128)(2,1)}, bf16[448,768]{1,0:T(8,128)(2,1)}, u32[]{:S(2)}, u32[]{:S(2)}) %collective-permute-start.23) | collective-permute-done | bytes 688160 | tf_op jit(solution)/shard_map/ppermute | solution.py:57
  261.0 23.2 %shard_map.241 = (bf16[2,448,768]{2,1,0:T(8,128)(2,1)}, f32[2,448,768]{2,1,0:T(8,128)}, bf16[2,448,768]{2,1,0:T(8,128)(2,1)}, f32[2,448,768]{2,1,0:T(8,128)}, bf...) custom-call(s32[1]{0:T(128)} %bitcast.38.refs_0_, bf16[448,768]{1,0:T(8,128)(2,1)} %bitcast.44.refs_1_, ...), custom_call_target="tpu_custom_call" | custom-call | flops 16911433728 | bytes 16777216 | tf_op jit(solution)/shard_map/pallas_call | solution.py:334
  289.1 15.5 %collective-permute-done.29 = bf16[448,768]{1,0:T(8,128)(2,1)S(1)} collective-permute-done((bf16[448,768]{1,0:T(8,128)(2,1)S(1)}, bf16[448,768]{1,0:T(8,128)(2,1)S(1)}, u32[]{:S(2)}, u32[]{:S(2)}) %collective-permute-start.29) | collective-permute-done | bytes 688160 | tf_op jit(solution)/shard_map/ppermute | solution.py:57
  316.9 12.3 %all-to-all-done.5 = bf16[8,56,768]{2,1,0:T(8,128)(2,1)} async-done(((bf16[8,56,768]{2,1,0:T(8,128)(2,1)}), bf16[8,56,768]{2,1,0:T(8,128)(2,1)}, u32[]{:S(2)}, u32[]{:S(2)}) %all-to-all-start.5) | async-done | bytes 688160 | tf_op jit(solution)/shard_map/all_to_all | solution.py:98
  342.3 10.9 %collective-permute-done.33.refs_2_ = bf16[208,768]{1,0:T(8,128)(2,1)S(1)} collective-permute-done((bf16[208,768]{1,0:T(8,128)(2,1)S(1)}, bf16[208,768]{1,0:T(8,128)(2,1)S(1)}, u32[]{:S(2)}, u32[]{:S(2)}) %collective-permute-start.33) | collective-permute-done | bytes 319520 | tf_op jit(solution)/shard_map/ppermute | solution.py:57
  355.7 10.2 %shard_map.242 = (bf16[832,576]{1,0:T(8,128)(2,1)S(1)}, bf16[2,208,768]{2,1,0:T(8,128)(2,1)S(1)}, f32[2,208,768]{2,1,0:T(8,128)}) custom-call(bf16[208,768]{1,0:T(8,128)(2,1)S(1)} %get-tuple-element.195.refs_0_, bf16[208,768]{1,0:T(8,128)(2,1)S(1)} %collective-permute-done.32.refs_1_, bf16[208,768]{1,0:T(8,128)(2,1)S(1)} %collective-permute-done.33.refs_2_, ...), custom_call_target="tpu_custom_call" | custom-call | flops 11000000512 | bytes 2097152 | tf_op jit(solution)/shard_map/pallas_call | solution.py:221
  407.0 5.4 shard_map.243
  416.4 11.9 %all-to-all-done.7 = bf16[8,152,768]{2,1,0:T(8,128)(2,1)} async-done(((bf16[8,152,768]{2,1,0:T(8,128)(2,1)}), bf16[8,152,768]{2,1,0:T(8,128)(2,1)}, u32[]{:S(2)}, u32[]{:S(2)}) %all-to-all-start.7) | async-done | bytes 1867808 | tf_op jit(solution)/shard_map/all_to_all | solution.py:98
  429.7 6.3 %shard_map.244 = bf16[8,96,2304]{2,1,0:T(8,128)(2,1)} custom-call(bf16[208,768]{1,0:T(8,128)(2,1)S(1)} %copy-done.9, bf16[208,768]{1,0:T(8,128)(2,1)S(1)} %copy-done.21, bf16[208,768]{1,0:T(8,128)(2,1)S(1)} %copy-done.18, bf16[208,768]{1,0:T(8,128)(2,1)} %collective-permute-done.11.refs_3_, bf16[208,768]{1,0:T(8,128)(2,1)} %get-tuple-element.192.refs_0_.refs_4_, ...), custom_call_target="tpu_custom_call" | custom-call | flops 5000000000 | bytes 2097152 | tf_op jit(solution)/shard_map/pallas_call | solution.py:221
  459.1 10.1 %shard_map.245 = (bf16[832,576]{1,0:T(8,128)(2,1)S(1)}, bf16[2,208,768]{2,1,0:T(8,128)(2,1)S(1)}, f32[2,208,768]{2,1,0:T(8,128)}) custom-call(bf16[208,768]{1,0:T(8,128)(2,1)S(1)} %get-tuple-element.97.refs_0_, bf16[208,768]{1,0:T(8,128)(2,1)S(1)} %collective-permute-done.42.refs_1_, bf16[208,768]{1,0:T(8,128)(2,1)S(1)} %collective-permute-done.43.refs_2_, ...), custom_call_target="tpu_custom_call" | custom-call | flops 11000000512 | bytes 2097152 | tf_op jit(solution)/shard_map/pallas_call | solution.py:221
  477.7 6.1 %all-to-all-start.9 = ((bf16[32,24,704]{2,1,0:T(8,128)(2,1)}), bf16[32,24,704]{2,1,0:T(8,128)(2,1)}, u32[]{:S(2)}, u32[]{:S(2)}) async-start(bf16[32,24,704]{2,1,0:T(8,128)(2,1)} %bitcast.69), calls=%async_computation.9 | async-start | bytes 2359296 | tf_op jit(solution)/shard_map/all_to_all | solution.py:98
  497.3 6.2 %collective-permute-done.46 = bf16[208,768]{1,0:T(8,128)(2,1)S(1)} collective-permute-done((bf16[208,768]{1,0:T(8,128)(2,1)S(1)}, bf16[208,768]{1,0:T(8,128)(2,1)S(1)}, u32[]{:S(2)}, u32[]{:S(2)}) %collective-permute-start.46) | collective-permute-done | bytes 319520 | tf_op jit(solution)/shard_map/ppermute | solution.py:57
  505.0 6.7 %all-to-all-done.9 = bf16[32,24,704]{2,1,0:T(8,128)(2,1)} async-done(((bf16[32,24,704]{2,1,0:T(8,128)(2,1)}), bf16[32,24,704]{2,1,0:T(8,128)(2,1)}, u32[]{:S(2)}, u32[]{:S(2)}) %all-to-all-start.9) | async-done | bytes 1081376 | tf_op jit(solution)/shard_map/all_to_all | solution.py:98
  513.4 15.2 %reduce-scatter.2.cloned.1.call-done = bf16[1,96,2304]{2,1,0:T(8,128)(2,1)} async-done(((bf16[8,96,2304]{2,1,0:T(8,128)(2,1)}), bf16[1,96,2304]{2,1,0:T(8,128)(2,1)}) %reduce-scatter.2.cloned.1.call-update) | async-done | bytes 442384 | tf_op jit(solution)/shard_map/reduce_scatter | solution.py:525
  (490 shorter events, 271.0 us)
Async XLA Ops:
  10.9 39.6 %all-to-all-start = ((bf16[32,24,704]{2,1,0:T(8,128)(2,1)}), bf16[32,24,704]{2,1,0:T(8,128)(2,1)}, u32[]{:S(2)}, u32[]{:S(2)}) async-start(bf16[32,24,704]{2,1,0:T(8,128)(2,1)} %bitcast.4), calls=%async_computation | async-start | bytes 2359296 | tf_op jit(solution)/shard_map/all_to_all | solution.py:98
  17.4 109.5 %all-gather.3.cloned.1.call-start = ((), (), s32[]{:S(2)}) async-start(), calls=%async_computation.13 | async-start | bytes 2654208 | tf_op jit(solution)/shard_map/all_gather | solution.py:395
  17.4 26.5 %collective-permute-start.1 = (bf16[208,768]{1,0:T(8,128)(2,1)S(1)}, bf16[208,768]{1,0:T(8,128)(2,1)S(1)}, u32[]{:S(2)}, u32[]{:S(2)}) collective-permute-start(bf16[208,768]{1,0:T(8,128)(2,1)S(1)} %bitcast.216), channel_id=1, source_target_pairs={{0,2},{1,3},{2,0},{3,1},{4,6},{5,7},{6,4},{7,5},{8,10},{9,11},{10,... | collective-permute-start | bytes 958472 | tf_op jit(solution)/shard_map/ppermute | solution.py:57
  18.7 26.8 %collective-permute-start = (bf16[208,768]{1,0:T(8,128)(2,1)S(1)}, bf16[208,768]{1,0:T(8,128)(2,1)S(1)}, u32[]{:S(2)}, u32[]{:S(2)}) collective-permute-start(bf16[208,768]{1,0:T(8,128)(2,1)S(1)} %bitcast.217), channel_id=1, source_target_pairs={{0,1},{1,0},{2,3},{3,2},{4,5},{5,4},{6,7},{7,6},{8,9},{9,8},{10,11... | collective-permute-start | bytes 958472 | tf_op jit(solution)/shard_map/ppermute | solution.py:57
  19.3 17.5 %collective-permute-start.5 = (s32[208]{0:T(256)S(1)}, s32[208]{0:T(256)S(1)}, u32[]{:S(2)}, u32[]{:S(2)}) collective-permute-start(s32[208]{0:T(256)S(1)} %bitcast.257), channel_id=1, source_target_pairs={{0,2},{1,3},{2,0},{3,1},{4,6},{5,7},{6,4},{7,5},{8,10},{9,11},{10,... | collective-permute-start | bytes 2504 | tf_op jit(solution)/shard_map/ppermute | solution.py:57
  19.7 18.5 %collective-permute-start.4 = (s32[208]{0:T(256)S(1)}, s32[208]{0:T(256)S(1)}, u32[]{:S(2)}, u32[]{:S(2)}) collective-permute-start(s32[208]{0:T(256)S(1)} %bitcast.258), channel_id=1, source_target_pairs={{0,1},{1,0},{2,3},{3,2},{4,5},{5,4},{6,7},{7,6},{8,9},{9,8},{10,11... | collective-permute-start | bytes 2504 | tf_op jit(solution)/shard_map/ppermute | solution.py:57
  20.4 19.2 %collective-permute-start.12 = (bf16[24,768]{1,0:T(8,128)(2,1)S(1)}, bf16[24,768]{1,0:T(8,128)(2,1)S(1)}, u32[]{:S(2)}, u32[]{:S(2)}) collective-permute-start(bf16[24,768]{1,0:T(8,128)(2,1)S(1)} %get-tuple-element.223), channel_id=1, source_target_pairs={{0,3},{1,2},{2,1},{3,0},{4,7},{5,6},{6,5},{7,4},{8,11},{9,10},{10,... | collective-permute-start | bytes 110600 | tf_op jit(solution)/shard_map/ppermute | solution.py:57
  51.4 27.2 %all-to-all-start.1 = ((bf16[8,48,768]{2,1,0:T(8,128)(2,1)}), bf16[8,48,768]{2,1,0:T(8,128)(2,1)}, u32[]{:S(2)}, u32[]{:S(2)}) async-start(bf16[8,48,768]{2,1,0:T(8,128)(2,1)} %broadcast_in_dim.29), calls=%async_computation.1 | async-start | bytes 1179648 | tf_op jit(solution)/shard_map/all_to_all | solution.py:98
  92.6 60.1 %all-to-all-start.2 = ((bf16[32,24,1344]{2,1,0:T(8,128)(2,1)}), bf16[32,24,1344]{2,1,0:T(8,128)(2,1)}, u32[]{:S(2)}, u32[]{:S(2)}) async-start(bf16[32,24,1344]{2,1,0:T(8,128)(2,1)} %pad_maximum_fusion), calls=%async_computation.2 | async-start | bytes 4325376 | tf_op jit(solution)/shard_map/all_to_all | solution.py:98
  102.7 21.3 %collective-permute-start.10 = (bf16[208,768]{1,0:T(8,128)(2,1)S(1)}, bf16[208,768]{1,0:T(8,128)(2,1)S(1)}, u32[]{:S(2)}, u32[]{:S(2)}) collective-permute-start(bf16[208,768]{1,0:T(8,128)(2,1)S(1)} %add_convert_fusion.3.refs_0_), channel_id=1, source_target_pairs={{0,2},{1,3},{2,0},{3,1},{4,6},{5,7},{6,4},{7,5},{8,10},{9,11},{10,... | collective-permute-start | bytes 958472 | tf_op jit(solution)/shard_map/ppermute | solution.py:57
  103.7 25.0 %collective-permute-start.9 = (bf16[208,768]{1,0:T(8,128)(2,1)S(1)}, bf16[208,768]{1,0:T(8,128)(2,1)S(1)}, u32[]{:S(2)}, u32[]{:S(2)}) collective-permute-start(bf16[208,768]{1,0:T(8,128)(2,1)S(1)} %add_convert_fusion.3.refs_0_), channel_id=1, source_target_pairs={{0,1},{1,0},{2,3},{3,2},{4,5},{5,4},{6,7},{7,6},{8,9},{9,8},{10,11... | collective-permute-start | bytes 958472 | tf_op jit(solution)/shard_map/ppermute | solution.py:57
  166.8 46.6 %all-to-all-start.3 = ((bf16[8,152,768]{2,1,0:T(8,128)(2,1)}), bf16[8,152,768]{2,1,0:T(8,128)(2,1)}, u32[]{:S(2)}, u32[]{:S(2)}) async-start(bf16[8,152,768]{2,1,0:T(8,128)(2,1)} %pad_maximum_fusion.1), calls=%async_computation.3 | async-start | bytes 3735552 | tf_op jit(solution)/shard_map/all_to_all | solution.py:98
  219.0 21.7 %all-to-all-start.4 = ((bf16[8,56,768]{2,1,0:T(8,128)(2,1)}), bf16[8,56,768]{2,1,0:T(8,128)(2,1)}, u32[]{:S(2)}, u32[]{:S(2)}) async-start(bf16[8,56,768]{2,1,0:T(8,128)(2,1)} %bitcast.227), calls=%async_computation.4 | async-start | bytes 1376256 | tf_op jit(solution)/shard_map/all_to_all | solution.py:98
  223.8 19.8 %collective-permute-start.26 = (bf16[448,768]{1,0:T(8,128)(2,1)}, bf16[448,768]{1,0:T(8,128)(2,1)}, u32[]{:S(2)}, u32[]{:S(2)}) collective-permute-start(bf16[448,768]{1,0:T(8,128)(2,1)} %bitcast.239), channel_id=1, source_target_pairs={{0,2},{1,3},{2,0},{3,1},{4,6},{5,7},{6,4},{7,5},{8,10},{9,11},{10,... | collective-permute-start | bytes 2064392 | tf_op jit(solution)/shard_map/ppermute | solution.py:57
  241.8 17.1 %collective-permute-start.25 = (bf16[448,768]{1,0:T(8,128)(2,1)}, bf16[448,768]{1,0:T(8,128)(2,1)}, u32[]{:S(2)}, u32[]{:S(2)}) collective-permute-start(bf16[448,768]{1,0:T(8,128)(2,1)} %bitcast.240), channel_id=1, source_target_pairs={{0,1},{1,0},{2,3},{3,2},{4,5},{5,4},{6,7},{7,6},{8,9},{9,8},{10,11... | collective-permute-start | bytes 2064392 | tf_op jit(solution)/shard_map/ppermute | solution.py:57
  288.0 16.7 %collective-permute-start.29 = (bf16[448,768]{1,0:T(8,128)(2,1)S(1)}, bf16[448,768]{1,0:T(8,128)(2,1)S(1)}, u32[]{:S(2)}, u32[]{:S(2)}) collective-permute-start(bf16[448,768]{1,0:T(8,128)(2,1)S(1)} %fusion.46), channel_id=1, source_target_pairs={{0,2},{1,3},{2,0},{3,1},{4,6},{5,7},{6,4},{7,5},{8,10},{9,11},{10,... | collective-permute-start | bytes 2064392 | tf_op jit(solution)/shard_map/ppermute | solution.py:57
  307.0 22.2 %all-to-all-start.5 = ((bf16[8,56,768]{2,1,0:T(8,128)(2,1)}), bf16[8,56,768]{2,1,0:T(8,128)(2,1)}, u32[]{:S(2)}, u32[]{:S(2)}) async-start(bf16[8,56,768]{2,1,0:T(8,128)(2,1)} %bitcast.228), calls=%async_computation.5 | async-start | bytes 1376256 | tf_op jit(solution)/shard_map/all_to_all | solution.py:98
  315.8 18.1 %collective-permute-start.31 = (bf16[448,768]{1,0:T(8,128)(2,1)}, bf16[448,768]{1,0:T(8,128)(2,1)}, u32[]{:S(2)}, u32[]{:S(2)}) collective-permute-start(bf16[448,768]{1,0:T(8,128)(2,1)} %fusion.47), channel_id=1, source_target_pairs={{0,2},{1,3},{2,0},{3,1},{4,6},{5,7},{6,4},{7,5},{8,10},{9,11},{10,... | collective-permute-start | bytes 2064392 | tf_op jit(solution)/shard_map/ppermute | solution.py:57
  329.2 41.5 %all-to-all-start.6 = ((bf16[32,24,768]{2,1,0:T(8,128)(2,1)}), bf16[32,24,768]{2,1,0:T(8,128)(2,1)}, u32[]{:S(2)}, u32[]{:S(2)}) async-start(bf16[32,24,768]{2,1,0:T(8,128)(2,1)} %bitcast.234), calls=%async_computation.6 | async-start | bytes 2359296 | tf_op jit(solution)/shard_map/all_to_all | solution.py:98
  380.4 47.9 %all-to-all-start.7 = ((bf16[8,152,768]{2,1,0:T(8,128)(2,1)}), bf16[8,152,768]{2,1,0:T(8,128)(2,1)}, u32[]{:S(2)}, u32[]{:S(2)}) async-start(bf16[8,152,768]{2,1,0:T(8,128)(2,1)} %pad_maximum_fusion.2), calls=%async_computation.7 | async-start | bytes 3735552 | tf_op jit(solution)/shard_map/all_to_all | solution.py:98
  385.7 142.9 %reduce-scatter.2.cloned.1.call-start = ((), (), s32[]{:S(2)}) async-start(), calls=%async_computation.12 | async-start | bytes 3981312 | tf_op jit(solution)/shard_map/reduce_scatter | solution.py:525
  415.6 20.4 %collective-permute-start.41 = (bf16[208,768]{1,0:T(8,128)(2,1)}, bf16[208,768]{1,0:T(8,128)(2,1)}, u32[]{:S(2)}, u32[]{:S(2)}) collective-permute-start(bf16[208,768]{1,0:T(8,128)(2,1)} %fusion.87), channel_id=1, source_target_pairs={{0,2},{1,3},{2,0},{3,1},{4,6},{5,7},{6,4},{7,5},{8,10},{9,11},{10,... | collective-permute-start | bytes 958472 | tf_op jit(solution)/shard_map/ppermute | solution.py:57
  452.9 22.5 %all-to-all-start.8 = ((bf16[8,24,768]{2,1,0:T(8,128)(2,1)}), bf16[8,24,768]{2,1,0:T(8,128)(2,1)S(1)}, u32[]{:S(2)}, u32[]{:S(2)}) async-start(bf16[8,24,768]{2,1,0:T(8,128)(2,1)} %bitcast.246), calls=%async_computation.8 | async-start | bytes 589824 | tf_op jit(solution)/shard_map/all_to_all | solution.py:98
  477.7 34.0 %all-to-all-start.9 = ((bf16[32,24,704]{2,1,0:T(8,128)(2,1)}), bf16[32,24,704]{2,1,0:T(8,128)(2,1)}, u32[]{:S(2)}, u32[]{:S(2)}) async-start(bf16[32,24,704]{2,1,0:T(8,128)(2,1)} %bitcast.69), calls=%async_computation.9 | async-start | bytes 2359296 | tf_op jit(solution)/shard_map/all_to_all | solution.py:98
  (145 other events, 1325.8 us)
Sparse Core Ops, SparseCore 0:
  45.6 60.3 all-gather.2
  436.1 92.3 reduce-scatter.1

commit v4 on v3

--- a/solution.py
+++ b/solution.py
@@ -68,9 +68,10 @@
     return jnp.concatenate(gather_blocks(block), axis=0)
 
 
-def scatter_blocks(send, keep):
+def scatter_blocks(send, keep, *others):
     got = swap(send, 1).astype(F32)
-    far = swap((keep[1] + got[1]).astype(BF), 2).astype(F32)
+    far = (keep[1] + got[1]).astype(BF)
+    far = swap(after(far, *others) if others else far, 2).astype(F32)
     return keep[0] + got[0] + far
 
 
@@ -121,12 +122,16 @@
     )
 
 
-def attend_kernel(*refs, count, heads):
-    a_refs, (w_ref, wo_ref, col_ref, row_ref) = refs[:count], refs[count : count + 4]
-    qkv_ref, out_ref, lse_ref, send_ref, keep_ref = refs[count + 4 :]
+def project_kernel(out_ref, wo_ref, send_ref, keep_ref):
+    put_partial(mm(out_ref[...], wo_ref[...]), send_ref, keep_ref)
+
+
+def attend_kernel(*refs, count, heads, lanes):
+    a_refs, (w_ref, col_ref, row_ref) = refs[:count], refs[count : count + 3]
+    qkv_ref, out_ref, lse_ref = refs[count + 3 :]
     tall = a_refs[0].shape[0]
     for k in range(count):
-        qkv_ref[k * tall : (k + 1) * tall] = mm(a_refs[k][...], w_ref[...]).astype(BF)
+        qkv_ref[k * tall : (k + 1) * tall] = mm(a_refs[k][...], w_ref[:, lanes]).astype(BF)
     part = heads * HD
     live = (col_ref[...] % 2).astype(F32)
     for h in range(heads):
@@ -140,10 +145,9 @@
         soft = (shifted * (1.0 / total)).astype(BF)
         out_ref[:, h * HD : (h + 1) * HD] = (dot(soft, v, 0, 0) * live).astype(BF)
         lse_ref[h : h + 1] = top + jnp.log(total)
-    put_partial(mm(out_ref[...], wo_ref[...]), send_ref, keep_ref)
-
-
-def attend_back_kernel(*refs, count, heads):
+
+
+def attend_back_kernel(*refs, count, heads, lanes):
     dy_refs, (w_ref, wo_ref, qkv_ref, lse_ref, col_ref, row_ref) = refs[:count], refs[count : count + 6]
     dqkv_ref, send_ref, keep_ref, do_ref = refs[count + 6 :]
     tall = dy_refs[0].shape[0]
@@ -167,17 +171,24 @@
         dqkv_ref[:, part + h * HD : part + (h + 1) * HD] = dk.astype(BF)
         dv = dot(soft.astype(BF), do, 1, 0)
         dqkv_ref[:, 2 * part + h * HD : 2 * part + (h + 1) * HD] = dv.astype(BF)
-    put_partial(dot(dqkv_ref[...], w_ref[...], 1, 1), send_ref, keep_ref)
+    put_partial(dot(dqkv_ref[...], w_ref[:, lanes], 1, 1), send_ref, keep_ref)
+
+
+def mlp_parts(w_ref):
+    groups, rows, width = w_ref.shape
+    half = rows // 2
+    return w_ref[:, :half].reshape(groups * half, width), w_ref[:, half:].reshape(groups * half, width)
 
 
 def mlp_kernel(*refs):
-    c_refs, (in_ref, out_ref, u_ref, g_ref, send_ref, keep_ref) = refs[:NF], refs[NF:]
+    c_refs, (w_ref, u_ref, g_ref, send_ref, keep_ref) = refs[:NF], refs[NF:]
+    w_in, w_out = mlp_parts(w_ref)
     for k in range(NF):
-        u = mm(c_refs[k][...], in_ref[...])
+        u = mm(c_refs[k][...], w_in)
         u_ref[k] = u
         g = gelu(u).astype(BF)
         g_ref[k] = g
-        partial = mm(g, out_ref[...])
+        partial = mm(g, w_out)
         if k % 2 == 0:
             keep_ref[k // 2] = partial
         else:
@@ -185,11 +196,12 @@
 
 
 def mlp_back_kernel(*refs):
-    dm_refs, (u_ref, in_ref, out_ref, du_ref, send_ref, keep_ref) = refs[:NF], refs[NF:]
+    dm_refs, (u_ref, w_ref, du_ref, send_ref, keep_ref) = refs[:NF], refs[NF:]
+    w_in, w_out = mlp_parts(w_ref)
     for k in range(NF):
-        du = (dot(dm_refs[k][...], out_ref[...], 1, 1) * gelu_slope(u_ref[k])).astype(BF)
+        du = (dot(dm_refs[k][...], w_out, 1, 1) * gelu_slope(u_ref[k])).astype(BF)
         du_ref[k] = du
-        partial = dot(du, in_ref[...], 1, 1)
+        partial = dot(du, w_in, 1, 1)
         if k % 2 == 0:
             keep_ref[k // 2] = partial
         else:
@@ -225,11 +237,12 @@
         out_specs=jax.tree.map(lambda _: space, outs),
         scratch_shapes=scratch,
         compiler_params=pltpu.CompilerParams(vmem_limit_bytes=48 * 2**20),
-        cost_estimate=pl.CostEstimate(flops=flops, bytes_accessed=2**21, transcendentals=0),
+        cost_estimate=pl.CostEstimate(flops=flops, bytes_accessed=2**16, transcendentals=0),
     )(*args)
 
 
 def attend(a_blocks, w_qkv, w_out, code_row):
+    w_qkv, lanes = w_qkv
     tokens, width = code_row.shape[0], w_qkv.shape[0]
     heads = HEADS // NF
     part = heads * HD
@@ -237,34 +250,38 @@
         jax.ShapeDtypeStruct((tokens, 3 * part), BF),
         jax.ShapeDtypeStruct((tokens, part), BF),
         jax.ShapeDtypeStruct((heads, tokens), F32),
-    ) + partial_shapes(tokens, width)
-    kernel = functools.partial(attend_kernel, count=len(a_blocks), heads=heads)
-    args = (*a_blocks, w_qkv, w_out, code_row[:, None], code_row[None])
-    return whole(kernel, outs, args, 8 * 10**9)
+    )
+    kernel = functools.partial(attend_kernel, count=len(a_blocks), heads=heads, lanes=lanes)
+    args = (*a_blocks, w_qkv, code_row[:, None], code_row[None])
+    qkv, out, lse = whole(kernel, outs, args, 4 * 10**8)
+    send, keep = whole(project_kernel, partial_shapes(tokens, width), (out, w_out), 10**8)
+    return qkv, out, lse, send, keep
 
 
 def attend_back(dy_blocks, w_qkv, w_out, qkv, lse, code_row):
+    w_qkv, lanes = w_qkv
     tokens, width = code_row.shape[0], w_qkv.shape[0]
     heads = HEADS // NF
     outs = (jax.ShapeDtypeStruct(qkv.shape, BF),) + partial_shapes(tokens, width)
-    kernel = functools.partial(attend_back_kernel, count=len(dy_blocks), heads=heads)
+    kernel = functools.partial(attend_back_kernel, count=len(dy_blocks), heads=heads, lanes=lanes)
     args = (*dy_blocks, w_qkv, w_out, qkv, lse, code_row[:, None], code_row[None])
     return whole(kernel, outs, args, 11 * 10**9, (pltpu.VMEM((tokens, heads * HD), BF),))
 
 
-def mlp(c_blocks, w_in, w_out):
+def mlp(c_blocks, weights):
     tall, width = c_blocks[0].shape
+    hidden = weights.shape[0] * weights.shape[1] // 2
     outs = (
-        jax.ShapeDtypeStruct((NF, tall, w_in.shape[1]), F32),
-        jax.ShapeDtypeStruct((NF, tall, w_in.shape[1]), BF),
+        jax.ShapeDtypeStruct((NF, tall, hidden), F32),
+        jax.ShapeDtypeStruct((NF, tall, hidden), BF),
     ) + partial_shapes(NF * tall, width)
-    return whole(mlp_kernel, outs, (*c_blocks, w_in, w_out), 5 * 10**9)
-
-
-def mlp_back(dm_blocks, u, w_in, w_out):
+    return whole(mlp_kernel, outs, (*c_blocks, weights), 3 * 10**8)
+
+
+def mlp_back(dm_blocks, u, weights):
     tall, width = dm_blocks[0].shape
     outs = (jax.ShapeDtypeStruct(u.shape, BF),) + partial_shapes(NF * tall, width)
-    return whole(mlp_back_kernel, outs, (*dm_blocks, u, w_in, w_out), 6 * 10**9)
+    return whole(mlp_back_kernel, outs, (*dm_blocks, u, weights), 6 * 10**9)
 
 
 def mlp_weights(c_blocks, dm_blocks, du, g, rest):
@@ -279,20 +296,13 @@
     return jnp.concatenate(parts + [rest], axis=2)
 
 
-def expert_kernel(*refs, blocks):
-    own_ref, x_refs, dz_refs = refs[0], refs[1 : 1 + blocks], refs[1 + blocks : 1 + 2 * blocks]
-    in_ref, out_ref, router_ref = refs[1 + 2 * blocks : 4 + 2 * blocks]
-    dx_send, dx_keep, y_send, y_keep, din_ref, dout_ref, drouter_ref = refs[4 + 2 * blocks :][:7]
-    din, dout = refs[-2:]
-    w_in, w_out, router = in_ref[...], out_ref[...], router_ref[...]
-    drouter = None
-    for i in range(blocks):
+def expert_kernel(*refs):
+    own_ref, x_refs, dz_refs, in_refs, out_refs = refs[0], refs[1:3], refs[3:5], refs[5:7], refs[7:9]
+    router_ref, dx_send, dx_keep, y_send, y_keep = refs[9:14]
+    din_own, din_far, dout_own, dout_far, drouter_ref, din_sum, dout_sum = refs[14:]
+    router = router_ref[...]
+    for i in range(2):
         x, dz = x_refs[i][...], dz_refs[i][...]
-        ue = mm(x, w_in)
-        cdf = 0.5 * (1.0 + lax.erf(ue * (0.5**0.5)))
-        slope = cdf + ue * jnp.exp(-0.5 * ue * ue) * 0.3989422804014327
-        ge = (ue * cdf).astype(BF)
-        y = mm(ge, w_out)
         logits = mm(x, router)
         lane = lax.broadcasted_iota(jnp.int32, logits.shape, 1)
         shifted = jnp.exp(logits - jnp.max(logits, axis=1, keepdims=True))
@@ -302,46 +312,55 @@
         gate = prob.astype(BF).astype(F32)
         dz_wide = dz.astype(F32)
         dyx = (gate * dz_wide).astype(BF)
-        due = (dot(dyx, w_out, 1, 1) * slope).astype(BF)
+        y = dx = None
+        for j in range(2):
+            w_in, w_out = in_refs[j][...], out_refs[j][...]
+            ue = mm(x, w_in)
+            cdf = 0.5 * (1.0 + lax.erf(ue * (0.5**0.5)))
+            slope = cdf + ue * jnp.exp(-0.5 * ue * ue) * 0.3989422804014327
+            ge = (ue * cdf).astype(BF)
+            due = (dot(dyx, w_out, 1, 1) * slope).astype(BF)
+            term = mm(ge, w_out)
+            y = term if j == 0 else y + term
+            term = dot(due, w_in, 1, 1)
+            dx = term if j == 0 else dx + term
+            din, dout = dot(x, due, 0, 0), dot(ge, dyx, 0, 0)
+            din_ref, dout_ref = (din_own, dout_own) if j == 0 else (din_sum, dout_sum)
+            if i == 0:
+                din_ref[...], dout_ref[...] = din, dout
+            else:
+                din_ref[...] += din
+                dout_ref[...] += dout
         dgate = jnp.sum(dz_wide * y, axis=1, keepdims=True)
         dlogits = (dgate * prob * (mine - probs)).astype(BF)
-        dx = dot(due, w_in, 1, 1) + dot(dlogits, router, 1, 1)
+        dx = dx + dot(dlogits, router, 1, 1)
         y = gate * y
-        if i % 2 == 0:
-            dx_keep[i // 2], y_keep[i // 2] = dx, y
+        if i == 0:
+            dx_keep[...], y_keep[...], drouter_ref[...] = dx, y, dot(x, dlogits, 0, 0)
         else:
-            dx_send[i // 2], y_send[i // 2] = dx.astype(BF), y.astype(BF)
-        if i == 0:
-            din[...], dout[...], drouter = dot(x, due, 0, 0), dot(ge, dyx, 0, 0), dot(x, dlogits, 0, 0)
-        else:
-            din[...] += dot(x, due, 0, 0)
-            dout[...] += dot(ge, dyx, 0, 0)
-            drouter += dot(x, dlogits, 0, 0)
-    din_ref[...], dout_ref[...], drouter_ref[...] = din[...].astype(BF), dout[...].astype(BF), drouter
+            dx_send[...], y_send[...] = dx.astype(BF), y.astype(BF)
+            drouter_ref[...] += dot(x, dlogits, 0, 0)
+    din_far[...], dout_far[...] = din_sum[...].astype(BF), dout_sum[...].astype(BF)
 
 
 def expert_compute(own, x_blocks, dz_blocks, w_in, w_out, router):
     tall, width = x_blocks[0].shape
-    hidden = w_in.shape[1]
-    count = len(x_blocks)
-    send = jax.ShapeDtypeStruct((count // 2, tall, width), BF)
-    keep = jax.ShapeDtypeStruct((count // 2, tall, width), F32)
-    outs = (
-        send, keep, send, keep, jax.ShapeDtypeStruct(w_in.shape, BF), jax.ShapeDtypeStruct(w_out.shape, BF),
-        jax.ShapeDtypeStruct(router.shape, F32),
-    )
+    square = w_in[0].shape
+    send, keep = jax.ShapeDtypeStruct((tall, width), BF), jax.ShapeDtypeStruct((tall, width), F32)
+    near, far = jax.ShapeDtypeStruct(square, F32), jax.ShapeDtypeStruct(square, BF)
+    outs = (send, keep, send, keep, near, far, near, far, jax.ShapeDtypeStruct(router.shape, F32))
     space = pl.BlockSpec(memory_space=pltpu.VMEM)
     return pl.pallas_call(
-        functools.partial(expert_kernel, blocks=count),
+        expert_kernel,
         out_shape=outs,
-        in_specs=[pl.BlockSpec(memory_space=pltpu.SMEM)] + [space] * (2 * count + 3),
+        in_specs=[pl.BlockSpec(memory_space=pltpu.SMEM)] + [space] * 9,
         out_specs=(space,) * len(outs),
-        scratch_shapes=[pltpu.VMEM(w_in.shape, F32), pltpu.VMEM(w_out.shape, F32)],
+        scratch_shapes=[pltpu.VMEM(square, F32), pltpu.VMEM(square, F32)],
         compiler_params=pltpu.CompilerParams(vmem_limit_bytes=56 * 2**20),
         cost_estimate=pl.CostEstimate(
-            flops=16 * count * tall * width * hidden, bytes_accessed=2**24, transcendentals=0
+            flops=64 * tall * width * square[1], bytes_accessed=2**24, transcendentals=0
         ),
-    )(own.astype(jnp.int32)[None], *x_blocks, *dz_blocks, w_in, w_out, router)
+    )(own.astype(jnp.int32)[None], *x_blocks, *dz_blocks, *w_in, *w_out, router)
 
 
 def make_shards(n_dp):
@@ -385,7 +404,7 @@
             return exchange(full.reshape((n_all, rows, -1)), ALL).reshape(width, -1)
 
         first = to_everyone(jnp.concatenate([small, qkv_block(0)], axis=2))
-        small_all, w_qkv0 = first[:, :128], first[:, 128:]
+        small_all, w_qkv0 = first[:, :128], (first, slice(128, 128 + 3 * part))
         norms = small_all[:, :8].T.astype(F32)
         gains, biases = norms[:4], norms[4:]
         w_router = small_all[:, 8 : 8 + experts]
@@ -393,29 +412,13 @@
         mlp_block = jnp.transpose(mlp_in.reshape(rows, n_dp, NF, hid), (2, 0, 1, 3))
         mlp_block = deal(mlp_block.reshape(NF, rows, n_dp * hid)).reshape(NF * rows, width)
         mlp_all = lax.all_gather(jnp.concatenate([mlp_block, mlp_out], axis=0), "dp")
-        w_mlp_in = mlp_all[:, : NF * rows].reshape(width, n_dp * hid)
-        w_mlp_out = mlp_all[:, NF * rows :].reshape(n_dp * hid, width)
 
         to_heads = [(j, j % n_dp * NF + j // n_dp) for j in range(n_all)]
         to_owner = [(b, a) for a, b in to_heads]
-        held = lax.ppermute(jnp.concatenate([attn_out[0], attn_out[1]], axis=0), ALL, to_heads)
-        held = exchange(jnp.broadcast_to(after(held, first)[None], (n_dp,) + held.shape), "dp")
-        w_out0, w_out1 = held[:, :rows].reshape(part, width), held[:, rows:].reshape(part, width)
-
-        in_block = jnp.transpose(exp_in.reshape(experts, rows, n_dp, NF, hid), (0, 3, 1, 2, 4))
-        in_block = in_block.reshape(experts * NF, rows, n_dp * hid)
-        if clones == 1:
-            held = jnp.broadcast_to(qkv_block(1)[None], (n_dp, NF, rows, 3 * part)).reshape(n_all, rows, -1)
-            in_block = jnp.concatenate([in_block, held], axis=2)
-            w_qkv0 = after(w_qkv0, in_block)
-            held = exchange(after(in_block, w_out0), ALL).reshape(width, -1)
-            w_exp_in, w_qkv1 = held[:, : n_dp * hid], held[:, n_dp * hid :]
-        else:
-            held = in_block.reshape(experts, NF, rows, n_dp * hid)
-            held = exchange(jnp.swapaxes(held, 0, 1), "fsdp")
-            held = exchange(jnp.swapaxes(held, 0, 1), "dp", groups)
-            w_exp_in = lax.all_gather(held, "dp", axis_index_groups=ring).reshape(width, n_dp * hid)
-            w_qkv1 = to_everyone(qkv_block(1))
+        held_out = lax.ppermute(attn_out, ALL, to_heads)
+        held = after(held_out[0], first)
+        w_out0 = exchange(jnp.broadcast_to(held[None], (n_dp, rows, width)), "dp").reshape(part, width)
+
         choice = expert_ids.reshape(tokens, 2)
         rank = ranks.reshape(tokens, 2)
         place = jnp.where(rank < capacity, choice * slots + rank, -1)
@@ -428,6 +431,32 @@
             return exchange(held, "dp", groups).reshape(experts * slots, width)
 
         top_grad = cotangent.reshape(tokens, width)
+        in_block = jnp.transpose(exp_in.reshape(experts, rows, n_dp, NF, hid), (3, 0, 1, 2, 4))
+        in_block = in_block.reshape(NF, experts, rows, n_dp * hid)
+        if clones == 1:
+            in_block = jnp.swapaxes(deal(in_block), 0, 1).reshape(experts, NF * rows, n_dp * hid)
+            held = deal(qkv_block(1)).reshape(NF * rows, 3 * part)
+            held = jnp.concatenate([held, held_out[1].reshape(NF * rows, part)], axis=1)
+            held = jnp.broadcast_to(held[None], (n_dp,) + held.shape)
+            in_block = jnp.concatenate([in_block, held], axis=2)
+
+        h0 = patches.reshape(tokens, width).astype(F32)
+        xhat0_all, _ = scale_rows(rows_all.astype(F32))
+        a0 = (xhat0_all * gains[0] + biases[0]).astype(BF)
+        qkv0, o0, lse0, send, keep = attend([a0], w_qkv0, w_out0, code_all)
+        h1 = h0 + scatter_blocks(after(send, in_block) if clones == 1 else send, keep)
+
+        if clones == 1:
+            held = exchange(after(in_block, w_out0), "dp").reshape(width, -1)
+            cut = n_dp * hid
+            w_exp_in, w_qkv1 = held[:, :cut], (held, slice(cut, cut + 3 * part))
+            w_out1 = held[:, cut + 3 * part :].reshape(part, width)
+        else:
+            held = exchange(in_block, "fsdp")
+            held = exchange(jnp.swapaxes(held, 0, 1), "dp", groups)
+            w_exp_in = lax.all_gather(held, "dp", axis_index_groups=ring).reshape(width, n_dp * hid)
+            w_qkv1 = (to_everyone(qkv_block(1)), slice(0, 3 * part))
+            w_out1 = lax.all_gather(held_out[1], "dp").reshape(part, width)
         if clones == 1:
             dz = mm(pick, top_grad).astype(BF).reshape(experts, slots, width)
             held = exchange(after(jnp.concatenate([dz, exp_out], axis=1), w_exp_in), "dp")
@@ -438,43 +467,38 @@
             w_exp_out = lax.all_gather(w_exp_out, "dp", axis_index_groups=ring)
         w_exp_out = w_exp_out.reshape(n_dp * hid, width)
 
-        h0 = patches.reshape(tokens, width).astype(F32)
-        xhat0_all, _ = scale_rows(rows_all.astype(F32))
-        a0 = (xhat0_all * gains[0] + biases[0]).astype(BF)
-        qkv0, o0, lse0, send, keep = attend([a0], w_qkv0, w_out0, code_all)
-        h1 = h0 + scatter_blocks(send, keep)
-
         xhat1, inv1 = scale_rows(h1)
         c0 = gather_blocks((xhat1 * gains[1] + biases[1]).astype(BF))
-        u0, g0, send, keep = mlp(c0, w_mlp_in, w_mlp_out)
+        u0, g0, send, keep = mlp(c0, mlp_all)
         h2 = h1 + scatter_blocks(send, keep)
 
+        w_in_far = swap(w_exp_in, 2)
         xhat2, inv2 = scale_rows(h2)
         a1 = gather_blocks(after((xhat2 * gains[2] + biases[2]).astype(BF), w_exp_in))
         qkv1, o1, lse1, send, keep = attend(a1, w_qkv1, w_out1, code_all)
-        h3 = h2 + scatter_blocks(send, keep)
+        h3 = h2 + scatter_blocks(send, keep, w_in_far)
 
         xhat3, inv3 = scale_rows(h3)
         c1 = after((xhat3 * gains[3] + biases[3]).astype(BF), dz, w_exp_out)
-        dz = gather_blocks(after(dz, c1))
-        x = to_experts(c1)
-        x = gather_blocks(x)
-        dx_send, dx_keep, y_send, y_keep, exp_in_part, exp_out_part, router_part = expert_compute(
-            own_dp % experts, x, dz, w_exp_in, w_exp_out, w_router
+        w_out_far = swap(w_exp_out, 2)
+        dz = (dz, swap(dz, 1))
+        x = after(to_experts(c1), w_out_far)
+        x = (x, swap(x, 1))
+        dx_send, dx_keep, y_send, y_keep, din_own, din_far, dout_own, dout_far, router_part = expert_compute(
+            own_dp % experts, x, dz, (w_exp_in, w_in_far), (w_exp_out, w_out_far), w_router
         )
-        dx = scatter_blocks(dx_send, dx_keep).astype(BF)
-        y = scatter_blocks(after(y_send, dx), y_keep).astype(BF)
-        y_summed = y
+        dx = (dx_keep + swap(dx_send, 1).astype(F32)).astype(BF)
+        y = (y_keep + swap(after(y_send, dx), 1).astype(F32)).astype(BF)
+        exp_in_part = (din_own + swap(after(din_far, dx), 2).astype(F32)).astype(BF)
+        exp_out_part = (dout_own + swap(after(dout_far, exp_in_part), 2).astype(F32)).astype(BF)
         dx = exchange(dx.reshape(experts, slots, width), "dp", groups)
 
         if clones == 1:
             back = exp_out_part.reshape(experts, hid, width)
             back = jnp.concatenate([y.reshape(experts, slots, width), back], axis=1)
-            in_got = exchange(after(exp_in_part.reshape(n_all, rows, n_dp * hid), dx), ALL)
+            in_got = exchange(after(exp_in_part.reshape(n_dp, NF * rows, n_dp * hid), dx), "dp")
             got = exchange(after(back, in_got), "dp")
             y, exp_out_grads = got[:, :slots], got[:, slots:].astype(F32)
-            in_got = in_got.reshape(experts, NF, rows, n_dp, hid)
-            exp_in_grads = jnp.transpose(in_got, (0, 2, 3, 1, 4))
         else:
             back = lax.psum_scatter(
                 exp_out_part.reshape(clones, experts, hid, width), "dp", axis_index_groups=ring
@@ -485,12 +509,8 @@
             held = lax.psum_scatter(
                 exp_in_part.reshape(clones, experts, NF, rows, n_dp * hid), "dp", axis_index_groups=ring
             )
-            held = exchange(held, "dp", groups)
-            held = exchange(jnp.swapaxes(held, 0, 1), "fsdp")
-            in_got = held.reshape(NF, experts, rows, n_dp, hid)
-            exp_in_grads = jnp.transpose(in_got, (1, 2, 3, 0, 4))
-        exp_in_grads = exp_in_grads.reshape(experts, rows, n_dp * NF * hid).astype(F32)
-        dc1 = mm_tn(pick, after(dx, exp_in_part, y_summed).reshape(experts * slots, width))
+            in_got = exchange(held, "dp", groups)
+        dc1 = mm_tn(pick, after(dx, exp_in_part).reshape(experts * slots, width))
 
         def rows_to_owners(grad):
             cols = grad.shape[1]
@@ -519,7 +539,7 @@
         grad = grad + norm_back(da1, xhat2, inv2, gains[2])
 
         dm = gather_blocks(grad.astype(BF))
-        du0, send, keep = mlp_back(dm, after(u0, attn_part), w_mlp_in, w_mlp_out)
+        du0, send, keep = mlp_back(dm, after(u0, attn_part), mlp_all)
         dc0 = scatter_blocks(send, keep)
         dense_part = mlp_weights(c0, dm, du0, after(g0, got), attn_part)
         dense_sum = lax.psum_scatter(dense_part, "dp")
@@ -549,6 +569,10 @@
         small_grads = jnp.sum(total[:, :, :128], axis=0)
         qkv_grad0 = qkv_layout(total[:, :, 128:])
         dense_sum = after(dense_sum, tail)
+        in_got = jnp.swapaxes(after(in_got, dqkv0).reshape(experts, NF, rows, n_dp * hid), 0, 1)
+        in_got = deal(in_got).reshape(NF, experts, rows, n_dp, hid)
+        exp_in_grads = jnp.transpose(in_got, (1, 2, 3, 0, 4))
+        exp_in_grads = exp_in_grads.reshape(experts, rows, n_dp * NF * hid).astype(F32)
         held = jnp.concatenate([dense_sum[:, :width], dense_sum[:, 2 * width : 2 * width + 3 * part]], axis=1)
         held = exchange(held.reshape(NF, rows, -1), "fsdp").astype(F32)
         mlp_in_grads = held[..., :width].reshape(NF, rows, n_dp, hid)

time: 565 us -> 547 us (0.968)
  waiting for transfers between devices: 223 us -> 174 us
  starting transfers between devices: 108 us -> 123 us
  other arithmetic: 47.8 us -> 61.3 us
  local copies, waits for them, and re-layouts: 70.6 us -> 77.3 us
    all_to_all x11, waiting for transfers between devices: 79.5 us -> 53.8 us  [exchange(): lax.all_to_all(value, axes, 0, 0, axis_index_groups=groups, tiled=True)]
    reduce_scatter x1, waiting for transfers between devices: 15.2 us -> 0.02 us  [shards(): dense_sum = lax.psum_scatter(dense_part, 'dp')]
    ppermute x46 -> x53, starting transfers between devices: 46.9 us -> 55.1 us  [swap(): return lax.ppermute(value, 'fsdp', [(i, i ^ bits) for i in range(NF)])]
    slice x5 -> x3, local copies, waits for them, and re-layouts: 8.73 us -> 2.13 us  [the longest x1 1.19 us: shards(): w_exp_in, w_qkv1 = (held[:, :cut], (held, slice(cut, cut + 3 * part)))]
    all_to_all x11, starting transfers between devices: 53.8 us -> 59.5 us  [exchange(): lax.all_to_all(value, axes, 0, 0, axis_index_groups=groups, tiled=True)]
    ppermute x46 -> x53, waiting for transfers between devices: 123 us -> 120 us  [swap(): return lax.ppermute(value, 'fsdp', [(i, i ^ bits) for i in range(NF)])]
    unnamed x221 -> x227, local copies, waits for them, and re-layouts: 21.2 us -> 24 us
    pallas_call x7 -> x9, Pallas kernels: 54.6 us -> 52.8 us  [whole(): pl.pallas_call(kernel, out_shape=outs, in_specs=[space] * len(args), out_...]
  transfers between devices with their start and end apart: 61 -> 68, of which waited for: 34 -> 30; matrix products, arithmetic and copies ran while one was open for 16% -> 21% of each run, Pallas kernels for 10% -> 10%
where the time goes in v4:
time: 547 us; the launch traced here: 537 us
  waiting for transfers between devices  174 us (32%)
  starting transfers between devices  123 us (22%)
  local copies, waits for them, and re-layouts  77.3 us (14%)
  Pallas kernels  73.1 us (13%)
  other arithmetic  61.3 us (11%)
  between operations  16 us (3%)
  matrix products  12.6 us (2%)
    ppermute x53, waiting for transfers between devices, swap(): return lax.ppermute(value, 'fsdp', [(i, i ^ bits) for i in range(NF)])  120 us
    all_to_all x11, starting transfers between devices, exchange(): lax.all_to_all(value, axes, 0, 0, axis_index_groups=groups, tiled=True)  59.5 us
    ppermute x53, starting transfers between devices, swap(): return lax.ppermute(value, 'fsdp', [(i, i ^ bits) for i in range(NF)])  55.1 us
    all_to_all x11, waiting for transfers between devices, exchange(): lax.all_to_all(value, axes, 0, 0, axis_index_groups=groups, tiled=True)  53.8 us
    pallas_call x9, Pallas kernels, whole(): pl.pallas_call(kernel, out_shape=outs, in_specs=[space] * len(args), out_...  52.8 us
    unnamed x227, local copies, waits for them, and re-layouts  24 us
    pallas_call x1, Pallas kernels, expert_compute(): pl.pallas_call(expert_kernel, out_shape=outs, in_specs=[pl.BlockSpec(memo...  20.3 us
    dot_general x6, matrix products, mm_tn(): lax.dot_general(left, right, (((0,), (0,)), ((), ())), preferred_element_...  11 us
  transfers between devices with their start and end apart: 68, of which 30 were waited for; matrix products, arithmetic and copies ran while one was open for 21% of the time, Pallas kernels for 10%

profile of v4, /device:TPU:5, one launch (start us, length us, event | category | flops | bytes accessed | tf_op | source)
XLA Modules:
  0.0 537.5 jit_solution(3212928893615882368)
XLA Ops:
  39.2 5.7 %collective-permute-start.6 = (bf16[2,24,768]{2,1,0:T(8,128)(2,1)}, bf16[2,24,768]{2,1,0:T(8,128)(2,1)S(1)}, u32[]{:S(2)}, u32[]{:S(2)}) collective-permute-start(bf16[2,24,768]{2,1,0:T(8,128)(2,1)} %param.23), channel_id=1, source_target_pairs={{0,0},{1,4},{2,8},{3,12},{4,16},{5,20},{6,24},{7,28},{8,1},{9,5},{... | collective-permute-start | bytes 221192 | tf_op jit(solution)/shard_map/ppermute | solution.py:418
  48.8 5.8 %collective-permute-done.8 = bf16[8,24,768]{2,1,0:T(8,128)(2,1)S(1)} collective-permute-done((bf16[8,24,768]{2,1,0:T(8,128)(2,1)}, bf16[8,24,768]{2,1,0:T(8,128)(2,1)S(1)}, u32[]{:S(2)}, u32[]{:S(2)}) %collective-permute-start.8) | collective-permute-done | bytes 294944 | tf_op jit(solution)/shard_map/ppermute | solution.py:57
  60.7 8.2 %all-to-all-start.1 = ((bf16[8,24,768]{2,1,0:T(8,128)(2,1)}), bf16[8,24,768]{2,1,0:T(8,128)(2,1)S(1)}, u32[]{:S(2)}, u32[]{:S(2)}) async-start(bf16[8,24,768]{2,1,0:T(8,128)(2,1)} %broadcast_in_dim.27), calls=%async_computation.1 | async-start | bytes 589824 | tf_op jit(solution)/shard_map/all_to_all | solution.py:99
  74.5 6.1 %shard_map.238 = (bf16[832,576]{1,0:T(8,128)(2,1)S(1)}, bf16[832,192]{1,0:T(8,128)(2,1)S(1)}, f32[3,832]{1,0:T(4,128)S(1)}) custom-call(bf16[832,768]{1,0:T(8,128)(2,1)S(1)} %get-tuple-element.191.refs_0_, bf16[768,704]{1,0:T(8,128)(2,1)S(1)} %bitcast.279, s32[832,1]{1,0:T(8,128)S(1)} %broadcast_in_dim.32.refs_2_.refs_5_.refs_8_, ...), custom_call_target="tpu_custom_call" | custom-call | flops 400000000 | bytes 65536 | tf_op jit(solution)/shard_map/pallas_call | solution.py:233
  90.5 5.7 %all-to-all-start.2 = ((bf16[8,96,1536]{2,1,0:T(8,128)(2,1)}), bf16[8,96,1536]{2,1,0:T(8,128)(2,1)S(1)}, u32[]{:S(2)}, u32[]{:S(2)}) async-start(bf16[8,96,1536]{2,1,0:T(8,128)(2,1)} %pad_maximum_fusion), calls=%async_computation.2 | async-start | bytes 4718592 | tf_op jit(solution)/shard_map/all_to_all | solution.py:99
  125.1 5.9 %collective-permute-done.22 = bf16[208,768]{1,0:T(8,128)(2,1)S(1)} collective-permute-done((bf16[208,768]{1,0:T(8,128)(2,1)S(1)}, bf16[208,768]{1,0:T(8,128)(2,1)S(1)}, u32[]{:S(2)}, u32[]{:S(2)}) %collective-permute-start.22) | collective-permute-done | bytes 319520 | tf_op jit(solution)/shard_map/ppermute | solution.py:57
  132.5 16.7 %all-to-all-done.2 = bf16[8,96,1536]{2,1,0:T(8,128)(2,1)S(1)} async-done(((bf16[8,96,1536]{2,1,0:T(8,128)(2,1)}), bf16[8,96,1536]{2,1,0:T(8,128)(2,1)S(1)}, u32[]{:S(2)}, u32[]{:S(2)}) %all-to-all-start.2) | async-done | bytes 2359328 | tf_op jit(solution)/shard_map/all_to_all | solution.py:99
  171.7 7.4 %shard_map.241 = (bf16[832,576]{1,0:T(8,128)(2,1)S(1)}, bf16[832,192]{1,0:T(8,128)(2,1)S(1)}, f32[3,832]{1,0:T(4,128)S(1)}) custom-call(bf16[208,768]{1,0:T(8,128)(2,1)} %add_convert_fusion.6.refs_0_, bf16[208,768]{1,0:T(8,128)(2,1)} %collective-permute-done.23.refs_1_, bf16[208,768]{1,0:T(8,128)(2,1)} %collective-permute-done.24.refs_2_, ...), custom_call_target="tpu_custom_call" | custom-call | flops 400000000 | bytes 65536 | tf_op jit(solution)/shard_map/pallas_call | solution.py:233
  183.6 11.6 %collective-permute-done.27.refs_6_ = bf16[768,768]{1,0:T(8,128)(2,1)} collective-permute-done((bf16[768,768]{1,0:T(8,128)(2,1)}, bf16[768,768]{1,0:T(8,128)(2,1)}, u32[]{:S(2)}, u32[]{:S(2)}) %collective-permute-start.27) | collective-permute-done | bytes 1179680 | tf_op jit(solution)/shard_map/ppermute | solution.py:57
  195.6 7.8 %collective-permute-done.28 = bf16[208,768]{1,0:T(8,128)(2,1)S(1)} collective-permute-done((bf16[208,768]{1,0:T(8,128)(2,1)S(1)}, bf16[208,768]{1,0:T(8,128)(2,1)S(1)}, u32[]{:S(2)}, u32[]{:S(2)}) %collective-permute-start.28) | collective-permute-done | bytes 319520 | tf_op jit(solution)/shard_map/ppermute | solution.py:57
  208.9 5.6 %all-to-all-start.4 = ((bf16[8,56,768]{2,1,0:T(8,128)(2,1)}), bf16[8,56,768]{2,1,0:T(8,128)(2,1)S(1)}, u32[]{:S(2)}, u32[]{:S(2)}) async-start(bf16[8,56,768]{2,1,0:T(8,128)(2,1)} %bitcast.60), calls=%async_computation.4 | async-start | bytes 1376256 | tf_op jit(solution)/shard_map/all_to_all | solution.py:99
  217.5 22.6 %collective-permute-done.29.refs_8_ = bf16[768,768]{1,0:T(8,128)(2,1)} collective-permute-done((bf16[768,768]{1,0:T(8,128)(2,1)}, bf16[768,768]{1,0:T(8,128)(2,1)}, u32[]{:S(2)}, u32[]{:S(2)}) %collective-permute-start.29) | collective-permute-done | bytes 1179680 | tf_op jit(solution)/shard_map/ppermute | solution.py:57
  245.2 20.3 %shard_map.243 = (bf16[448,768]{1,0:T(8,128)(2,1)}, f32[448,768]{1,0:T(8,128)}, bf16[448,768]{1,0:T(8,128)(2,1)}, f32[448,768]{1,0:T(8,128)}, f32[768,768]{1,0:T...) custom-call(s32[1]{0:T(128)} %bitcast.55.refs_0_, ...), custom_call_target="tpu_custom_call" | custom-call | flops 16911433728 | bytes 16777216 | tf_op jit(solution)/shard_map/pallas_call | solution.py:353
  276.1 21.6 %collective-permute-done.34 = bf16[768,768]{1,0:T(8,128)(2,1)} collective-permute-done((bf16[768,768]{1,0:T(8,128)(2,1)}, bf16[768,768]{1,0:T(8,128)(2,1)}, u32[]{:S(2)}, u32[]{:S(2)}) %collective-permute-start.34) | collective-permute-done | bytes 1179680 | tf_op jit(solution)/shard_map/ppermute | solution.py:57
  301.0 5.9 %all-to-all-start.6 = ((bf16[8,96,768]{2,1,0:T(8,128)(2,1)}), bf16[8,96,768]{2,1,0:T(8,128)(2,1)}, u32[]{:S(2)}, u32[]{:S(2)}) async-start(bf16[8,96,768]{2,1,0:T(8,128)(2,1)} %bitcast.290), calls=%async_computation.6 | async-start | bytes 2359296 | tf_op jit(solution)/shard_map/all_to_all | solution.py:99
  320.8 10.7 %shard_map.244 = (bf16[832,576]{1,0:T(8,128)(2,1)S(1)}, bf16[2,208,768]{2,1,0:T(8,128)(2,1)S(1)}, f32[2,208,768]{2,1,0:T(8,128)S(1)}) custom-call(bf16[208,768]{1,0:T(8,128)(2,1)S(1)} %get-tuple-element.183.refs_0_, bf16[208,768]{1,0:T(8,128)(2,1)S(1)} %collective-permute-done.36.refs_1_, bf16[208,768]{1,0:T(8,128)(2,1)S(1)} %collective-permute-done.37.refs_2_, ...), custom_call_target="tpu_custom_call" | custom-call | flops 11000000512 | bytes 65536 | tf_op jit(solution)/shard_map/pallas_call | solution.py:233
  340.5 6.0 %collective-permute-done.35 = bf16[768,768]{1,0:T(8,128)(2,1)} collective-permute-done((bf16[768,768]{1,0:T(8,128)(2,1)}, bf16[768,768]{1,0:T(8,128)(2,1)}, u32[]{:S(2)}, u32[]{:S(2)}) %collective-permute-start.35) | collective-permute-done | bytes 1179680 | tf_op jit(solution)/shard_map/ppermute | solution.py:57
  349.5 5.6 %all-to-all-start.7 = ((bf16[8,152,768]{2,1,0:T(8,128)(2,1)}), bf16[8,152,768]{2,1,0:T(8,128)(2,1)}, u32[]{:S(2)}, u32[]{:S(2)}) async-start(bf16[8,152,768]{2,1,0:T(8,128)(2,1)} %pad_maximum_fusion.2), calls=%async_computation.7 | async-start | bytes 3735552 | tf_op jit(solution)/shard_map/all_to_all | solution.py:99
  374.8 5.6 %shard_map.245 = (bf16[4,208,768]{2,1,0:T(8,128)(2,1)S(1)}, bf16[2,208,768]{2,1,0:T(8,128)(2,1)S(1)}, f32[2,208,768]{2,1,0:T(8,128)S(1)}) custom-call(bf16[208,768]{1,0:T(8,128)(2,1)S(1)} %get-tuple-element.180.refs_0_.refs_4_, bf16[208,768]{1,0:T(8,128)(2,1)} %collective-permute-done.41.refs_1_.refs_5_, ...), custom_call_target="tpu_custom_call" | custom-call | flops 6000000000 | bytes 65536 | tf_op jit(solution)/shard_map/pallas_call | solution.py:233
  385.0 12.6 %all-to-all-done.7 = bf16[8,152,768]{2,1,0:T(8,128)(2,1)} async-done(((bf16[8,152,768]{2,1,0:T(8,128)(2,1)}), bf16[8,152,768]{2,1,0:T(8,128)(2,1)}, u32[]{:S(2)}, u32[]{:S(2)}) %all-to-all-start.7) | async-done | bytes 1867808 | tf_op jit(solution)/shard_map/all_to_all | solution.py:99
  401.2 6.3 %shard_map.246 = bf16[8,96,2304]{2,1,0:T(8,128)(2,1)} custom-call(bf16[208,768]{1,0:T(8,128)(2,1)S(1)} %copy-done.9, bf16[208,768]{1,0:T(8,128)(2,1)S(1)} %copy-done.21, bf16[208,768]{1,0:T(8,128)(2,1)} %collective-permute-done.16.refs_2_, bf16[208,768]{1,0:T(8,128)(2,1)} %collective-permute-done.17.refs_3_, bf16[208,768]{1,0:T(8,128)(2,1)S(1)} %copy-done.23, ...), custom_call_target="tpu_custom_call" | custom-call | flops 5000000000 | bytes 65536 | tf_op jit(solution)/shard_map/pallas_call | solution.py:233
  414.2 5.5 %collective-permute-done.47.refs_2_ = bf16[208,768]{1,0:T(8,128)(2,1)S(1)} collective-permute-done((bf16[208,768]{1,0:T(8,128)(2,1)S(1)}, bf16[208,768]{1,0:T(8,128)(2,1)S(1)}, u32[]{:S(2)}, u32[]{:S(2)}) %collective-permute-start.47) | collective-permute-done | bytes 319520 | tf_op jit(solution)/shard_map/ppermute | solution.py:57
  428.6 10.3 %shard_map.247 = (bf16[832,576]{1,0:T(8,128)(2,1)S(1)}, bf16[2,208,768]{2,1,0:T(8,128)(2,1)S(1)}, f32[2,208,768]{2,1,0:T(8,128)}) custom-call(bf16[208,768]{1,0:T(8,128)(2,1)S(1)} %get-tuple-element.109.refs_0_, bf16[208,768]{1,0:T(8,128)(2,1)S(1)} %collective-permute-done.46.refs_1_, bf16[208,768]{1,0:T(8,128)(2,1)S(1)} %collective-permute-done.47.refs_2_, ...), custom_call_target="tpu_custom_call" | custom-call | flops 11000000512 | bytes 65536 | tf_op jit(solution)/shard_map/pallas_call | solution.py:233
  485.9 22.8 %all-to-all-done.9 = bf16[32,24,704]{2,1,0:T(8,128)(2,1)} async-done(((bf16[32,24,704]{2,1,0:T(8,128)(2,1)}), bf16[32,24,704]{2,1,0:T(8,128)(2,1)}, u32[]{:S(2)}, u32[]{:S(2)}) %all-to-all-start.9) | async-done | bytes 1081376 | tf_op jit(solution)/shard_map/all_to_all | solution.py:99
  (520 shorter events, 279.2 us)
Async XLA Ops:
  7.2 49.3 %collective-permute-start.1 = (bf16[208,768]{1,0:T(8,128)(2,1)}, bf16[208,768]{1,0:T(8,128)(2,1)S(1)}, u32[]{:S(2)}, u32[]{:S(2)}) collective-permute-start(bf16[208,768]{1,0:T(8,128)(2,1)} %bitcast.283), channel_id=1, source_target_pairs={{0,2},{1,3},{2,0},{3,1},{4,6},{5,7},{6,4},{7,5},{8,10},{9,11},{10,... | collective-permute-start | bytes 958472 | tf_op jit(solution)/shard_map/ppermute | solution.py:57
  8.5 50.7 %collective-permute-start = (bf16[208,768]{1,0:T(8,128)(2,1)}, bf16[208,768]{1,0:T(8,128)(2,1)S(1)}, u32[]{:S(2)}, u32[]{:S(2)}) collective-permute-start(bf16[208,768]{1,0:T(8,128)(2,1)} %bitcast.284), channel_id=1, source_target_pairs={{0,1},{1,0},{2,3},{3,2},{4,5},{5,4},{6,7},{7,6},{8,9},{9,8},{10,11... | collective-permute-start | bytes 958472 | tf_op jit(solution)/shard_map/ppermute | solution.py:57
  10.4 20.2 %collective-permute-start.3 = (s32[208]{0:T(256)S(1)}, s32[208]{0:T(256)}, u32[]{:S(2)}, u32[]{:S(2)}) collective-permute-start(s32[208]{0:T(256)S(1)} %bitcast.328), channel_id=1, source_target_pairs={{0,1},{1,0},{2,3},{3,2},{4,5},{5,4},{6,7},{7,6},{8,9},{9,8},{10,11... | collective-permute-start | bytes 2504 | tf_op jit(solution)/shard_map/ppermute | solution.py:57
  12.7 20.5 %collective-permute-start.10 = (bf16[24,576]{1,0:T(8,128)(2,1)}, bf16[24,576]{1,0:T(8,128)(2,1)S(1)}, u32[]{:S(2)}, u32[]{:S(2)}) collective-permute-start(bf16[24,576]{1,0:T(8,128)(2,1)} %get-tuple-element.228), channel_id=1, source_target_pairs={{0,3},{1,2},{2,1},{3,0},{4,7},{5,6},{6,5},{7,4},{8,11},{9,10},{10,... | collective-permute-start | bytes 82952 | tf_op jit(solution)/shard_map/ppermute | solution.py:57
  16.1 43.9 %all-to-all-start = ((bf16[32,24,704]{2,1,0:T(8,128)(2,1)}), bf16[32,24,704]{2,1,0:T(8,128)(2,1)S(1)}, u32[]{:S(2)}, u32[]{:S(2)}) async-start(bf16[32,24,704]{2,1,0:T(8,128)(2,1)} %bitcast.4), calls=%async_computation | async-start | bytes 2359296 | tf_op jit(solution)/shard_map/all_to_all | solution.py:99
  21.2 90.5 %all-gather.3.cloned.1.call-start = ((), (), s32[]{:S(2)}) async-start(), calls=%async_computation.13 | async-start | bytes 2654208 | tf_op jit(solution)/shard_map/all_gather | solution.py:414
  60.7 21.6 %all-to-all-start.1 = ((bf16[8,24,768]{2,1,0:T(8,128)(2,1)}), bf16[8,24,768]{2,1,0:T(8,128)(2,1)S(1)}, u32[]{:S(2)}, u32[]{:S(2)}) async-start(bf16[8,24,768]{2,1,0:T(8,128)(2,1)} %broadcast_in_dim.27), calls=%async_computation.1 | async-start | bytes 589824 | tf_op jit(solution)/shard_map/all_to_all | solution.py:99
  90.5 58.7 %all-to-all-start.2 = ((bf16[8,96,1536]{2,1,0:T(8,128)(2,1)}), bf16[8,96,1536]{2,1,0:T(8,128)(2,1)S(1)}, u32[]{:S(2)}, u32[]{:S(2)}) async-start(bf16[8,96,1536]{2,1,0:T(8,128)(2,1)} %pad_maximum_fusion), calls=%async_computation.2 | async-start | bytes 4718592 | tf_op jit(solution)/shard_map/all_to_all | solution.py:99
  150.4 53.7 %all-to-all-start.3 = ((bf16[8,152,768]{2,1,0:T(8,128)(2,1)}), bf16[8,152,768]{2,1,0:T(8,128)(2,1)}, u32[]{:S(2)}, u32[]{:S(2)}) async-start(bf16[8,152,768]{2,1,0:T(8,128)(2,1)} %pad_maximum_fusion.1), calls=%async_computation.3 | async-start | bytes 3735552 | tf_op jit(solution)/shard_map/all_to_all | solution.py:99
  167.3 27.9 %collective-permute-start.27 = (bf16[768,768]{1,0:T(8,128)(2,1)}, bf16[768,768]{1,0:T(8,128)(2,1)}, u32[]{:S(2)}, u32[]{:S(2)}) collective-permute-start(bf16[768,768]{1,0:T(8,128)(2,1)} %slice.296.refs_5_), channel_id=1, source_target_pairs={{0,2},{1,3},{2,0},{3,1},{4,6},{5,7},{6,4},{7,5},{8,10},{9,11},{10,... | collective-permute-start | bytes 3538952 | tf_op jit(solution)/shard_map/ppermute | solution.py:57
  208.9 31.2 %all-to-all-start.4 = ((bf16[8,56,768]{2,1,0:T(8,128)(2,1)}), bf16[8,56,768]{2,1,0:T(8,128)(2,1)S(1)}, u32[]{:S(2)}, u32[]{:S(2)}) async-start(bf16[8,56,768]{2,1,0:T(8,128)(2,1)} %bitcast.60), calls=%async_computation.4 | async-start | bytes 1376256 | tf_op jit(solution)/shard_map/all_to_all | solution.py:99
  214.5 25.6 %collective-permute-start.29 = (bf16[768,768]{1,0:T(8,128)(2,1)}, bf16[768,768]{1,0:T(8,128)(2,1)}, u32[]{:S(2)}, u32[]{:S(2)}) collective-permute-start(bf16[768,768]{1,0:T(8,128)(2,1)} %bitcast.301), channel_id=1, source_target_pairs={{0,2},{1,3},{2,0},{3,1},{4,6},{5,7},{6,4},{7,5},{8,10},{9,11},{10,... | collective-permute-start | bytes 3538952 | tf_op jit(solution)/shard_map/ppermute | solution.py:57
  215.0 28.3 %collective-permute-start.31 = (bf16[448,768]{1,0:T(8,128)(2,1)S(1)}, bf16[448,768]{1,0:T(8,128)(2,1)}, u32[]{:S(2)}, u32[]{:S(2)}) collective-permute-start(bf16[448,768]{1,0:T(8,128)(2,1)S(1)} %bitcast.306), channel_id=1, source_target_pairs={{0,1},{1,0},{2,3},{3,2},{4,5},{5,4},{6,7},{7,6},{8,9},{9,8},{10,11... | collective-permute-start | bytes 2064392 | tf_op jit(solution)/shard_map/ppermute | solution.py:57
  270.2 27.5 %collective-permute-start.34 = (bf16[768,768]{1,0:T(8,128)(2,1)}, bf16[768,768]{1,0:T(8,128)(2,1)}, u32[]{:S(2)}, u32[]{:S(2)}) collective-permute-start(bf16[768,768]{1,0:T(8,128)(2,1)} %get-tuple-element.91), channel_id=1, source_target_pairs={{0,2},{1,3},{2,0},{3,1},{4,6},{5,7},{6,4},{7,5},{8,10},{9,11},{10,... | collective-permute-start | bytes 3538952 | tf_op jit(solution)/shard_map/ppermute | solution.py:57
  270.6 30.3 %all-to-all-start.5 = ((bf16[8,56,768]{2,1,0:T(8,128)(2,1)}), bf16[8,56,768]{2,1,0:T(8,128)(2,1)S(1)}, u32[]{:S(2)}, u32[]{:S(2)}) async-start(bf16[8,56,768]{2,1,0:T(8,128)(2,1)} %bitcast.65), calls=%async_computation.5 | async-start | bytes 1376256 | tf_op jit(solution)/shard_map/all_to_all | solution.py:99
  301.0 33.8 %all-to-all-start.6 = ((bf16[8,96,768]{2,1,0:T(8,128)(2,1)}), bf16[8,96,768]{2,1,0:T(8,128)(2,1)}, u32[]{:S(2)}, u32[]{:S(2)}) async-start(bf16[8,96,768]{2,1,0:T(8,128)(2,1)} %bitcast.290), calls=%async_computation.6 | async-start | bytes 2359296 | tf_op jit(solution)/shard_map/all_to_all | solution.py:99
  319.1 27.3 %collective-permute-start.35 = (bf16[768,768]{1,0:T(8,128)(2,1)}, bf16[768,768]{1,0:T(8,128)(2,1)}, u32[]{:S(2)}, u32[]{:S(2)}) collective-permute-start(bf16[768,768]{1,0:T(8,128)(2,1)} %get-tuple-element.92), channel_id=1, source_target_pairs={{0,2},{1,3},{2,0},{3,1},{4,6},{5,7},{6,4},{7,5},{8,10},{9,11},{10,... | collective-permute-start | bytes 3538952 | tf_op jit(solution)/shard_map/ppermute | solution.py:57
  349.5 48.2 %all-to-all-start.7 = ((bf16[8,152,768]{2,1,0:T(8,128)(2,1)}), bf16[8,152,768]{2,1,0:T(8,128)(2,1)}, u32[]{:S(2)}, u32[]{:S(2)}) async-start(bf16[8,152,768]{2,1,0:T(8,128)(2,1)} %pad_maximum_fusion.2), calls=%async_computation.7 | async-start | bytes 3735552 | tf_op jit(solution)/shard_map/all_to_all | solution.py:99
  355.1 155.3 %reduce-scatter.2.cloned.1.call-start = ((), (), s32[]{:S(2)}) async-start(), calls=%async_computation.12 | async-start | bytes 3981312 | tf_op jit(solution)/shard_map/reduce_scatter | solution.py:545
  384.5 23.1 %collective-permute-start.45 = (bf16[208,768]{1,0:T(8,128)(2,1)}, bf16[208,768]{1,0:T(8,128)(2,1)}, u32[]{:S(2)}, u32[]{:S(2)}) collective-permute-start(bf16[208,768]{1,0:T(8,128)(2,1)} %fusion.77), channel_id=1, source_target_pairs={{0,2},{1,3},{2,0},{3,1},{4,6},{5,7},{6,4},{7,5},{8,10},{9,11},{10,... | collective-permute-start | bytes 958472 | tf_op jit(solution)/shard_map/ppermute | solution.py:57
  441.9 29.8 %collective-permute-start.52 = (bf16[8,24,768]{2,1,0:T(8,128)(2,1)}, bf16[8,24,768]{2,1,0:T(8,128)(2,1)}, u32[]{:S(2)}, u32[]{:S(2)}) collective-permute-start(bf16[8,24,768]{2,1,0:T(8,128)(2,1)} %get-tuple-element.204), channel_id=1, source_target_pairs={{0,3},{1,2},{2,1},{3,0},{4,7},{5,6},{6,5},{7,4},{8,11},{9,10},{10,... | collective-permute-start | bytes 884744 | tf_op jit(solution)/shard_map/ppermute | solution.py:57
  442.2 29.6 %collective-permute-start.53 = (bf16[8,24,768]{2,1,0:T(8,128)(2,1)}, bf16[8,24,768]{2,1,0:T(8,128)(2,1)}, u32[]{:S(2)}, u32[]{:S(2)}) collective-permute-start(bf16[8,24,768]{2,1,0:T(8,128)(2,1)} %get-tuple-element.203), channel_id=1, source_target_pairs={{0,2},{1,3},{2,0},{3,1},{4,6},{5,7},{6,4},{7,5},{8,10},{9,11},{10,... | collective-permute-start | bytes 884744 | tf_op jit(solution)/shard_map/ppermute | solution.py:57
  443.3 28.5 %collective-permute-start.54 = (bf16[8,24,768]{2,1,0:T(8,128)(2,1)}, bf16[8,24,768]{2,1,0:T(8,128)(2,1)}, u32[]{:S(2)}, u32[]{:S(2)}) collective-permute-start(bf16[8,24,768]{2,1,0:T(8,128)(2,1)} %get-tuple-element.202), channel_id=1, source_target_pairs={{0,1},{1,0},{2,3},{3,2},{4,5},{5,4},{6,7},{7,6},{8,9},{9,8},{10,11... | collective-permute-start | bytes 884744 | tf_op jit(solution)/shard_map/ppermute | solution.py:57
  461.4 47.3 %all-to-all-start.9 = ((bf16[32,24,704]{2,1,0:T(8,128)(2,1)}), bf16[32,24,704]{2,1,0:T(8,128)(2,1)}, u32[]{:S(2)}, u32[]{:S(2)}) async-start(bf16[32,24,704]{2,1,0:T(8,128)(2,1)} %bitcast.82), calls=%async_computation.9 | async-start | bytes 2359296 | tf_op jit(solution)/shard_map/all_to_all | solution.py:99
  (155 other events, 1086.8 us)
Sparse Core Ops, SparseCore 0:
  46.7 51.4 all-gather.2
  407.7 98.5 reduce-scatter.1

commit v5 on v4

--- a/solution.py
+++ b/solution.py
@@ -281,7 +281,7 @@
 def mlp_back(dm_blocks, u, weights):
     tall, width = dm_blocks[0].shape
     outs = (jax.ShapeDtypeStruct(u.shape, BF),) + partial_shapes(NF * tall, width)
-    return whole(mlp_back_kernel, outs, (*dm_blocks, u, weights), 6 * 10**9)
+    return whole(mlp_back_kernel, outs, (*dm_blocks, u, weights), 10**8)
 
 
 def mlp_weights(c_blocks, dm_blocks, du, g, rest):
@@ -289,7 +289,7 @@
     if rows % 16 == 0:
         outs = jax.ShapeDtypeStruct((groups, rows, 3 * width), BF)
         args = (*c_blocks, *dm_blocks, du, g, rest)
-        return whole(mlp_weights_kernel, outs, args, 5 * 10**9, (pltpu.VMEM((width, width), F32),))
+        return whole(mlp_weights_kernel, outs, args, 10**8, (pltpu.VMEM((width, width), F32),))
     parts = [mm_tn(jnp.concatenate(c_blocks, axis=0), du.reshape(-1, width))]
     parts.append(mm_tn(g.reshape(-1, width), jnp.concatenate(dm_blocks, axis=0)))
     parts = [value.astype(BF).reshape(groups, rows, width) for value in parts]
@@ -541,12 +541,12 @@
         dm = gather_blocks(grad.astype(BF))
         du0, send, keep = mlp_back(dm, after(u0, attn_part), mlp_all)
         dc0 = scatter_blocks(send, keep)
-        dense_part = mlp_weights(c0, dm, du0, after(g0, got), attn_part)
+        dense_part = mlp_weights(c0, dm, du0, g0, attn_part)
         dense_sum = lax.psum_scatter(dense_part, "dp")
         gain1, bias1 = sums(dc0, xhat1)
         grad = grad + norm_back(dc0, xhat1, inv1, gains[1])
 
-        dy0 = gather_blocks(grad.astype(BF))
+        dy0 = gather_blocks(after(grad.astype(BF), got))
         dqkv0, send, keep = attend_back([after(dy0[0], dense_part), *dy0[1:]], w_qkv0, w_out0, qkv0, lse0, code_all)
         out_part0 = mm_tn(o0, jnp.concatenate(dy0, axis=0)).astype(BF).reshape(n_dp, rows, width)
         out_got0 = exchange(after(out_part0, got), "dp")

time: 547 us -> 527 us (0.963)
  waiting for transfers between devices: 174 us -> 165 us
  local copies, waits for them, and re-layouts: 77.3 us -> 68.5 us
    all_to_all x11, waiting for transfers between devices: 53.8 us -> 22.3 us  [exchange(): lax.all_to_all(value, axes, 0, 0, axis_index_groups=groups, tiled=True)]
    ppermute x53, waiting for transfers between devices: 120 us -> 140 us  [swap(): return lax.ppermute(value, 'fsdp', [(i, i ^ bits) for i in range(NF)])]
    unnamed x227 -> x201, local copies, waits for them, and re-layouts: 24 us -> 22.3 us
  transfers between devices with their start and end apart: 68 -> 68, of which waited for: 30 -> 34; matrix products, arithmetic and copies ran while one was open for 21% -> 20% of each run, Pallas kernels for 10% -> 10%
where the time goes in v5:
time: 527 us; the launch traced here: 516 us
  waiting for transfers between devices  165 us (31%)
  starting transfers between devices  121 us (23%)
  Pallas kernels  73.6 us (14%)
  local copies, waits for them, and re-layouts  68.5 us (13%)
  other arithmetic  58.8 us (11%)
  between operations  16 us (3%)
  matrix products  14.2 us (3%)
    ppermute x53, waiting for transfers between devices, swap(): return lax.ppermute(value, 'fsdp', [(i, i ^ bits) for i in range(NF)])  140 us
    all_to_all x11, starting transfers between devices, exchange(): lax.all_to_all(value, axes, 0, 0, axis_index_groups=groups, tiled=True)  60 us
    ppermute x53, starting transfers between devices, swap(): return lax.ppermute(value, 'fsdp', [(i, i ^ bits) for i in range(NF)])  53 us
    pallas_call x9, Pallas kernels, whole(): pl.pallas_call(kernel, out_shape=outs, in_specs=[space] * len(args), out_...  52.9 us
    unnamed x201, local copies, waits for them, and re-layouts  22.3 us
    all_to_all x11, waiting for transfers between devices, exchange(): lax.all_to_all(value, axes, 0, 0, axis_index_groups=groups, tiled=True)  22.3 us
    pallas_call x1, Pallas kernels, expert_compute(): pl.pallas_call(expert_kernel, out_shape=outs, in_specs=[pl.BlockSpec(memo...  20.7 us
    dot_general x6, matrix products, mm_tn(): lax.dot_general(left, right, (((0,), (0,)), ((), ())), preferred_element_...  12.6 us
  transfers between devices with their start and end apart: 68, of which 34 were waited for; matrix products, arithmetic and copies ran while one was open for 20% of the time, Pallas kernels for 10%

profile of v5, /device:TPU:5, one launch (start us, length us, event | category | flops | bytes accessed | tf_op | source)
XLA Modules:
  0.0 516.5 jit_solution(15601878248425833324)
XLA Ops:
  39.2 5.7 %collective-permute-start.6 = (bf16[2,24,768]{2,1,0:T(8,128)(2,1)}, bf16[2,24,768]{2,1,0:T(8,128)(2,1)S(1)}, u32[]{:S(2)}, u32[]{:S(2)}) collective-permute-start(bf16[2,24,768]{2,1,0:T(8,128)(2,1)} %param.23), channel_id=1, source_target_pairs={{0,0},{1,4},{2,8},{3,12},{4,16},{5,20},{6,24},{7,28},{8,1},{9,5},{... | collective-permute-start | bytes 221192 | tf_op jit(solution)/shard_map/ppermute | solution.py:418
  48.8 5.7 %collective-permute-done.8 = bf16[8,24,768]{2,1,0:T(8,128)(2,1)S(1)} collective-permute-done((bf16[8,24,768]{2,1,0:T(8,128)(2,1)}, bf16[8,24,768]{2,1,0:T(8,128)(2,1)S(1)}, u32[]{:S(2)}, u32[]{:S(2)}) %collective-permute-start.8) | collective-permute-done | bytes 294944 | tf_op jit(solution)/shard_map/ppermute | solution.py:57
  60.7 8.2 %all-to-all-start.1 = ((bf16[8,24,768]{2,1,0:T(8,128)(2,1)}), bf16[8,24,768]{2,1,0:T(8,128)(2,1)S(1)}, u32[]{:S(2)}, u32[]{:S(2)}) async-start(bf16[8,24,768]{2,1,0:T(8,128)(2,1)} %broadcast_in_dim.27), calls=%async_computation.1 | async-start | bytes 589824 | tf_op jit(solution)/shard_map/all_to_all | solution.py:99
  74.5 6.1 %shard_map.238 = (bf16[832,576]{1,0:T(8,128)(2,1)S(1)}, bf16[832,192]{1,0:T(8,128)(2,1)S(1)}, f32[3,832]{1,0:T(4,128)S(1)}) custom-call(bf16[832,768]{1,0:T(8,128)(2,1)S(1)} %get-tuple-element.191.refs_0_, bf16[768,704]{1,0:T(8,128)(2,1)S(1)} %bitcast.279, s32[832,1]{1,0:T(8,128)S(1)} %broadcast_in_dim.32.refs_2_.refs_5_.refs_8_, ...), custom_call_target="tpu_custom_call" | custom-call | flops 400000000 | bytes 65536 | tf_op jit(solution)/shard_map/pallas_call | solution.py:233
  90.5 5.6 %all-to-all-start.2 = ((bf16[8,96,1536]{2,1,0:T(8,128)(2,1)}), bf16[8,96,1536]{2,1,0:T(8,128)(2,1)S(1)}, u32[]{:S(2)}, u32[]{:S(2)}) async-start(bf16[8,96,1536]{2,1,0:T(8,128)(2,1)} %pad_maximum_fusion), calls=%async_computation.2 | async-start | bytes 4718592 | tf_op jit(solution)/shard_map/all_to_all | solution.py:99
  124.7 5.9 %collective-permute-done.22 = bf16[208,768]{1,0:T(8,128)(2,1)S(1)} collective-permute-done((bf16[208,768]{1,0:T(8,128)(2,1)S(1)}, bf16[208,768]{1,0:T(8,128)(2,1)S(1)}, u32[]{:S(2)}, u32[]{:S(2)}) %collective-permute-start.22) | collective-permute-done | bytes 319520 | tf_op jit(solution)/shard_map/ppermute | solution.py:57
  132.2 16.9 %all-to-all-done.2 = bf16[8,96,1536]{2,1,0:T(8,128)(2,1)S(1)} async-done(((bf16[8,96,1536]{2,1,0:T(8,128)(2,1)}), bf16[8,96,1536]{2,1,0:T(8,128)(2,1)S(1)}, u32[]{:S(2)}, u32[]{:S(2)}) %all-to-all-start.2) | async-done | bytes 2359328 | tf_op jit(solution)/shard_map/all_to_all | solution.py:99
  159.2 5.5 %collective-permute-done.24.refs_2_ = bf16[208,768]{1,0:T(8,128)(2,1)} collective-permute-done((bf16[208,768]{1,0:T(8,128)(2,1)}, bf16[208,768]{1,0:T(8,128)(2,1)}, u32[]{:S(2)}, u32[]{:S(2)}) %collective-permute-start.24) | collective-permute-done | bytes 319520 | tf_op jit(solution)/shard_map/ppermute | solution.py:57
  171.5 7.4 %shard_map.241 = (bf16[832,576]{1,0:T(8,128)(2,1)S(1)}, bf16[832,192]{1,0:T(8,128)(2,1)S(1)}, f32[3,832]{1,0:T(4,128)S(1)}) custom-call(bf16[208,768]{1,0:T(8,128)(2,1)} %add_convert_fusion.6.refs_0_, bf16[208,768]{1,0:T(8,128)(2,1)} %collective-permute-done.23.refs_1_, bf16[208,768]{1,0:T(8,128)(2,1)} %collective-permute-done.24.refs_2_, ...), custom_call_target="tpu_custom_call" | custom-call | flops 400000000 | bytes 65536 | tf_op jit(solution)/shard_map/pallas_call | solution.py:233
  183.4 11.7 %collective-permute-done.27.refs_6_ = bf16[768,768]{1,0:T(8,128)(2,1)} collective-permute-done((bf16[768,768]{1,0:T(8,128)(2,1)}, bf16[768,768]{1,0:T(8,128)(2,1)}, u32[]{:S(2)}, u32[]{:S(2)}) %collective-permute-start.27) | collective-permute-done | bytes 1179680 | tf_op jit(solution)/shard_map/ppermute | solution.py:57
  195.4 8.0 %collective-permute-done.28 = bf16[208,768]{1,0:T(8,128)(2,1)S(1)} collective-permute-done((bf16[208,768]{1,0:T(8,128)(2,1)S(1)}, bf16[208,768]{1,0:T(8,128)(2,1)S(1)}, u32[]{:S(2)}, u32[]{:S(2)}) %collective-permute-start.28) | collective-permute-done | bytes 319520 | tf_op jit(solution)/shard_map/ppermute | solution.py:57
  209.1 5.6 %all-to-all-start.4 = ((bf16[8,56,768]{2,1,0:T(8,128)(2,1)}), bf16[8,56,768]{2,1,0:T(8,128)(2,1)}, u32[]{:S(2)}, u32[]{:S(2)}) async-start(bf16[8,56,768]{2,1,0:T(8,128)(2,1)} %bitcast.60), calls=%async_computation.4 | async-start | bytes 1376256 | tf_op jit(solution)/shard_map/all_to_all | solution.py:99
  217.6 22.5 %collective-permute-done.29.refs_8_ = bf16[768,768]{1,0:T(8,128)(2,1)} collective-permute-done((bf16[768,768]{1,0:T(8,128)(2,1)S(1)}, bf16[768,768]{1,0:T(8,128)(2,1)}, u32[]{:S(2)}, u32[]{:S(2)}) %collective-permute-start.29) | collective-permute-done | bytes 1179680 | tf_op jit(solution)/shard_map/ppermute | solution.py:57
  246.0 20.7 %shard_map.243 = (bf16[448,768]{1,0:T(8,128)(2,1)}, f32[448,768]{1,0:T(8,128)}, bf16[448,768]{1,0:T(8,128)(2,1)}, f32[448,768]{1,0:T(8,128)}, f32[768,768]{1,0:T...) custom-call(s32[1]{0:T(128)} %bitcast.55.refs_0_, ...), custom_call_target="tpu_custom_call" | custom-call | flops 16911433728 | bytes 16777216 | tf_op jit(solution)/shard_map/pallas_call | solution.py:353
  271.8 5.4 %all-to-all-start.5 = ((bf16[8,56,768]{2,1,0:T(8,128)(2,1)}), bf16[8,56,768]{2,1,0:T(8,128)(2,1)}, u32[]{:S(2)}, u32[]{:S(2)}) async-start(bf16[8,56,768]{2,1,0:T(8,128)(2,1)} %bitcast.65), calls=%async_computation.5 | async-start | bytes 1376256 | tf_op jit(solution)/shard_map/all_to_all | solution.py:99
  277.2 21.6 %collective-permute-done.34 = bf16[768,768]{1,0:T(8,128)(2,1)S(1)} collective-permute-done((bf16[768,768]{1,0:T(8,128)(2,1)}, bf16[768,768]{1,0:T(8,128)(2,1)S(1)}, u32[]{:S(2)}, u32[]{:S(2)}) %collective-permute-start.34) | collective-permute-done | bytes 1179680 | tf_op jit(solution)/shard_map/ppermute | solution.py:57
  304.1 5.6 %all-to-all-start.6 = ((bf16[8,96,768]{2,1,0:T(8,128)(2,1)}), bf16[8,96,768]{2,1,0:T(8,128)(2,1)}, u32[]{:S(2)}, u32[]{:S(2)}) async-start(bf16[8,96,768]{2,1,0:T(8,128)(2,1)} %bitcast.64), calls=%async_computation.6 | async-start | bytes 2359296 | tf_op jit(solution)/shard_map/all_to_all | solution.py:99
  322.5 10.7 %shard_map.244 = (bf16[832,576]{1,0:T(8,128)(2,1)S(1)}, bf16[2,208,768]{2,1,0:T(8,128)(2,1)S(1)}, f32[2,208,768]{2,1,0:T(8,128)S(1)}) custom-call(bf16[208,768]{1,0:T(8,128)(2,1)S(1)} %get-tuple-element.183.refs_0_, bf16[208,768]{1,0:T(8,128)(2,1)S(1)} %collective-permute-done.36.refs_1_, bf16[208,768]{1,0:T(8,128)(2,1)S(1)} %collective-permute-done.37.refs_2_, ...), custom_call_target="tpu_custom_call" | custom-call | flops 11000000512 | bytes 65536 | tf_op jit(solution)/shard_map/pallas_call | solution.py:233
  351.2 5.6 %all-to-all-start.7 = ((bf16[8,152,768]{2,1,0:T(8,128)(2,1)}), bf16[8,152,768]{2,1,0:T(8,128)(2,1)}, u32[]{:S(2)}, u32[]{:S(2)}) async-start(bf16[8,152,768]{2,1,0:T(8,128)(2,1)} %pad_maximum_fusion.2), calls=%async_computation.7 | async-start | bytes 3735552 | tf_op jit(solution)/shard_map/all_to_all | solution.py:99
  384.7 6.0 %shard_map.246 = bf16[8,96,2304]{2,1,0:T(8,128)(2,1)} custom-call(bf16[208,768]{1,0:T(8,128)(2,1)S(1)} %copy-done.8, bf16[208,768]{1,0:T(8,128)(2,1)S(1)} %copy-done.11, bf16[208,768]{1,0:T(8,128)(2,1)} %collective-permute-done.16.refs_2_, bf16[208,768]{1,0:T(8,128)(2,1)} %collective-permute-done.17.refs_3_, ...), custom_call_target="tpu_custom_call" | custom-call | flops 100000000 | bytes 65536 | tf_op jit(solution)/shard_map/pallas_call | solution.py:233
  401.4 5.6 %collective-permute-done.47.refs_2_ = bf16[208,768]{1,0:T(8,128)(2,1)S(1)} collective-permute-done((bf16[208,768]{1,0:T(8,128)(2,1)S(1)}, bf16[208,768]{1,0:T(8,128)(2,1)S(1)}, u32[]{:S(2)}, u32[]{:S(2)}) %collective-permute-start.47) | collective-permute-done | bytes 319520 | tf_op jit(solution)/shard_map/ppermute | solution.py:57
  421.0 11.1 %shard_map.247 = (bf16[832,576]{1,0:T(8,128)(2,1)S(1)}, bf16[2,208,768]{2,1,0:T(8,128)(2,1)S(1)}, f32[2,208,768]{2,1,0:T(8,128)}) custom-call(bf16[208,768]{1,0:T(8,128)(2,1)S(1)} %get-tuple-element.109.refs_0_, bf16[208,768]{1,0:T(8,128)(2,1)S(1)} %collective-permute-done.46.refs_1_, bf16[208,768]{1,0:T(8,128)(2,1)S(1)} %collective-permute-done.47.refs_2_, ...), custom_call_target="tpu_custom_call" | custom-call | flops 11000000512 | bytes 65536 | tf_op jit(solution)/shard_map/pallas_call | solution.py:233
  454.0 10.9 %collective-permute-done.52 = bf16[8,24,768]{2,1,0:T(8,128)(2,1)S(1)} collective-permute-done((bf16[8,24,768]{2,1,0:T(8,128)(2,1)S(1)}, bf16[8,24,768]{2,1,0:T(8,128)(2,1)S(1)}, u32[]{:S(2)}, u32[]{:S(2)}) %collective-permute-start.52) | collective-permute-done | bytes 294944 | tf_op jit(solution)/shard_map/ppermute | solution.py:57
  464.9 7.2 %collective-permute-done.53 = bf16[8,24,768]{2,1,0:T(8,128)(2,1)S(1)} collective-permute-done((bf16[8,24,768]{2,1,0:T(8,128)(2,1)S(1)}, bf16[8,24,768]{2,1,0:T(8,128)(2,1)S(1)}, u32[]{:S(2)}, u32[]{:S(2)}) %collective-permute-start.53) | collective-permute-done | bytes 294944 | tf_op jit(solution)/shard_map/ppermute | solution.py:57
  (494 shorter events, 275.2 us)
Async XLA Ops:
  7.2 49.3 %collective-permute-start.1 = (bf16[208,768]{1,0:T(8,128)(2,1)}, bf16[208,768]{1,0:T(8,128)(2,1)S(1)}, u32[]{:S(2)}, u32[]{:S(2)}) collective-permute-start(bf16[208,768]{1,0:T(8,128)(2,1)} %bitcast.283), channel_id=1, source_target_pairs={{0,2},{1,3},{2,0},{3,1},{4,6},{5,7},{6,4},{7,5},{8,10},{9,11},{10,... | collective-permute-start | bytes 958472 | tf_op jit(solution)/shard_map/ppermute | solution.py:57
  8.5 50.6 %collective-permute-start = (bf16[208,768]{1,0:T(8,128)(2,1)}, bf16[208,768]{1,0:T(8,128)(2,1)S(1)}, u32[]{:S(2)}, u32[]{:S(2)}) collective-permute-start(bf16[208,768]{1,0:T(8,128)(2,1)} %bitcast.284), channel_id=1, source_target_pairs={{0,1},{1,0},{2,3},{3,2},{4,5},{5,4},{6,7},{7,6},{8,9},{9,8},{10,11... | collective-permute-start | bytes 958472 | tf_op jit(solution)/shard_map/ppermute | solution.py:57
  10.4 20.2 %collective-permute-start.3 = (s32[208]{0:T(256)S(1)}, s32[208]{0:T(256)}, u32[]{:S(2)}, u32[]{:S(2)}) collective-permute-start(s32[208]{0:T(256)S(1)} %bitcast.324), channel_id=1, source_target_pairs={{0,1},{1,0},{2,3},{3,2},{4,5},{5,4},{6,7},{7,6},{8,9},{9,8},{10,11... | collective-permute-start | bytes 2504 | tf_op jit(solution)/shard_map/ppermute | solution.py:57
  12.7 20.4 %collective-permute-start.10 = (bf16[24,576]{1,0:T(8,128)(2,1)}, bf16[24,576]{1,0:T(8,128)(2,1)S(1)}, u32[]{:S(2)}, u32[]{:S(2)}) collective-permute-start(bf16[24,576]{1,0:T(8,128)(2,1)} %get-tuple-element.228), channel_id=1, source_target_pairs={{0,3},{1,2},{2,1},{3,0},{4,7},{5,6},{6,5},{7,4},{8,11},{9,10},{10,... | collective-permute-start | bytes 82952 | tf_op jit(solution)/shard_map/ppermute | solution.py:57
  16.1 43.9 %all-to-all-start = ((bf16[32,24,704]{2,1,0:T(8,128)(2,1)}), bf16[32,24,704]{2,1,0:T(8,128)(2,1)S(1)}, u32[]{:S(2)}, u32[]{:S(2)}) async-start(bf16[32,24,704]{2,1,0:T(8,128)(2,1)} %bitcast.4), calls=%async_computation | async-start | bytes 2359296 | tf_op jit(solution)/shard_map/all_to_all | solution.py:99
  21.2 90.1 %all-gather.3.cloned.1.call-start = ((), (), s32[]{:S(2)}) async-start(), calls=%async_computation.13 | async-start | bytes 2654208 | tf_op jit(solution)/shard_map/all_gather | solution.py:414
  60.7 22.7 %all-to-all-start.1 = ((bf16[8,24,768]{2,1,0:T(8,128)(2,1)}), bf16[8,24,768]{2,1,0:T(8,128)(2,1)S(1)}, u32[]{:S(2)}, u32[]{:S(2)}) async-start(bf16[8,24,768]{2,1,0:T(8,128)(2,1)} %broadcast_in_dim.27), calls=%async_computation.1 | async-start | bytes 589824 | tf_op jit(solution)/shard_map/all_to_all | solution.py:99
  90.5 58.7 %all-to-all-start.2 = ((bf16[8,96,1536]{2,1,0:T(8,128)(2,1)}), bf16[8,96,1536]{2,1,0:T(8,128)(2,1)S(1)}, u32[]{:S(2)}, u32[]{:S(2)}) async-start(bf16[8,96,1536]{2,1,0:T(8,128)(2,1)} %pad_maximum_fusion), calls=%async_computation.2 | async-start | bytes 4718592 | tf_op jit(solution)/shard_map/all_to_all | solution.py:99
  150.3 53.7 %all-to-all-start.3 = ((bf16[8,152,768]{2,1,0:T(8,128)(2,1)}), bf16[8,152,768]{2,1,0:T(8,128)(2,1)}, u32[]{:S(2)}, u32[]{:S(2)}) async-start(bf16[8,152,768]{2,1,0:T(8,128)(2,1)} %pad_maximum_fusion.1), calls=%async_computation.3 | async-start | bytes 3735552 | tf_op jit(solution)/shard_map/all_to_all | solution.py:99
  167.2 27.9 %collective-permute-start.27 = (bf16[768,768]{1,0:T(8,128)(2,1)}, bf16[768,768]{1,0:T(8,128)(2,1)}, u32[]{:S(2)}, u32[]{:S(2)}) collective-permute-start(bf16[768,768]{1,0:T(8,128)(2,1)} %slice.296.refs_5_), channel_id=1, source_target_pairs={{0,2},{1,3},{2,0},{3,1},{4,6},{5,7},{6,4},{7,5},{8,10},{9,11},{10,... | collective-permute-start | bytes 3538952 | tf_op jit(solution)/shard_map/ppermute | solution.py:57
  209.1 31.0 %all-to-all-start.4 = ((bf16[8,56,768]{2,1,0:T(8,128)(2,1)}), bf16[8,56,768]{2,1,0:T(8,128)(2,1)}, u32[]{:S(2)}, u32[]{:S(2)}) async-start(bf16[8,56,768]{2,1,0:T(8,128)(2,1)} %bitcast.60), calls=%async_computation.4 | async-start | bytes 1376256 | tf_op jit(solution)/shard_map/all_to_all | solution.py:99
  214.7 25.4 %collective-permute-start.29 = (bf16[768,768]{1,0:T(8,128)(2,1)S(1)}, bf16[768,768]{1,0:T(8,128)(2,1)}, u32[]{:S(2)}, u32[]{:S(2)}) collective-permute-start(bf16[768,768]{1,0:T(8,128)(2,1)S(1)} %bitcast.300), channel_id=1, source_target_pairs={{0,2},{1,3},{2,0},{3,1},{4,6},{5,7},{6,4},{7,5},{8,10},{9,11},{10,... | collective-permute-start | bytes 3538952 | tf_op jit(solution)/shard_map/ppermute | solution.py:57
  215.1 28.2 %collective-permute-start.31 = (bf16[448,768]{1,0:T(8,128)(2,1)}, bf16[448,768]{1,0:T(8,128)(2,1)}, u32[]{:S(2)}, u32[]{:S(2)}) collective-permute-start(bf16[448,768]{1,0:T(8,128)(2,1)} %bitcast.305), channel_id=1, source_target_pairs={{0,1},{1,0},{2,3},{3,2},{4,5},{5,4},{6,7},{7,6},{8,9},{9,8},{10,11... | collective-permute-start | bytes 2064392 | tf_op jit(solution)/shard_map/ppermute | solution.py:57
  271.4 27.4 %collective-permute-start.34 = (bf16[768,768]{1,0:T(8,128)(2,1)}, bf16[768,768]{1,0:T(8,128)(2,1)S(1)}, u32[]{:S(2)}, u32[]{:S(2)}) collective-permute-start(bf16[768,768]{1,0:T(8,128)(2,1)} %get-tuple-element.91), channel_id=1, source_target_pairs={{0,2},{1,3},{2,0},{3,1},{4,6},{5,7},{6,4},{7,5},{8,10},{9,11},{10,... | collective-permute-start | bytes 3538952 | tf_op jit(solution)/shard_map/ppermute | solution.py:57
  271.8 30.0 %all-to-all-start.5 = ((bf16[8,56,768]{2,1,0:T(8,128)(2,1)}), bf16[8,56,768]{2,1,0:T(8,128)(2,1)}, u32[]{:S(2)}, u32[]{:S(2)}) async-start(bf16[8,56,768]{2,1,0:T(8,128)(2,1)} %bitcast.65), calls=%async_computation.5 | async-start | bytes 1376256 | tf_op jit(solution)/shard_map/all_to_all | solution.py:99
  304.1 33.4 %all-to-all-start.6 = ((bf16[8,96,768]{2,1,0:T(8,128)(2,1)}), bf16[8,96,768]{2,1,0:T(8,128)(2,1)}, u32[]{:S(2)}, u32[]{:S(2)}) async-start(bf16[8,96,768]{2,1,0:T(8,128)(2,1)} %bitcast.64), calls=%async_computation.6 | async-start | bytes 2359296 | tf_op jit(solution)/shard_map/all_to_all | solution.py:99
  320.9 27.3 %collective-permute-start.35 = (bf16[768,768]{1,0:T(8,128)(2,1)}, bf16[768,768]{1,0:T(8,128)(2,1)}, u32[]{:S(2)}, u32[]{:S(2)}) collective-permute-start(bf16[768,768]{1,0:T(8,128)(2,1)} %get-tuple-element.92), channel_id=1, source_target_pairs={{0,2},{1,3},{2,0},{3,1},{4,6},{5,7},{6,4},{7,5},{8,10},{9,11},{10,... | collective-permute-start | bytes 3538952 | tf_op jit(solution)/shard_map/ppermute | solution.py:57
  351.2 48.2 %all-to-all-start.7 = ((bf16[8,152,768]{2,1,0:T(8,128)(2,1)}), bf16[8,152,768]{2,1,0:T(8,128)(2,1)}, u32[]{:S(2)}, u32[]{:S(2)}) async-start(bf16[8,152,768]{2,1,0:T(8,128)(2,1)} %pad_maximum_fusion.2), calls=%async_computation.7 | async-start | bytes 3735552 | tf_op jit(solution)/shard_map/all_to_all | solution.py:99
  356.8 132.3 %reduce-scatter.2.cloned.1.call-start = ((), (), s32[]{:S(2)}) async-start(), calls=%async_computation.12 | async-start | bytes 3981312 | tf_op jit(solution)/shard_map/reduce_scatter | solution.py:545
  414.8 23.8 %all-to-all-start.8 = ((bf16[8,24,768]{2,1,0:T(8,128)(2,1)}), bf16[8,24,768]{2,1,0:T(8,128)(2,1)S(1)}, u32[]{:S(2)}, u32[]{:S(2)}) async-start(bf16[8,24,768]{2,1,0:T(8,128)(2,1)} %bitcast.312), calls=%async_computation.8 | async-start | bytes 589824 | tf_op jit(solution)/shard_map/all_to_all | solution.py:99
  440.1 45.7 %all-to-all-start.9 = ((bf16[32,24,704]{2,1,0:T(8,128)(2,1)}), bf16[32,24,704]{2,1,0:T(8,128)(2,1)}, u32[]{:S(2)}, u32[]{:S(2)}) async-start(bf16[32,24,704]{2,1,0:T(8,128)(2,1)} %bitcast.82), calls=%async_computation.9 | async-start | bytes 2359296 | tf_op jit(solution)/shard_map/all_to_all | solution.py:99
  449.2 22.9 %collective-permute-start.53 = (bf16[8,24,768]{2,1,0:T(8,128)(2,1)S(1)}, bf16[8,24,768]{2,1,0:T(8,128)(2,1)S(1)}, u32[]{:S(2)}, u32[]{:S(2)}) collective-permute-start(bf16[8,24,768]{2,1,0:T(8,128)(2,1)S(1)} %get-tuple-element.203), channel_id=1, source_target_pairs={{0,2},{1,3},{2,0},{3,1},{4,6},{5,7},{6,4},{7,5},{8,10},{9,11},{10,... | collective-permute-start | bytes 884744 | tf_op jit(solution)/shard_map/ppermute | solution.py:57
  449.5 22.6 %collective-permute-start.54 = (bf16[8,24,768]{2,1,0:T(8,128)(2,1)S(1)}, bf16[8,24,768]{2,1,0:T(8,128)(2,1)S(1)}, u32[]{:S(2)}, u32[]{:S(2)}) collective-permute-start(bf16[8,24,768]{2,1,0:T(8,128)(2,1)S(1)} %get-tuple-element.202), channel_id=1, source_target_pairs={{0,1},{1,0},{2,3},{3,2},{4,5},{5,4},{6,7},{7,6},{8,9},{9,8},{10,11... | collective-permute-start | bytes 884744 | tf_op jit(solution)/shard_map/ppermute | solution.py:57
  452.8 30.2 %collective-permute-start.50 = (bf16[208,768]{1,0:T(8,128)(2,1)}, bf16[208,768]{1,0:T(8,128)(2,1)}, u32[]{:S(2)}, u32[]{:S(2)}) collective-permute-start(bf16[208,768]{1,0:T(8,128)(2,1)} %get-tuple-element.201), channel_id=1, source_target_pairs={{0,2},{1,3},{2,0},{3,1},{4,6},{5,7},{6,4},{7,5},{8,10},{9,11},{10,... | collective-permute-start | bytes 958472 | tf_op jit(solution)/shard_map/ppermute | solution.py:57
  (142 other events, 1009.5 us)
Sparse Core Ops, SparseCore 0:
  46.7 51.4 all-gather.2
  390.9 98.2 reduce-scatter.1

commit v6 on v5

--- a/solution.py
+++ b/solution.py
@@ -296,51 +296,73 @@
     return jnp.concatenate(parts + [rest], axis=2)
 
 
-def expert_kernel(*refs):
-    own_ref, x_refs, dz_refs, in_refs, out_refs = refs[0], refs[1:3], refs[3:5], refs[5:7], refs[7:9]
-    router_ref, dx_send, dx_keep, y_send, y_keep = refs[9:14]
-    din_own, din_far, dout_own, dout_far, drouter_ref, din_sum, dout_sum = refs[14:]
+def expert_gate(own, x, router):
+    logits = mm(x, router)
+    lane = lax.broadcasted_iota(jnp.int32, logits.shape, 1)
+    shifted = jnp.exp(logits - jnp.max(logits, axis=1, keepdims=True))
+    probs = shifted / jnp.sum(shifted, axis=1, keepdims=True)
+    mine = (lane == own).astype(F32)
+    return probs, mine, jnp.sum(probs * mine, axis=1, keepdims=True)
+
+
+def expert_quarter(x, dyx, w_in, w_out):
+    ue = mm(x, w_in)
+    cdf = 0.5 * (1.0 + lax.erf(ue * (0.5**0.5)))
+    slope = cdf + ue * jnp.exp(-0.5 * ue * ue) * 0.3989422804014327
+    ge = (ue * cdf).astype(BF)
+    due = (dot(dyx, w_out, 1, 1) * slope).astype(BF)
+    return mm(ge, w_out), dot(due, w_in, 1, 1), dot(x, due, 0, 0), dot(ge, dyx, 0, 0)
+
+
+def expert_near_kernel(own_ref, x0, x1, dz0, dz1, in_ref, out_ref, router_ref, y_ref, dx_ref, din_ref, dout_ref):
+    for i, (x_ref, dz_ref) in enumerate(((x0, dz0), (x1, dz1))):
+        x = x_ref[...]
+        gate = expert_gate(own_ref[0], x, router_ref[...])[2].astype(BF).astype(F32)
+        dyx = (gate * dz_ref[...].astype(F32)).astype(BF)
+        y_ref[i], dx_ref[i], din, dout = expert_quarter(x, dyx, in_ref[...], out_ref[...])
+        if i == 0:
+            din_ref[...], dout_ref[...] = din, dout
+        else:
+            din_ref[...] += din
+            dout_ref[...] += dout
+
+
+def expert_far_kernel(*refs):
+    own_ref, x_refs, dz_refs, (in_ref, out_ref, router_ref, y_ref, dx_ref) = refs[0], refs[1:3], refs[3:5], refs[5:10]
+    dx_send, dx_keep, y_send, y_keep, din_ref, dout_ref, drouter_ref, din_sum, dout_sum = refs[10:]
     router = router_ref[...]
     for i in range(2):
-        x, dz = x_refs[i][...], dz_refs[i][...]
-        logits = mm(x, router)
-        lane = lax.broadcasted_iota(jnp.int32, logits.shape, 1)
-        shifted = jnp.exp(logits - jnp.max(logits, axis=1, keepdims=True))
-        probs = shifted / jnp.sum(shifted, axis=1, keepdims=True)
-        mine = (lane == own_ref[0]).astype(F32)
-        prob = jnp.sum(probs * mine, axis=1, keepdims=True)
+        x, dz = x_refs[i][...], dz_refs[i][...].astype(F32)
+        probs, mine, prob = expert_gate(own_ref[0], x, router)
         gate = prob.astype(BF).astype(F32)
-        dz_wide = dz.astype(F32)
-        dyx = (gate * dz_wide).astype(BF)
-        y = dx = None
-        for j in range(2):
-            w_in, w_out = in_refs[j][...], out_refs[j][...]
-            ue = mm(x, w_in)
-            cdf = 0.5 * (1.0 + lax.erf(ue * (0.5**0.5)))
-            slope = cdf + ue * jnp.exp(-0.5 * ue * ue) * 0.3989422804014327
-            ge = (ue * cdf).astype(BF)
-            due = (dot(dyx, w_out, 1, 1) * slope).astype(BF)
-            term = mm(ge, w_out)
-            y = term if j == 0 else y + term
-            term = dot(due, w_in, 1, 1)
-            dx = term if j == 0 else dx + term
-            din, dout = dot(x, due, 0, 0), dot(ge, dyx, 0, 0)
-            din_ref, dout_ref = (din_own, dout_own) if j == 0 else (din_sum, dout_sum)
-            if i == 0:
-                din_ref[...], dout_ref[...] = din, dout
-            else:
-                din_ref[...] += din
-                dout_ref[...] += dout
-        dgate = jnp.sum(dz_wide * y, axis=1, keepdims=True)
+        y, dx, din, dout = expert_quarter(x, (gate * dz).astype(BF), in_ref[...], out_ref[...])
+        y, dx = y + y_ref[i], dx + dx_ref[i]
+        dgate = jnp.sum(dz * y, axis=1, keepdims=True)
         dlogits = (dgate * prob * (mine - probs)).astype(BF)
         dx = dx + dot(dlogits, router, 1, 1)
         y = gate * y
         if i == 0:
-            dx_keep[...], y_keep[...], drouter_ref[...] = dx, y, dot(x, dlogits, 0, 0)
-        else:
+            din_sum[...], dout_sum[...], drouter_ref[...] = din, dout, dot(x, dlogits, 0, 0)
+            dx_keep[...], y_keep[...] = dx, y
+        else:
+            din_sum[...] += din
+            dout_sum[...] += dout
+            drouter_ref[...] += dot(x, dlogits, 0, 0)
             dx_send[...], y_send[...] = dx.astype(BF), y.astype(BF)
-            drouter_ref[...] += dot(x, dlogits, 0, 0)
-    din_far[...], dout_far[...] = din_sum[...].astype(BF), dout_sum[...].astype(BF)
+    din_ref[...], dout_ref[...] = din_sum[...].astype(BF), dout_sum[...].astype(BF)
+
+
+def expert_call(kernel, outs, own, args, flops, scratch=()):
+    space = pl.BlockSpec(memory_space=pltpu.VMEM)
+    return pl.pallas_call(
+        kernel,
+        out_shape=outs,
+        in_specs=[pl.BlockSpec(memory_space=pltpu.SMEM)] + [space] * len(args),
+        out_specs=(space,) * len(outs),
+        scratch_shapes=scratch,
+        compiler_params=pltpu.CompilerParams(vmem_limit_bytes=56 * 2**20),
+        cost_estimate=pl.CostEstimate(flops=flops, bytes_accessed=2**20, transcendentals=0),
+    )(own.astype(jnp.int32)[None], *args)
 
 
 def expert_compute(own, x_blocks, dz_blocks, w_in, w_out, router):
@@ -348,19 +370,16 @@
     square = w_in[0].shape
     send, keep = jax.ShapeDtypeStruct((tall, width), BF), jax.ShapeDtypeStruct((tall, width), F32)
     near, far = jax.ShapeDtypeStruct(square, F32), jax.ShapeDtypeStruct(square, BF)
-    outs = (send, keep, send, keep, near, far, near, far, jax.ShapeDtypeStruct(router.shape, F32))
-    space = pl.BlockSpec(memory_space=pltpu.VMEM)
-    return pl.pallas_call(
-        expert_kernel,
-        out_shape=outs,
-        in_specs=[pl.BlockSpec(memory_space=pltpu.SMEM)] + [space] * 9,
-        out_specs=(space,) * len(outs),
-        scratch_shapes=[pltpu.VMEM(square, F32), pltpu.VMEM(square, F32)],
-        compiler_params=pltpu.CompilerParams(vmem_limit_bytes=56 * 2**20),
-        cost_estimate=pl.CostEstimate(
-            flops=64 * tall * width * square[1], bytes_accessed=2**24, transcendentals=0
-        ),
-    )(own.astype(jnp.int32)[None], *x_blocks, *dz_blocks, *w_in, *w_out, router)
+    both = jax.ShapeDtypeStruct((2, tall, width), F32)
+    flops = 24 * tall * width * square[1]
+    args = (*x_blocks, *dz_blocks, w_in[0], w_out[0], router)
+    y, dx, din_own, dout_own = expert_call(expert_near_kernel, (both, both, near, near), own, args, 10**7)
+    args = (*x_blocks, *dz_blocks, w_in[1], w_out[1], router, y, dx)
+    outs = (send, keep, send, keep, far, far, jax.ShapeDtypeStruct(router.shape, F32))
+    scratch = (pltpu.VMEM(square, F32), pltpu.VMEM(square, F32))
+    got = expert_call(expert_far_kernel, outs, own, args, flops, scratch)
+    dx_send, dx_keep, y_send, y_keep, din_far, dout_far, drouter = got
+    return dx_send, dx_keep, y_send, y_keep, din_own, din_far, dout_own, dout_far, drouter
 
 
 def make_shards(n_dp):
@@ -482,7 +501,7 @@
         c1 = after((xhat3 * gains[3] + biases[3]).astype(BF), dz, w_exp_out)
         w_out_far = swap(w_exp_out, 2)
         dz = (dz, swap(dz, 1))
-        x = after(to_experts(c1), w_out_far)
+        x = to_experts(c1)
         x = (x, swap(x, 1))
         dx_send, dx_keep, y_send, y_keep, din_own, din_far, dout_own, dout_far, router_part = expert_compute(
             own_dp % experts, x, dz, (w_exp_in, w_in_far), (w_exp_out, w_out_far), w_router
@@ -574,7 +593,7 @@
         exp_in_grads = jnp.transpose(in_got, (1, 2, 3, 0, 4))
         exp_in_grads = exp_in_grads.reshape(experts, rows, n_dp * NF * hid).astype(F32)
         held = jnp.concatenate([dense_sum[:, :width], dense_sum[:, 2 * width : 2 * width + 3 * part]], axis=1)
-        held = exchange(held.reshape(NF, rows, -1), "fsdp").astype(F32)
+        held = deal(held.reshape(NF, rows, -1)).astype(F32)
         mlp_in_grads = held[..., :width].reshape(NF, rows, n_dp, hid)
         mlp_in_grads = jnp.transpose(mlp_in_grads, (1, 2, 0, 3)).reshape(rows, n_dp * NF * hid)
         qkv_grad1 = qkv_layout(held[..., width:])

time: 527 us -> 524 us (level)
  waiting for transfers between devices: 165 us -> 158 us
  Pallas kernels: 73.6 us -> 79.7 us
    ppermute x53 -> x56, waiting for transfers between devices: 140 us -> 118 us  [swap(): return lax.ppermute(value, 'fsdp', [(i, i ^ bits) for i in range(NF)])]
    all_to_all x11 -> x10, waiting for transfers between devices: 22.3 us -> 35.5 us  [exchange(): lax.all_to_all(value, axes, 0, 0, axis_index_groups=groups, tiled=True)]
    all_to_all x11 -> x10, starting transfers between devices: 60 us -> 53.8 us  [exchange(): lax.all_to_all(value, axes, 0, 0, axis_index_groups=groups, tiled=True)]
    pallas_call x1 -> x2, Pallas kernels: 20.7 us -> 26.4 us  [expert_call(): pl.pallas_call(kernel, out_shape=outs, in_specs=[pl.BlockSpec(memory_spac...]
    ppermute x53 -> x56, starting transfers between devices: 53 us -> 54.3 us  [swap(): return lax.ppermute(value, 'fsdp', [(i, i ^ bits) for i in range(NF)])]
    unnamed x201 -> x207, local copies, waits for them, and re-layouts: 22.3 us -> 21.2 us
  transfers between devices with their start and end apart: 68 -> 70, of which waited for: 34 -> 34; matrix products, arithmetic and copies ran while one was open for 20% -> 22% of each run, Pallas kernels for 10% -> 13%
where the time goes in v6:
time: 524 us; the launch traced here: 515 us
  waiting for transfers between devices  158 us (30%)
  starting transfers between devices  117 us (22%)
  Pallas kernels  79.7 us (15%)
  local copies, waits for them, and re-layouts  72.8 us (14%)
  other arithmetic  58 us (11%)
  between operations  16.1 us (3%)
  matrix products  14.2 us (3%)
    ppermute x56, waiting for transfers between devices, swap(): return lax.ppermute(value, 'fsdp', [(i, i ^ bits) for i in range(NF)])  118 us
    ppermute x56, starting transfers between devices, swap(): return lax.ppermute(value, 'fsdp', [(i, i ^ bits) for i in range(NF)])  54.3 us
    all_to_all x10, starting transfers between devices, exchange(): lax.all_to_all(value, axes, 0, 0, axis_index_groups=groups, tiled=True)  53.8 us
    pallas_call x9, Pallas kernels, whole(): pl.pallas_call(kernel, out_shape=outs, in_specs=[space] * len(args), out_...  53.3 us
    all_to_all x10, waiting for transfers between devices, exchange(): lax.all_to_all(value, axes, 0, 0, axis_index_groups=groups, tiled=True)  35.5 us
    pallas_call x2, Pallas kernels, expert_call(): pl.pallas_call(kernel, out_shape=outs, in_specs=[pl.BlockSpec(memory_spac...  26.4 us
    unnamed x207, local copies, waits for them, and re-layouts  21.2 us
    dot_general x6, matrix products, mm_tn(): lax.dot_general(left, right, (((0,), (0,)), ((), ())), preferred_element_...  12.6 us
  transfers between devices with their start and end apart: 70, of which 34 were waited for; matrix products, arithmetic and copies ran while one was open for 22% of the time, Pallas kernels for 13%

profile of v6, /device:TPU:5, one launch (start us, length us, event | category | flops | bytes accessed | tf_op | source)
XLA Modules:
  0.0 515.3 jit_solution(17582578463170158326)
XLA Ops:
  39.2 5.6 %collective-permute-start.6 = (bf16[2,24,768]{2,1,0:T(8,128)(2,1)}, bf16[2,24,768]{2,1,0:T(8,128)(2,1)S(1)}, u32[]{:S(2)}, u32[]{:S(2)}) collective-permute-start(bf16[2,24,768]{2,1,0:T(8,128)(2,1)} %param.23), channel_id=1, source_target_pairs={{0,0},{1,4},{2,8},{3,12},{4,16},{5,20},{6,24},{7,28},{8,1},{9,5},{... | collective-permute-start | bytes 221192 | tf_op jit(solution)/shard_map/ppermute | solution.py:437
  48.8 5.7 %collective-permute-done.8 = bf16[8,24,768]{2,1,0:T(8,128)(2,1)S(1)} collective-permute-done((bf16[8,24,768]{2,1,0:T(8,128)(2,1)}, bf16[8,24,768]{2,1,0:T(8,128)(2,1)S(1)}, u32[]{:S(2)}, u32[]{:S(2)}) %collective-permute-start.8) | collective-permute-done | bytes 294944 | tf_op jit(solution)/shard_map/ppermute | solution.py:57
  60.7 8.2 %all-to-all-start.1 = ((bf16[8,24,768]{2,1,0:T(8,128)(2,1)}), bf16[8,24,768]{2,1,0:T(8,128)(2,1)S(1)}, u32[]{:S(2)}, u32[]{:S(2)}) async-start(bf16[8,24,768]{2,1,0:T(8,128)(2,1)} %broadcast_in_dim.27), calls=%async_computation.1 | async-start | bytes 589824 | tf_op jit(solution)/shard_map/all_to_all | solution.py:99
  74.6 6.2 %shard_map.238 = (bf16[832,576]{1,0:T(8,128)(2,1)S(1)}, bf16[832,192]{1,0:T(8,128)(2,1)S(1)}, f32[3,832]{1,0:T(4,128)S(1)}) custom-call(bf16[832,768]{1,0:T(8,128)(2,1)S(1)} %get-tuple-element.193.refs_0_, bf16[768,704]{1,0:T(8,128)(2,1)S(1)} %bitcast.302, s32[832,1]{1,0:T(8,128)S(1)} %broadcast_in_dim.32.refs_2_.refs_5_.refs_8_, ...), custom_call_target="tpu_custom_call" | custom-call | flops 400000000 | bytes 65536 | tf_op jit(solution)/shard_map/pallas_call | solution.py:233
  90.5 5.6 %all-to-all-start.2 = ((bf16[8,96,1536]{2,1,0:T(8,128)(2,1)}), bf16[8,96,1536]{2,1,0:T(8,128)(2,1)S(1)}, u32[]{:S(2)}, u32[]{:S(2)}) async-start(bf16[8,96,1536]{2,1,0:T(8,128)(2,1)} %pad_maximum_fusion), calls=%async_computation.2 | async-start | bytes 4718592 | tf_op jit(solution)/shard_map/all_to_all | solution.py:99
  124.8 5.9 %collective-permute-done.22 = bf16[208,768]{1,0:T(8,128)(2,1)S(1)} collective-permute-done((bf16[208,768]{1,0:T(8,128)(2,1)S(1)}, bf16[208,768]{1,0:T(8,128)(2,1)S(1)}, u32[]{:S(2)}, u32[]{:S(2)}) %collective-permute-start.22) | collective-permute-done | bytes 319520 | tf_op jit(solution)/shard_map/ppermute | solution.py:57
  132.2 17.0 %all-to-all-done.2 = bf16[8,96,1536]{2,1,0:T(8,128)(2,1)S(1)} async-done(((bf16[8,96,1536]{2,1,0:T(8,128)(2,1)}), bf16[8,96,1536]{2,1,0:T(8,128)(2,1)S(1)}, u32[]{:S(2)}, u32[]{:S(2)}) %all-to-all-start.2) | async-done | bytes 2359328 | tf_op jit(solution)/shard_map/all_to_all | solution.py:99
  159.2 5.5 %collective-permute-done.24.refs_2_ = bf16[208,768]{1,0:T(8,128)(2,1)} collective-permute-done((bf16[208,768]{1,0:T(8,128)(2,1)}, bf16[208,768]{1,0:T(8,128)(2,1)}, u32[]{:S(2)}, u32[]{:S(2)}) %collective-permute-start.24) | collective-permute-done | bytes 319520 | tf_op jit(solution)/shard_map/ppermute | solution.py:57
  171.6 7.5 %shard_map.241 = (bf16[832,576]{1,0:T(8,128)(2,1)S(1)}, bf16[832,192]{1,0:T(8,128)(2,1)S(1)}, f32[3,832]{1,0:T(4,128)S(1)}) custom-call(bf16[208,768]{1,0:T(8,128)(2,1)} %add_convert_fusion.6.refs_0_, bf16[208,768]{1,0:T(8,128)(2,1)} %collective-permute-done.23.refs_1_, bf16[208,768]{1,0:T(8,128)(2,1)} %collective-permute-done.24.refs_2_, ...), custom_call_target="tpu_custom_call" | custom-call | flops 400000000 | bytes 65536 | tf_op jit(solution)/shard_map/pallas_call | solution.py:233
  183.5 11.7 %collective-permute-done.27.refs_5_ = bf16[768,768]{1,0:T(8,128)(2,1)} collective-permute-done((bf16[768,768]{1,0:T(8,128)(2,1)}, bf16[768,768]{1,0:T(8,128)(2,1)}, u32[]{:S(2)}, u32[]{:S(2)}) %collective-permute-start.27) | collective-permute-done | bytes 1179680 | tf_op jit(solution)/shard_map/ppermute | solution.py:57
  195.5 8.0 %collective-permute-done.28 = bf16[208,768]{1,0:T(8,128)(2,1)S(1)} collective-permute-done((bf16[208,768]{1,0:T(8,128)(2,1)S(1)}, bf16[208,768]{1,0:T(8,128)(2,1)S(1)}, u32[]{:S(2)}, u32[]{:S(2)}) %collective-permute-start.28) | collective-permute-done | bytes 319520 | tf_op jit(solution)/shard_map/ppermute | solution.py:57
  209.2 5.6 %all-to-all-start.4 = ((bf16[8,56,768]{2,1,0:T(8,128)(2,1)}), bf16[8,56,768]{2,1,0:T(8,128)(2,1)}, u32[]{:S(2)}, u32[]{:S(2)}) async-start(bf16[8,56,768]{2,1,0:T(8,128)(2,1)} %bitcast.323), calls=%async_computation.4 | async-start | bytes 1376256 | tf_op jit(solution)/shard_map/all_to_all | solution.py:99
  217.7 13.7 %all-to-all-done.4 = bf16[8,56,768]{2,1,0:T(8,128)(2,1)} async-done(((bf16[8,56,768]{2,1,0:T(8,128)(2,1)}), bf16[8,56,768]{2,1,0:T(8,128)(2,1)}, u32[]{:S(2)}, u32[]{:S(2)}) %all-to-all-start.4) | async-done | bytes 688160 | tf_op jit(solution)/shard_map/all_to_all | solution.py:99
  235.5 12.3 %shard_map.243 = (f32[2,448,768]{2,1,0:T(8,128)}, f32[2,448,768]{2,1,0:T(8,128)}, f32[768,768]{1,0:T(8,128)}, f32[768,768]{1,0:T(8,128)}) custom-call(s32[1]{0:T(128)} %bitcast.55.own_ref.refs_0_, bf16[448,768]{1,0:T(8,128)(2,1)} %bitcast.61.x0.refs_1_, bf16[448,768]{1,0:T(8,128)(2,1)} %collective-permute-done.29.x1.refs_2_, bf16[448,768]{1,0:T(8,128)(2,1)} %bitcast.325, ...), custom_call_target="tpu_custom_call" | custom-call | flops 10000000 | bytes 1048576 | tf_op jit(solution)/shard_map/pallas_call | solution.py:357
  247.8 14.1 %shard_map.244 = (bf16[448,768]{1,0:T(8,128)(2,1)}, f32[448,768]{1,0:T(8,128)}, bf16[448,768]{1,0:T(8,128)(2,1)}, f32[448,768]{1,0:T(8,128)}, bf16[768,768]{1,0:...) custom-call(s32[1]{0:T(128)} %bitcast.55.own_ref.refs_0_, bf16[448,768]{1,0:T(8,128)(2,1)} %bitcast.61.x0.refs_1_, ...), custom_call_target="tpu_custom_call" | custom-call | flops 6341787648 | bytes 1048576 | tf_op jit(solution)/shard_map/pallas_call | solution.py:357
  271.3 22.6 %collective-permute-done.34 = bf16[768,768]{1,0:T(8,128)(2,1)S(1)} collective-permute-done((bf16[768,768]{1,0:T(8,128)(2,1)}, bf16[768,768]{1,0:T(8,128)(2,1)S(1)}, u32[]{:S(2)}, u32[]{:S(2)}) %collective-permute-start.34) | collective-permute-done | bytes 1179680 | tf_op jit(solution)/shard_map/ppermute | solution.py:57
  307.1 5.6 %collective-permute-done.37.refs_2_ = bf16[208,768]{1,0:T(8,128)(2,1)S(1)} collective-permute-done((bf16[208,768]{1,0:T(8,128)(2,1)S(1)}, bf16[208,768]{1,0:T(8,128)(2,1)S(1)}, u32[]{:S(2)}, u32[]{:S(2)}) %collective-permute-start.37) | collective-permute-done | bytes 319520 | tf_op jit(solution)/shard_map/ppermute | solution.py:57
  316.7 10.8 %shard_map.245 = (bf16[832,576]{1,0:T(8,128)(2,1)S(1)}, bf16[2,208,768]{2,1,0:T(8,128)(2,1)S(1)}, f32[2,208,768]{2,1,0:T(8,128)S(1)}) custom-call(bf16[208,768]{1,0:T(8,128)(2,1)S(1)} %get-tuple-element.185.refs_0_, bf16[208,768]{1,0:T(8,128)(2,1)S(1)} %collective-permute-done.36.refs_1_, bf16[208,768]{1,0:T(8,128)(2,1)S(1)} %collective-permute-done.37.refs_2_, ...), custom_call_target="tpu_custom_call" | custom-call | flops 11000000512 | bytes 65536 | tf_op jit(solution)/shard_map/pallas_call | solution.py:233
  345.3 5.6 %all-to-all-start.7 = ((bf16[8,152,768]{2,1,0:T(8,128)(2,1)}), bf16[8,152,768]{2,1,0:T(8,128)(2,1)}, u32[]{:S(2)}, u32[]{:S(2)}) async-start(bf16[8,152,768]{2,1,0:T(8,128)(2,1)} %pad_maximum_fusion.2), calls=%async_computation.7 | async-start | bytes 3735552 | tf_op jit(solution)/shard_map/all_to_all | solution.py:99
  378.3 6.0 %shard_map.247 = bf16[8,96,2304]{2,1,0:T(8,128)(2,1)} custom-call(bf16[208,768]{1,0:T(8,128)(2,1)S(1)} %copy-done.8, bf16[208,768]{1,0:T(8,128)(2,1)S(1)} %copy-done.11, bf16[208,768]{1,0:T(8,128)(2,1)} %collective-permute-done.16.refs_2_, bf16[208,768]{1,0:T(8,128)(2,1)} %collective-permute-done.17.refs_3_, ...), custom_call_target="tpu_custom_call" | custom-call | flops 100000000 | bytes 65536 | tf_op jit(solution)/shard_map/pallas_call | solution.py:233
  395.6 5.5 %collective-permute-done.47.refs_2_ = bf16[208,768]{1,0:T(8,128)(2,1)S(1)} collective-permute-done((bf16[208,768]{1,0:T(8,128)(2,1)S(1)}, bf16[208,768]{1,0:T(8,128)(2,1)S(1)}, u32[]{:S(2)}, u32[]{:S(2)}) %collective-permute-start.47) | collective-permute-done | bytes 319520 | tf_op jit(solution)/shard_map/ppermute | solution.py:57
  418.5 11.2 %shard_map.248 = (bf16[832,576]{1,0:T(8,128)(2,1)S(1)}, bf16[2,208,768]{2,1,0:T(8,128)(2,1)S(1)}, f32[2,208,768]{2,1,0:T(8,128)}) custom-call(bf16[208,768]{1,0:T(8,128)(2,1)S(1)} %get-tuple-element.111.refs_0_, bf16[208,768]{1,0:T(8,128)(2,1)S(1)} %collective-permute-done.46.refs_1_, bf16[208,768]{1,0:T(8,128)(2,1)S(1)} %collective-permute-done.47.refs_2_, ...), custom_call_target="tpu_custom_call" | custom-call | flops 11000000512 | bytes 65536 | tf_op jit(solution)/shard_map/pallas_call | solution.py:233
  451.8 10.4 %collective-permute-done.55 = bf16[8,24,768]{2,1,0:T(8,128)(2,1)S(1)} collective-permute-done((bf16[8,24,768]{2,1,0:T(8,128)(2,1)S(1)}, bf16[8,24,768]{2,1,0:T(8,128)(2,1)S(1)}, u32[]{:S(2)}, u32[]{:S(2)}) %collective-permute-start.55) | collective-permute-done | bytes 294944 | tf_op jit(solution)/shard_map/ppermute | solution.py:57
  462.2 5.9 %collective-permute-done.56 = bf16[8,24,768]{2,1,0:T(8,128)(2,1)S(1)} collective-permute-done((bf16[8,24,768]{2,1,0:T(8,128)(2,1)S(1)}, bf16[8,24,768]{2,1,0:T(8,128)(2,1)S(1)}, u32[]{:S(2)}, u32[]{:S(2)}) %collective-permute-start.56) | collective-permute-done | bytes 294944 | tf_op jit(solution)/shard_map/ppermute | solution.py:57
  (507 shorter events, 283.1 us)
Async XLA Ops:
  7.2 49.3 %collective-permute-start.1 = (bf16[208,768]{1,0:T(8,128)(2,1)}, bf16[208,768]{1,0:T(8,128)(2,1)S(1)}, u32[]{:S(2)}, u32[]{:S(2)}) collective-permute-start(bf16[208,768]{1,0:T(8,128)(2,1)} %bitcast.306), channel_id=1, source_target_pairs={{0,2},{1,3},{2,0},{3,1},{4,6},{5,7},{6,4},{7,5},{8,10},{9,11},{10,... | collective-permute-start | bytes 958472 | tf_op jit(solution)/shard_map/ppermute | solution.py:57
  8.5 50.7 %collective-permute-start = (bf16[208,768]{1,0:T(8,128)(2,1)}, bf16[208,768]{1,0:T(8,128)(2,1)S(1)}, u32[]{:S(2)}, u32[]{:S(2)}) collective-permute-start(bf16[208,768]{1,0:T(8,128)(2,1)} %bitcast.307), channel_id=1, source_target_pairs={{0,1},{1,0},{2,3},{3,2},{4,5},{5,4},{6,7},{7,6},{8,9},{9,8},{10,11... | collective-permute-start | bytes 958472 | tf_op jit(solution)/shard_map/ppermute | solution.py:57
  10.1 20.0 %collective-permute-start.4 = (s32[208]{0:T(256)S(1)}, s32[208]{0:T(256)S(1)}, u32[]{:S(2)}, u32[]{:S(2)}) collective-permute-start(s32[208]{0:T(256)S(1)} %bitcast.351), channel_id=1, source_target_pairs={{0,2},{1,3},{2,0},{3,1},{4,6},{5,7},{6,4},{7,5},{8,10},{9,11},{10,... | collective-permute-start | bytes 2504 | tf_op jit(solution)/shard_map/ppermute | solution.py:57
  10.4 20.2 %collective-permute-start.3 = (s32[208]{0:T(256)S(1)}, s32[208]{0:T(256)}, u32[]{:S(2)}, u32[]{:S(2)}) collective-permute-start(s32[208]{0:T(256)S(1)} %bitcast.352), channel_id=1, source_target_pairs={{0,1},{1,0},{2,3},{3,2},{4,5},{5,4},{6,7},{7,6},{8,9},{9,8},{10,11... | collective-permute-start | bytes 2504 | tf_op jit(solution)/shard_map/ppermute | solution.py:57
  12.7 20.4 %collective-permute-start.10 = (bf16[24,576]{1,0:T(8,128)(2,1)}, bf16[24,576]{1,0:T(8,128)(2,1)S(1)}, u32[]{:S(2)}, u32[]{:S(2)}) collective-permute-start(bf16[24,576]{1,0:T(8,128)(2,1)} %get-tuple-element.237), channel_id=1, source_target_pairs={{0,3},{1,2},{2,1},{3,0},{4,7},{5,6},{6,5},{7,4},{8,11},{9,10},{10,... | collective-permute-start | bytes 82952 | tf_op jit(solution)/shard_map/ppermute | solution.py:57
  16.1 43.9 %all-to-all-start = ((bf16[32,24,704]{2,1,0:T(8,128)(2,1)}), bf16[32,24,704]{2,1,0:T(8,128)(2,1)S(1)}, u32[]{:S(2)}, u32[]{:S(2)}) async-start(bf16[32,24,704]{2,1,0:T(8,128)(2,1)} %bitcast.4), calls=%async_computation | async-start | bytes 2359296 | tf_op jit(solution)/shard_map/all_to_all | solution.py:99
  21.2 90.1 %all-gather.3.cloned.1.call-start = ((), (), s32[]{:S(2)}) async-start(), calls=%async_computation.12 | async-start | bytes 2654208 | tf_op jit(solution)/shard_map/all_gather | solution.py:433
  60.7 22.7 %all-to-all-start.1 = ((bf16[8,24,768]{2,1,0:T(8,128)(2,1)}), bf16[8,24,768]{2,1,0:T(8,128)(2,1)S(1)}, u32[]{:S(2)}, u32[]{:S(2)}) async-start(bf16[8,24,768]{2,1,0:T(8,128)(2,1)} %broadcast_in_dim.27), calls=%async_computation.1 | async-start | bytes 589824 | tf_op jit(solution)/shard_map/all_to_all | solution.py:99
  90.5 58.7 %all-to-all-start.2 = ((bf16[8,96,1536]{2,1,0:T(8,128)(2,1)}), bf16[8,96,1536]{2,1,0:T(8,128)(2,1)S(1)}, u32[]{:S(2)}, u32[]{:S(2)}) async-start(bf16[8,96,1536]{2,1,0:T(8,128)(2,1)} %pad_maximum_fusion), calls=%async_computation.2 | async-start | bytes 4718592 | tf_op jit(solution)/shard_map/all_to_all | solution.py:99
  150.4 53.7 %all-to-all-start.3 = ((bf16[8,152,768]{2,1,0:T(8,128)(2,1)}), bf16[8,152,768]{2,1,0:T(8,128)(2,1)}, u32[]{:S(2)}, u32[]{:S(2)}) async-start(bf16[8,152,768]{2,1,0:T(8,128)(2,1)} %pad_maximum_fusion.1), calls=%async_computation.3 | async-start | bytes 3735552 | tf_op jit(solution)/shard_map/all_to_all | solution.py:99
  167.2 27.9 %collective-permute-start.27 = (bf16[768,768]{1,0:T(8,128)(2,1)}, bf16[768,768]{1,0:T(8,128)(2,1)}, u32[]{:S(2)}, u32[]{:S(2)}) collective-permute-start(bf16[768,768]{1,0:T(8,128)(2,1)} %slice.296.in_ref), channel_id=1, source_target_pairs={{0,2},{1,3},{2,0},{3,1},{4,6},{5,7},{6,4},{7,5},{8,10},{9,11},{10,... | collective-permute-start | bytes 3538952 | tf_op jit(solution)/shard_map/ppermute | solution.py:57
  209.2 22.3 %all-to-all-start.4 = ((bf16[8,56,768]{2,1,0:T(8,128)(2,1)}), bf16[8,56,768]{2,1,0:T(8,128)(2,1)}, u32[]{:S(2)}, u32[]{:S(2)}) async-start(bf16[8,56,768]{2,1,0:T(8,128)(2,1)} %bitcast.323), calls=%async_computation.4 | async-start | bytes 1376256 | tf_op jit(solution)/shard_map/all_to_all | solution.py:99
  214.8 33.0 %collective-permute-start.31 = (bf16[768,768]{1,0:T(8,128)(2,1)S(1)}, bf16[768,768]{1,0:T(8,128)(2,1)}, u32[]{:S(2)}, u32[]{:S(2)}) collective-permute-start(bf16[768,768]{1,0:T(8,128)(2,1)S(1)} %bitcast.316), channel_id=1, source_target_pairs={{0,2},{1,3},{2,0},{3,1},{4,6},{5,7},{6,4},{7,5},{8,10},{9,11},{10,... | collective-permute-start | bytes 3538952 | tf_op jit(solution)/shard_map/ppermute | solution.py:57
  266.6 27.4 %collective-permute-start.34 = (bf16[768,768]{1,0:T(8,128)(2,1)}, bf16[768,768]{1,0:T(8,128)(2,1)S(1)}, u32[]{:S(2)}, u32[]{:S(2)}) collective-permute-start(bf16[768,768]{1,0:T(8,128)(2,1)} %get-tuple-element.93), channel_id=1, source_target_pairs={{0,2},{1,3},{2,0},{3,1},{4,6},{5,7},{6,4},{7,5},{8,10},{9,11},{10,... | collective-permute-start | bytes 3538952 | tf_op jit(solution)/shard_map/ppermute | solution.py:57
  266.9 30.0 %all-to-all-start.5 = ((bf16[8,56,768]{2,1,0:T(8,128)(2,1)}), bf16[8,56,768]{2,1,0:T(8,128)(2,1)}, u32[]{:S(2)}, u32[]{:S(2)}) async-start(bf16[8,56,768]{2,1,0:T(8,128)(2,1)} %bitcast.65), calls=%async_computation.5 | async-start | bytes 1376256 | tf_op jit(solution)/shard_map/all_to_all | solution.py:99
  299.2 32.4 %all-to-all-start.6 = ((bf16[8,96,768]{2,1,0:T(8,128)(2,1)}), bf16[8,96,768]{2,1,0:T(8,128)(2,1)}, u32[]{:S(2)}, u32[]{:S(2)}) async-start(bf16[8,96,768]{2,1,0:T(8,128)(2,1)} %bitcast.64), calls=%async_computation.6 | async-start | bytes 2359296 | tf_op jit(solution)/shard_map/all_to_all | solution.py:99
  315.0 27.3 %collective-permute-start.35 = (bf16[768,768]{1,0:T(8,128)(2,1)}, bf16[768,768]{1,0:T(8,128)(2,1)}, u32[]{:S(2)}, u32[]{:S(2)}) collective-permute-start(bf16[768,768]{1,0:T(8,128)(2,1)} %get-tuple-element.94), channel_id=1, source_target_pairs={{0,2},{1,3},{2,0},{3,1},{4,6},{5,7},{6,4},{7,5},{8,10},{9,11},{10,... | collective-permute-start | bytes 3538952 | tf_op jit(solution)/shard_map/ppermute | solution.py:57
  345.3 48.2 %all-to-all-start.7 = ((bf16[8,152,768]{2,1,0:T(8,128)(2,1)}), bf16[8,152,768]{2,1,0:T(8,128)(2,1)}, u32[]{:S(2)}, u32[]{:S(2)}) async-start(bf16[8,152,768]{2,1,0:T(8,128)(2,1)} %pad_maximum_fusion.2), calls=%async_computation.7 | async-start | bytes 3735552 | tf_op jit(solution)/shard_map/all_to_all | solution.py:99
  350.9 139.4 %reduce-scatter.2.cloned.1.call-start = ((), (), s32[]{:S(2)}) async-start(), calls=%async_computation.11 | async-start | bytes 3981312 | tf_op jit(solution)/shard_map/reduce_scatter | solution.py:564
  412.4 24.2 %all-to-all-start.8 = ((bf16[8,24,768]{2,1,0:T(8,128)(2,1)}), bf16[8,24,768]{2,1,0:T(8,128)(2,1)}, u32[]{:S(2)}, u32[]{:S(2)}) async-start(bf16[8,24,768]{2,1,0:T(8,128)(2,1)} %bitcast.340), calls=%async_computation.8 | async-start | bytes 589824 | tf_op jit(solution)/shard_map/all_to_all | solution.py:99
  438.0 47.3 %all-to-all-start.9 = ((bf16[32,24,704]{2,1,0:T(8,128)(2,1)}), bf16[32,24,704]{2,1,0:T(8,128)(2,1)}, u32[]{:S(2)}, u32[]{:S(2)}) async-start(bf16[32,24,704]{2,1,0:T(8,128)(2,1)} %bitcast.314), calls=%async_computation.9 | async-start | bytes 2359296 | tf_op jit(solution)/shard_map/all_to_all | solution.py:99
  447.0 21.0 %collective-permute-start.56 = (bf16[8,24,768]{2,1,0:T(8,128)(2,1)S(1)}, bf16[8,24,768]{2,1,0:T(8,128)(2,1)S(1)}, u32[]{:S(2)}, u32[]{:S(2)}) collective-permute-start(bf16[8,24,768]{2,1,0:T(8,128)(2,1)S(1)} %get-tuple-element.205), channel_id=1, source_target_pairs={{0,2},{1,3},{2,0},{3,1},{4,6},{5,7},{6,4},{7,5},{8,10},{9,11},{10,... | collective-permute-start | bytes 884744 | tf_op jit(solution)/shard_map/ppermute | solution.py:57
  447.3 20.8 %collective-permute-start.57 = (bf16[8,24,768]{2,1,0:T(8,128)(2,1)S(1)}, bf16[8,24,768]{2,1,0:T(8,128)(2,1)S(1)}, u32[]{:S(2)}, u32[]{:S(2)}) collective-permute-start(bf16[8,24,768]{2,1,0:T(8,128)(2,1)S(1)} %get-tuple-element.204), channel_id=1, source_target_pairs={{0,1},{1,0},{2,3},{3,2},{4,5},{5,4},{6,7},{7,6},{8,9},{9,8},{10,11... | collective-permute-start | bytes 884744 | tf_op jit(solution)/shard_map/ppermute | solution.py:57
  450.6 30.8 %collective-permute-start.50 = (bf16[208,768]{1,0:T(8,128)(2,1)}, bf16[208,768]{1,0:T(8,128)(2,1)S(1)}, u32[]{:S(2)}, u32[]{:S(2)}) collective-permute-start(bf16[208,768]{1,0:T(8,128)(2,1)} %get-tuple-element.203), channel_id=1, source_target_pairs={{0,2},{1,3},{2,0},{3,1},{4,6},{5,7},{6,4},{7,5},{8,10},{9,11},{10,... | collective-permute-start | bytes 958472 | tf_op jit(solution)/shard_map/ppermute | solution.py:57
  (147 other events, 996.0 us)
Sparse Core Ops, SparseCore 0:
  46.7 51.4 all-gather.2
  384.5 100.0 reduce-scatter.1

commit v7 on v6

--- a/solution.py
+++ b/solution.py
@@ -415,15 +415,15 @@
             return jnp.transpose(weight, (2, 0, 1, 3)).reshape(NF, rows, 3 * part)
 
         small = jnp.concatenate(
-            [norm_gains.T, norm_biases.T, router, jnp.zeros((rows, 128 - 8 - experts), BF)], axis=1
+            [norm_gains.T, norm_biases.T, router, jnp.zeros((rows, 64 - 8 - experts), BF)], axis=1
         )
-        small = jnp.broadcast_to(small[None], (NF, rows, 128))
+        small = jnp.broadcast_to(small[None], (NF, rows, 64))
         def to_everyone(blocks):
             full = jnp.broadcast_to(blocks[None], (n_dp,) + blocks.shape)
             return exchange(full.reshape((n_all, rows, -1)), ALL).reshape(width, -1)
 
-        first = to_everyone(jnp.concatenate([small, qkv_block(0)], axis=2))
-        small_all, w_qkv0 = first[:, :128], (first, slice(128, 128 + 3 * part))
+        first = to_everyone(jnp.concatenate([qkv_block(0), small], axis=2))
+        small_all, w_qkv0 = first[:, 3 * part :], (first, slice(0, 3 * part))
         norms = small_all[:, :8].T.astype(F32)
         gains, biases = norms[:4], norms[4:]
         w_router = small_all[:, 8 : 8 + experts]
@@ -581,12 +581,12 @@
             gain0, bias0 = gain0 + block_gain, bias0 + block_bias
         columns = jnp.stack([gain0, gain1, gain2, gain3, bias0, bias1, bias2, bias3], axis=1)
         columns = jnp.concatenate(
-            [columns, router_part, jnp.zeros((width, 128 - 8 - experts), F32), qkv_part0], axis=1
+            [qkv_part0, columns, router_part, jnp.zeros((width, 64 - 8 - experts), F32)], axis=1
         )
         tail = rows_to_owners(after(columns, out_got0))
         total = jnp.sum(tail, axis=0)
-        small_grads = jnp.sum(total[:, :, :128], axis=0)
-        qkv_grad0 = qkv_layout(total[:, :, 128:])
+        small_grads = jnp.sum(total[:, :, 3 * part :], axis=0)
+        qkv_grad0 = qkv_layout(total[:, :, : 3 * part])
         dense_sum = after(dense_sum, tail)
         in_got = jnp.swapaxes(after(in_got, dqkv0).reshape(experts, NF, rows, n_dp * hid), 0, 1)
         in_got = deal(in_got).reshape(NF, experts, rows, n_dp, hid)

time: 524 us -> 520 us (level)
  starting transfers between devices: 117 us -> 128 us
  waiting for transfers between devices: 158 us -> 151 us
    ppermute x56, waiting for transfers between devices: 118 us -> 92.8 us  [swap(): return lax.ppermute(value, 'fsdp', [(i, i ^ bits) for i in range(NF)])]
    all_to_all x10, waiting for transfers between devices: 35.5 us -> 49.4 us  [exchange(): lax.all_to_all(value, axes, 0, 0, axis_index_groups=groups, tiled=True)]
    ppermute x56, starting transfers between devices: 54.3 us -> 64 us  [swap(): return lax.ppermute(value, 'fsdp', [(i, i ^ bits) for i in range(NF)])]
    unnamed x207 -> x169, local copies, waits for them, and re-layouts: 21.2 us -> 19.9 us
  transfers between devices with their start and end apart: 70 -> 70, of which waited for: 34 -> 29; matrix products, arithmetic and copies ran while one was open for 22% -> 21% of each run, Pallas kernels for 13% -> 12%
where the time goes in v7:
time: 520 us; the launch traced here: 511 us
  waiting for transfers between devices  151 us (29%)
  starting transfers between devices  128 us (25%)
  Pallas kernels  77.5 us (15%)
  local copies, waits for them, and re-layouts  72.6 us (14%)
  other arithmetic  53.4 us (10%)
  between operations  15.9 us (3%)
  matrix products  13.4 us (3%)
    ppermute x56, waiting for transfers between devices, swap(): return lax.ppermute(value, 'fsdp', [(i, i ^ bits) for i in range(NF)])  92.8 us
    ppermute x56, starting transfers between devices, swap(): return lax.ppermute(value, 'fsdp', [(i, i ^ bits) for i in range(NF)])  64 us
    all_to_all x10, starting transfers between devices, exchange(): lax.all_to_all(value, axes, 0, 0, axis_index_groups=groups, tiled=True)  55.6 us
    pallas_call x9, Pallas kernels, whole(): pl.pallas_call(kernel, out_shape=outs, in_specs=[space] * len(args), out_...  51.6 us
    all_to_all x10, waiting for transfers between devices, exchange(): lax.all_to_all(value, axes, 0, 0, axis_index_groups=groups, tiled=True)  49.4 us
    pallas_call x2, Pallas kernels, expert_call(): pl.pallas_call(kernel, out_shape=outs, in_specs=[pl.BlockSpec(memory_spac...  25.9 us
    unnamed x169, local copies, waits for them, and re-layouts  19.9 us
    dot_general x6, matrix products, mm_tn(): lax.dot_general(left, right, (((0,), (0,)), ((), ())), preferred_element_...  11.9 us
  transfers between devices with their start and end apart: 70, of which 29 were waited for; matrix products, arithmetic and copies ran while one was open for 21% of the time, Pallas kernels for 12%

profile of v7, /device:TPU:5, one launch (start us, length us, event | category | flops | bytes accessed | tf_op | source)
XLA Modules:
  0.0 511.5 jit_solution(15021606187689517983)
XLA Ops:
  15.5 5.2 %all-to-all-start = ((bf16[32,24,640]{2,1,0:T(8,128)(2,1)}), bf16[32,24,640]{2,1,0:T(8,128)(2,1)S(1)}, u32[]{:S(2)}, u32[]{:S(2)}) async-start(bf16[32,24,640]{2,1,0:T(8,128)(2,1)} %bitcast.4), calls=%async_computation | async-start | bytes 1966080 | tf_op jit(solution)/shard_map/all_to_all | solution.py:99
  38.1 5.7 %collective-permute-start.6 = (bf16[2,24,768]{2,1,0:T(8,128)(2,1)}, bf16[2,24,768]{2,1,0:T(8,128)(2,1)S(1)}, u32[]{:S(2)}, u32[]{:S(2)}) collective-permute-start(bf16[2,24,768]{2,1,0:T(8,128)(2,1)} %param.23), channel_id=1, source_target_pairs={{0,0},{1,4},{2,8},{3,12},{4,16},{5,20},{6,24},{7,28},{8,1},{9,5},{... | collective-permute-start | bytes 221192 | tf_op jit(solution)/shard_map/ppermute | solution.py:437
  59.8 8.7 %all-to-all-start.1 = ((bf16[8,24,768]{2,1,0:T(8,128)(2,1)}), bf16[8,24,768]{2,1,0:T(8,128)(2,1)S(1)}, u32[]{:S(2)}, u32[]{:S(2)}) async-start(bf16[8,24,768]{2,1,0:T(8,128)(2,1)} %broadcast_in_dim.27), calls=%async_computation.1 | async-start | bytes 589824 | tf_op jit(solution)/shard_map/all_to_all | solution.py:99
  73.8 6.1 %shard_map.238 = (bf16[832,576]{1,0:T(8,128)(2,1)S(1)}, bf16[832,192]{1,0:T(8,128)(2,1)S(1)}, f32[3,832]{1,0:T(4,128)S(1)}) custom-call(bf16[832,768]{1,0:T(8,128)(2,1)S(1)} %get-tuple-element.193.refs_0_, bf16[768,640]{1,0:T(8,128)(2,1)S(1)} %bitcast.303, s32[832,1]{1,0:T(8,128)S(1)} %broadcast_in_dim.32.refs_2_.refs_5_.refs_8_, ...), custom_call_target="tpu_custom_call" | custom-call | flops 400000000 | bytes 65536 | tf_op jit(solution)/shard_map/pallas_call | solution.py:233
  88.4 5.8 %all-to-all-start.2 = ((bf16[8,96,1536]{2,1,0:T(8,128)(2,1)}), bf16[8,96,1536]{2,1,0:T(8,128)(2,1)S(1)}, u32[]{:S(2)}, u32[]{:S(2)}) async-start(bf16[8,96,1536]{2,1,0:T(8,128)(2,1)} %pad_maximum_fusion), calls=%async_computation.2 | async-start | bytes 4718592 | tf_op jit(solution)/shard_map/all_to_all | solution.py:99
  115.1 5.2 %shard_map.240 = (f32[4,208,768]{2,1,0:T(8,128)}, bf16[4,208,768]{2,1,0:T(8,128)(2,1)S(1)}, bf16[2,208,768]{2,1,0:T(8,128)(2,1)S(1)}, f32[2,208,768]{2,1,0:T(8,128)S(1)}) custom-call(bf16[208,768]{1,0:T(8,128)(2,1)S(1)} %copy-done.7, bf16[208,768]{1,0:T(8,128)(2,1)S(1)} %copy-done.13, bf16[208,768]{1,0:T(8,128)(2,1)S(1)} %copy-done.10, ...), custom_call_target="tpu_custom_call" | custom-call | flops 300000000 | bytes 65536 | tf_op jit(solution)/shard_map/pallas_call | solution.py:233
  125.1 6.5 %collective-permute-done.22 = bf16[208,768]{1,0:T(8,128)(2,1)S(1)} collective-permute-done((bf16[208,768]{1,0:T(8,128)(2,1)S(1)}, bf16[208,768]{1,0:T(8,128)(2,1)S(1)}, u32[]{:S(2)}, u32[]{:S(2)}) %collective-permute-start.22) | collective-permute-done | bytes 319520 | tf_op jit(solution)/shard_map/ppermute | solution.py:57
  132.7 14.6 %all-to-all-done.2 = bf16[8,96,1536]{2,1,0:T(8,128)(2,1)S(1)} async-done(((bf16[8,96,1536]{2,1,0:T(8,128)(2,1)}), bf16[8,96,1536]{2,1,0:T(8,128)(2,1)S(1)}, u32[]{:S(2)}, u32[]{:S(2)}) %all-to-all-start.2) | async-done | bytes 2359328 | tf_op jit(solution)/shard_map/all_to_all | solution.py:99
  170.6 7.4 %shard_map.241 = (bf16[832,576]{1,0:T(8,128)(2,1)S(1)}, bf16[832,192]{1,0:T(8,128)(2,1)S(1)}, f32[3,832]{1,0:T(4,128)S(1)}) custom-call(bf16[208,768]{1,0:T(8,128)(2,1)} %add_convert_fusion.6.refs_0_, bf16[208,768]{1,0:T(8,128)(2,1)} %collective-permute-done.23.refs_1_, bf16[208,768]{1,0:T(8,128)(2,1)} %collective-permute-done.24.refs_2_, ...), custom_call_target="tpu_custom_call" | custom-call | flops 400000000 | bytes 65536 | tf_op jit(solution)/shard_map/pallas_call | solution.py:233
  181.8 11.4 %collective-permute-done.27.refs_5_ = bf16[768,768]{1,0:T(8,128)(2,1)} collective-permute-done((bf16[768,768]{1,0:T(8,128)(2,1)}, bf16[768,768]{1,0:T(8,128)(2,1)}, u32[]{:S(2)}, u32[]{:S(2)}) %collective-permute-start.27) | collective-permute-done | bytes 1179680 | tf_op jit(solution)/shard_map/ppermute | solution.py:57
  194.5 7.0 %collective-permute-done.28 = bf16[208,768]{1,0:T(8,128)(2,1)S(1)} collective-permute-done((bf16[208,768]{1,0:T(8,128)(2,1)S(1)}, bf16[208,768]{1,0:T(8,128)(2,1)S(1)}, u32[]{:S(2)}, u32[]{:S(2)}) %collective-permute-start.28) | collective-permute-done | bytes 319520 | tf_op jit(solution)/shard_map/ppermute | solution.py:57
  207.2 5.6 %all-to-all-start.4 = ((bf16[8,56,768]{2,1,0:T(8,128)(2,1)}), bf16[8,56,768]{2,1,0:T(8,128)(2,1)}, u32[]{:S(2)}, u32[]{:S(2)}) async-start(bf16[8,56,768]{2,1,0:T(8,128)(2,1)} %bitcast.323), calls=%async_computation.4 | async-start | bytes 1376256 | tf_op jit(solution)/shard_map/all_to_all | solution.py:99
  216.6 12.8 %all-to-all-done.4 = bf16[8,56,768]{2,1,0:T(8,128)(2,1)} async-done(((bf16[8,56,768]{2,1,0:T(8,128)(2,1)}), bf16[8,56,768]{2,1,0:T(8,128)(2,1)}, u32[]{:S(2)}, u32[]{:S(2)}) %all-to-all-start.4) | async-done | bytes 688160 | tf_op jit(solution)/shard_map/all_to_all | solution.py:99
  233.5 12.3 %shard_map.243 = (f32[2,448,768]{2,1,0:T(8,128)}, f32[2,448,768]{2,1,0:T(8,128)}, f32[768,768]{1,0:T(8,128)}, f32[768,768]{1,0:T(8,128)}) custom-call(s32[1]{0:T(128)} %bitcast.55.own_ref.refs_0_, bf16[448,768]{1,0:T(8,128)(2,1)} %bitcast.61.x0.refs_1_, bf16[448,768]{1,0:T(8,128)(2,1)} %collective-permute-done.29.x1.refs_2_, bf16[448,768]{1,0:T(8,128)(2,1)} %bitcast.325, ...), custom_call_target="tpu_custom_call" | custom-call | flops 10000000 | bytes 1048576 | tf_op jit(solution)/shard_map/pallas_call | solution.py:357
  245.8 13.6 %shard_map.244 = (bf16[448,768]{1,0:T(8,128)(2,1)}, f32[448,768]{1,0:T(8,128)}, bf16[448,768]{1,0:T(8,128)(2,1)}, f32[448,768]{1,0:T(8,128)}, bf16[768,768]{1,0:...) custom-call(s32[1]{0:T(128)} %bitcast.55.own_ref.refs_0_, bf16[448,768]{1,0:T(8,128)(2,1)} %bitcast.61.x0.refs_1_, ...), custom_call_target="tpu_custom_call" | custom-call | flops 6341787648 | bytes 1048576 | tf_op jit(solution)/shard_map/pallas_call | solution.py:357
  269.8 21.8 %collective-permute-done.34 = bf16[768,768]{1,0:T(8,128)(2,1)S(1)} collective-permute-done((bf16[768,768]{1,0:T(8,128)(2,1)}, bf16[768,768]{1,0:T(8,128)(2,1)S(1)}, u32[]{:S(2)}, u32[]{:S(2)}) %collective-permute-start.34) | collective-permute-done | bytes 1179680 | tf_op jit(solution)/shard_map/ppermute | solution.py:57
  314.5 10.7 %shard_map.245 = (bf16[832,576]{1,0:T(8,128)(2,1)S(1)}, bf16[2,208,768]{2,1,0:T(8,128)(2,1)S(1)}, f32[2,208,768]{2,1,0:T(8,128)S(1)}) custom-call(bf16[208,768]{1,0:T(8,128)(2,1)S(1)} %get-tuple-element.185.refs_0_, bf16[208,768]{1,0:T(8,128)(2,1)S(1)} %collective-permute-done.36.refs_1_, bf16[208,768]{1,0:T(8,128)(2,1)S(1)} %collective-permute-done.37.refs_2_, ...), custom_call_target="tpu_custom_call" | custom-call | flops 11000000512 | bytes 65536 | tf_op jit(solution)/shard_map/pallas_call | solution.py:233
  342.8 5.5 %all-to-all-start.7 = ((bf16[8,152,768]{2,1,0:T(8,128)(2,1)}), bf16[8,152,768]{2,1,0:T(8,128)(2,1)}, u32[]{:S(2)}, u32[]{:S(2)}) async-start(bf16[8,152,768]{2,1,0:T(8,128)(2,1)} %pad_maximum_fusion.2), calls=%async_computation.7 | async-start | bytes 3735552 | tf_op jit(solution)/shard_map/all_to_all | solution.py:99
  366.9 5.3 %shard_map.246 = (bf16[4,208,768]{2,1,0:T(8,128)(2,1)S(1)}, bf16[2,208,768]{2,1,0:T(8,128)(2,1)S(1)}, f32[2,208,768]{2,1,0:T(8,128)S(1)}) custom-call(bf16[208,768]{1,0:T(8,128)(2,1)S(1)} %get-tuple-element.182.refs_0_.refs_4_, bf16[208,768]{1,0:T(8,128)(2,1)S(1)} %collective-permute-done.41.refs_1_.refs_5_, ...), custom_call_target="tpu_custom_call" | custom-call | flops 100000000 | bytes 65536 | tf_op jit(solution)/shard_map/pallas_call | solution.py:233
  376.1 5.8 %shard_map.247 = bf16[8,96,2304]{2,1,0:T(8,128)(2,1)} custom-call(bf16[208,768]{1,0:T(8,128)(2,1)S(1)} %copy-done.8, bf16[208,768]{1,0:T(8,128)(2,1)S(1)} %copy-done.14, bf16[208,768]{1,0:T(8,128)(2,1)S(1)} %copy-done.11, bf16[208,768]{1,0:T(8,128)(2,1)S(1)} %copy-done.17, bf16[208,768]{1,0:T(8,128)(2,1)S(1)} %get-tuple-element.182.refs_0_.refs_4_, ...), custom_call_target="tpu_custom_call" | custom-call | flops 100000000 | bytes 65536 | tf_op jit(solution)/shard_map/pallas_call | solution.py:233
  404.5 10.2 %shard_map.248 = (bf16[832,576]{1,0:T(8,128)(2,1)S(1)}, bf16[2,208,768]{2,1,0:T(8,128)(2,1)S(1)}, f32[2,208,768]{2,1,0:T(8,128)}) custom-call(bf16[208,768]{1,0:T(8,128)(2,1)S(1)} %get-tuple-element.111.refs_0_, bf16[208,768]{1,0:T(8,128)(2,1)S(1)} %collective-permute-done.46.refs_1_, bf16[208,768]{1,0:T(8,128)(2,1)S(1)} %collective-permute-done.47.refs_2_, ...), custom_call_target="tpu_custom_call" | custom-call | flops 11000000512 | bytes 65536 | tf_op jit(solution)/shard_map/pallas_call | solution.py:233
  437.4 6.1 %all-to-all-start.9 = ((bf16[32,24,640]{2,1,0:T(8,128)(2,1)}), bf16[32,24,640]{2,1,0:T(8,128)(2,1)}, u32[]{:S(2)}, u32[]{:S(2)}) async-start(bf16[32,24,640]{2,1,0:T(8,128)(2,1)} %bitcast.82), calls=%async_computation.9 | async-start | bytes 1966080 | tf_op jit(solution)/shard_map/all_to_all | solution.py:99
  456.7 5.2 %reshape.412 = f32[8,24,3072]{2,1,0:T(8,128)} reshape(f32[8,24,8,4,96]{4,3,2,1,0:T(4,128)} %copy.130) | data formatting | bytes 4718592 | tf_op jit(solution)/shard_map/convert_element_type | solution.py:594
  464.7 16.8 %all-to-all-done.9 = bf16[32,24,640]{2,1,0:T(8,128)(2,1)} async-done(((bf16[32,24,640]{2,1,0:T(8,128)(2,1)}), bf16[32,24,640]{2,1,0:T(8,128)(2,1)}, u32[]{:S(2)}, u32[]{:S(2)}) %all-to-all-start.9) | async-done | bytes 983072 | tf_op jit(solution)/shard_map/all_to_all | solution.py:99
  (468 shorter events, 280.4 us)
Async XLA Ops:
  7.2 48.0 %collective-permute-start.1 = (bf16[208,768]{1,0:T(8,128)(2,1)}, bf16[208,768]{1,0:T(8,128)(2,1)S(1)}, u32[]{:S(2)}, u32[]{:S(2)}) collective-permute-start(bf16[208,768]{1,0:T(8,128)(2,1)} %bitcast.307), channel_id=1, source_target_pairs={{0,2},{1,3},{2,0},{3,1},{4,6},{5,7},{6,4},{7,5},{8,10},{9,11},{10,... | collective-permute-start | bytes 958472 | tf_op jit(solution)/shard_map/ppermute | solution.py:57
  8.5 49.7 %collective-permute-start = (bf16[208,768]{1,0:T(8,128)(2,1)}, bf16[208,768]{1,0:T(8,128)(2,1)S(1)}, u32[]{:S(2)}, u32[]{:S(2)}) collective-permute-start(bf16[208,768]{1,0:T(8,128)(2,1)} %bitcast.308), channel_id=1, source_target_pairs={{0,1},{1,0},{2,3},{3,2},{4,5},{5,4},{6,7},{7,6},{8,9},{9,8},{10,11... | collective-permute-start | bytes 958472 | tf_op jit(solution)/shard_map/ppermute | solution.py:57
  10.1 19.5 %collective-permute-start.4 = (s32[208]{0:T(256)S(1)}, s32[208]{0:T(256)S(1)}, u32[]{:S(2)}, u32[]{:S(2)}) collective-permute-start(s32[208]{0:T(256)S(1)} %bitcast.351), channel_id=1, source_target_pairs={{0,2},{1,3},{2,0},{3,1},{4,6},{5,7},{6,4},{7,5},{8,10},{9,11},{10,... | collective-permute-start | bytes 2504 | tf_op jit(solution)/shard_map/ppermute | solution.py:57
  10.4 19.7 %collective-permute-start.3 = (s32[208]{0:T(256)S(1)}, s32[208]{0:T(256)S(1)}, u32[]{:S(2)}, u32[]{:S(2)}) collective-permute-start(s32[208]{0:T(256)S(1)} %bitcast.352), channel_id=1, source_target_pairs={{0,1},{1,0},{2,3},{3,2},{4,5},{5,4},{6,7},{7,6},{8,9},{9,8},{10,11... | collective-permute-start | bytes 2504 | tf_op jit(solution)/shard_map/ppermute | solution.py:57
  12.1 19.9 %collective-permute-start.10 = (bf16[24,576]{1,0:T(8,128)(2,1)S(1)}, bf16[24,576]{1,0:T(8,128)(2,1)S(1)}, u32[]{:S(2)}, u32[]{:S(2)}) collective-permute-start(bf16[24,576]{1,0:T(8,128)(2,1)S(1)} %get-tuple-element.237), channel_id=1, source_target_pairs={{0,3},{1,2},{2,1},{3,0},{4,7},{5,6},{6,5},{7,4},{8,11},{9,10},{10,... | collective-permute-start | bytes 82952 | tf_op jit(solution)/shard_map/ppermute | solution.py:57
  15.5 43.5 %all-to-all-start = ((bf16[32,24,640]{2,1,0:T(8,128)(2,1)}), bf16[32,24,640]{2,1,0:T(8,128)(2,1)S(1)}, u32[]{:S(2)}, u32[]{:S(2)}) async-start(bf16[32,24,640]{2,1,0:T(8,128)(2,1)} %bitcast.4), calls=%async_computation | async-start | bytes 1966080 | tf_op jit(solution)/shard_map/all_to_all | solution.py:99
  20.7 90.5 %all-gather.3.cloned.1.call-start = ((), (), s32[]{:S(2)}) async-start(), calls=%async_computation.12 | async-start | bytes 2654208 | tf_op jit(solution)/shard_map/all_gather | solution.py:433
  59.8 21.2 %all-to-all-start.1 = ((bf16[8,24,768]{2,1,0:T(8,128)(2,1)}), bf16[8,24,768]{2,1,0:T(8,128)(2,1)S(1)}, u32[]{:S(2)}, u32[]{:S(2)}) async-start(bf16[8,24,768]{2,1,0:T(8,128)(2,1)} %broadcast_in_dim.27), calls=%async_computation.1 | async-start | bytes 589824 | tf_op jit(solution)/shard_map/all_to_all | solution.py:99
  88.4 58.8 %all-to-all-start.2 = ((bf16[8,96,1536]{2,1,0:T(8,128)(2,1)}), bf16[8,96,1536]{2,1,0:T(8,128)(2,1)S(1)}, u32[]{:S(2)}, u32[]{:S(2)}) async-start(bf16[8,96,1536]{2,1,0:T(8,128)(2,1)} %pad_maximum_fusion), calls=%async_computation.2 | async-start | bytes 4718592 | tf_op jit(solution)/shard_map/all_to_all | solution.py:99
  148.4 53.7 %all-to-all-start.3 = ((bf16[8,152,768]{2,1,0:T(8,128)(2,1)}), bf16[8,152,768]{2,1,0:T(8,128)(2,1)}, u32[]{:S(2)}, u32[]{:S(2)}) async-start(bf16[8,152,768]{2,1,0:T(8,128)(2,1)} %pad_maximum_fusion.1), calls=%async_computation.3 | async-start | bytes 3735552 | tf_op jit(solution)/shard_map/all_to_all | solution.py:99
  165.3 27.9 %collective-permute-start.27 = (bf16[768,768]{1,0:T(8,128)(2,1)}, bf16[768,768]{1,0:T(8,128)(2,1)}, u32[]{:S(2)}, u32[]{:S(2)}) collective-permute-start(bf16[768,768]{1,0:T(8,128)(2,1)} %slice.296.in_ref), channel_id=1, source_target_pairs={{0,2},{1,3},{2,0},{3,1},{4,6},{5,7},{6,4},{7,5},{8,10},{9,11},{10,... | collective-permute-start | bytes 3538952 | tf_op jit(solution)/shard_map/ppermute | solution.py:57
  207.2 22.3 %all-to-all-start.4 = ((bf16[8,56,768]{2,1,0:T(8,128)(2,1)}), bf16[8,56,768]{2,1,0:T(8,128)(2,1)}, u32[]{:S(2)}, u32[]{:S(2)}) async-start(bf16[8,56,768]{2,1,0:T(8,128)(2,1)} %bitcast.323), calls=%async_computation.4 | async-start | bytes 1376256 | tf_op jit(solution)/shard_map/all_to_all | solution.py:99
  212.8 33.0 %collective-permute-start.31 = (bf16[768,768]{1,0:T(8,128)(2,1)S(1)}, bf16[768,768]{1,0:T(8,128)(2,1)}, u32[]{:S(2)}, u32[]{:S(2)}) collective-permute-start(bf16[768,768]{1,0:T(8,128)(2,1)S(1)} %bitcast.316), channel_id=1, source_target_pairs={{0,2},{1,3},{2,0},{3,1},{4,6},{5,7},{6,4},{7,5},{8,10},{9,11},{10,... | collective-permute-start | bytes 3538952 | tf_op jit(solution)/shard_map/ppermute | solution.py:57
  264.1 27.4 %collective-permute-start.34 = (bf16[768,768]{1,0:T(8,128)(2,1)}, bf16[768,768]{1,0:T(8,128)(2,1)S(1)}, u32[]{:S(2)}, u32[]{:S(2)}) collective-permute-start(bf16[768,768]{1,0:T(8,128)(2,1)} %get-tuple-element.93), channel_id=1, source_target_pairs={{0,2},{1,3},{2,0},{3,1},{4,6},{5,7},{6,4},{7,5},{8,10},{9,11},{10,... | collective-permute-start | bytes 3538952 | tf_op jit(solution)/shard_map/ppermute | solution.py:57
  265.4 29.1 %all-to-all-start.5 = ((bf16[8,56,768]{2,1,0:T(8,128)(2,1)}), bf16[8,56,768]{2,1,0:T(8,128)(2,1)}, u32[]{:S(2)}, u32[]{:S(2)}) async-start(bf16[8,56,768]{2,1,0:T(8,128)(2,1)} %bitcast.65), calls=%async_computation.5 | async-start | bytes 1376256 | tf_op jit(solution)/shard_map/all_to_all | solution.py:99
  296.2 32.9 %all-to-all-start.6 = ((bf16[8,96,768]{2,1,0:T(8,128)(2,1)}), bf16[8,96,768]{2,1,0:T(8,128)(2,1)}, u32[]{:S(2)}, u32[]{:S(2)}) async-start(bf16[8,96,768]{2,1,0:T(8,128)(2,1)} %bitcast.64), calls=%async_computation.6 | async-start | bytes 2359296 | tf_op jit(solution)/shard_map/all_to_all | solution.py:99
  312.5 18.1 %collective-permute-start.33 = (bf16[448,768]{1,0:T(8,128)(2,1)}, bf16[448,768]{1,0:T(8,128)(2,1)}, u32[]{:S(2)}, u32[]{:S(2)}) collective-permute-start(bf16[448,768]{1,0:T(8,128)(2,1)} %get-tuple-element.88), channel_id=1, source_target_pairs={{0,1},{1,0},{2,3},{3,2},{4,5},{5,4},{6,7},{7,6},{8,9},{9,8},{10,11... | collective-permute-start | bytes 2064392 | tf_op jit(solution)/shard_map/ppermute | solution.py:57
  312.5 27.3 %collective-permute-start.35 = (bf16[768,768]{1,0:T(8,128)(2,1)}, bf16[768,768]{1,0:T(8,128)(2,1)}, u32[]{:S(2)}, u32[]{:S(2)}) collective-permute-start(bf16[768,768]{1,0:T(8,128)(2,1)} %get-tuple-element.94), channel_id=1, source_target_pairs={{0,2},{1,3},{2,0},{3,1},{4,6},{5,7},{6,4},{7,5},{8,10},{9,11},{10,... | collective-permute-start | bytes 3538952 | tf_op jit(solution)/shard_map/ppermute | solution.py:57
  342.8 48.1 %all-to-all-start.7 = ((bf16[8,152,768]{2,1,0:T(8,128)(2,1)}), bf16[8,152,768]{2,1,0:T(8,128)(2,1)}, u32[]{:S(2)}, u32[]{:S(2)}) async-start(bf16[8,152,768]{2,1,0:T(8,128)(2,1)} %pad_maximum_fusion.2), calls=%async_computation.7 | async-start | bytes 3735552 | tf_op jit(solution)/shard_map/all_to_all | solution.py:99
  348.3 138.1 %reduce-scatter.2.cloned.1.call-start = ((), (), s32[]{:S(2)}) async-start(), calls=%async_computation.11 | async-start | bytes 3981312 | tf_op jit(solution)/shard_map/reduce_scatter | solution.py:564
  417.1 30.5 %collective-permute-start.55 = (bf16[8,24,768]{2,1,0:T(8,128)(2,1)}, bf16[8,24,768]{2,1,0:T(8,128)(2,1)}, u32[]{:S(2)}, u32[]{:S(2)}) collective-permute-start(bf16[8,24,768]{2,1,0:T(8,128)(2,1)} %get-tuple-element.206), channel_id=1, source_target_pairs={{0,3},{1,2},{2,1},{3,0},{4,7},{5,6},{6,5},{7,4},{8,11},{9,10},{10,... | collective-permute-start | bytes 884744 | tf_op jit(solution)/shard_map/ppermute | solution.py:57
  418.3 29.3 %collective-permute-start.56 = (bf16[8,24,768]{2,1,0:T(8,128)(2,1)}, bf16[8,24,768]{2,1,0:T(8,128)(2,1)}, u32[]{:S(2)}, u32[]{:S(2)}) collective-permute-start(bf16[8,24,768]{2,1,0:T(8,128)(2,1)} %get-tuple-element.205), channel_id=1, source_target_pairs={{0,2},{1,3},{2,0},{3,1},{4,6},{5,7},{6,4},{7,5},{8,10},{9,11},{10,... | collective-permute-start | bytes 884744 | tf_op jit(solution)/shard_map/ppermute | solution.py:57
  418.5 29.1 %collective-permute-start.57 = (bf16[8,24,768]{2,1,0:T(8,128)(2,1)}, bf16[8,24,768]{2,1,0:T(8,128)(2,1)}, u32[]{:S(2)}, u32[]{:S(2)}) collective-permute-start(bf16[8,24,768]{2,1,0:T(8,128)(2,1)} %get-tuple-element.204), channel_id=1, source_target_pairs={{0,1},{1,0},{2,3},{3,2},{4,5},{5,4},{6,7},{7,6},{8,9},{9,8},{10,11... | collective-permute-start | bytes 884744 | tf_op jit(solution)/shard_map/ppermute | solution.py:57
  437.4 44.0 %all-to-all-start.9 = ((bf16[32,24,640]{2,1,0:T(8,128)(2,1)}), bf16[32,24,640]{2,1,0:T(8,128)(2,1)}, u32[]{:S(2)}, u32[]{:S(2)}) async-start(bf16[32,24,640]{2,1,0:T(8,128)(2,1)} %bitcast.82), calls=%async_computation.9 | async-start | bytes 1966080 | tf_op jit(solution)/shard_map/all_to_all | solution.py:99
  (128 other events, 841.8 us)
Sparse Core Ops, SparseCore 0:
  44.8 52.8 all-gather.2
  382.1 98.8 reduce-scatter.1
